TPU v7x, 32 devices: a whole 2x2x4 slice. The times are simulated.
32 devices in a mesh: dp: 2 (over x), space: 16 (over z, y, core).
Axes of the slice: x: 2, y: 2, z: 4, core: 2. Of those that a mesh axis runs over, the one named last changes fastest.
Arguments:
- fields: bfloat16 [2, 2048, 100], P('dp', 'space'), may hold values from -6 to 6
- target: bfloat16 [2, 2048, 100], P('dp', 'space'), may hold values from -12 to 12
- area_weight: float32 [2048], P('space'), may hold values from 0.1 to 2.6
- grid_count: int32 [16], P('space'), may hold values from 64 to 128, as said below
- mesh_query: bfloat16 [512, 1024], P('space'), may hold values from -160 to 160
- enc_index: int32 [512, 12], P('space'), may hold values from -1 to 383, as said below
- proc_index: int32 [512, 16], P('space'), may hold values from 0 to 95, as said below
- dec_index: int32 [2048, 3], P('space'), may hold values from 0 to 95, as said below
- w_embed: bfloat16 [100, 1024], P(None, 'dp'), may hold values from -0.625 to 0.625
- w_enc_kv: bfloat16 [1024, 2048], P(None, 'dp'), may hold values from -0.1875 to 0.1875
- w_qkv: bfloat16 [1024, 3072], P(None, 'dp'), may hold values from -0.1875 to 0.1875
- w_out: bfloat16 [1024, 1024], P('dp'), may hold values from -0.1875 to 0.1875
- w_dec1: bfloat16 [1024, 1024], P(None, 'dp'), may hold values from -0.1875 to 0.1875
- w_dec2: bfloat16 [1024, 100], P('dp'), may hold values from -0.1875 to 0.1875
Outputs:
- prediction: bfloat16 [2, 2048, 100], P('dp', 'space')
- loss: float32 [], replicated
Inputs may be any that keep to these rules, and one draw needn't show every extreme that they name: The first grid_count slots of a device are real points; some device holds 128 and some other 64. `enc_index`: an entry e >= 0 of mesh node m names slot e mod 128 of device m // 32 - 1 + e // 128, an existing device, and a slot below its grid_count; -1 marks padding, each row has 6 to 12 real entries, first. `proc_index`: an entry e of mesh node m names node e mod 32 of device m // 32 - 1 + e // 32, an existing device; the first entry is the node itself. `dec_index`: an entry e of grid slot g names node e mod 32 of device g // 128 - 1 + e // 32, an existing device.
All inputs are finite; a program needn't handle non-finite values.
Results may differ from a plain program's by a relative error of at most 0.012.
Values may be sent and summed in bfloat16 or wider, within the bound.
No kernel may reach another device: no remote copies, remote signals or barrier semaphores. Data moves between devices by JAX's collectives and lax.ppermute only.
A program may use at most 64 MiB of HBM per device.

v0:
```python
import math

import jax
import jax.numpy as jnp
from jax import lax
from jax.sharding import PartitionSpec as P

HEADS = 16


def with_halo(cells, sides, width):
    for axis, dim in sides:
        count = lax.axis_size(axis)
        ends = count - 1
        head = lax.slice_in_dim(cells, 0, width, axis=dim)
        tail = lax.slice_in_dim(cells, cells.shape[dim] - width, cells.shape[dim], axis=dim)
        cells = jnp.concatenate(
            [
                lax.ppermute(tail, axis, [(i, (i + 1) % count) for i in range(ends)]),
                cells,
                lax.ppermute(head, axis, [((i + 1) % count, i) for i in range(ends)]),
            ],
            axis=dim,
        )
    return cells


def layer_norm(values):
    centre = jnp.mean(values, axis=-1, keepdims=True)
    shifted = values - centre
    spread = jnp.mean(shifted * shifted, axis=-1, keepdims=True)
    return shifted / jnp.sqrt(spread + 1e-05)


def attend(queries, gathered, present):
    node_count, width = queries.shape
    per_head_width = width // HEADS
    split_query_heads = queries.reshape(node_count, HEADS, per_head_width)
    split_key_heads = gathered[:, :, :width].reshape(node_count, -1, HEADS, per_head_width)
    split_value_heads = gathered[:, :, width:].reshape(node_count, -1, HEADS, per_head_width)
    attention_logits = jnp.einsum(
        "gtz,gxtz->gtx", split_query_heads, split_key_heads, preferred_element_type=jnp.float32
    ) / math.sqrt(per_head_width)
    attention_logits = jnp.where(present[:, None, :], attention_logits, -jnp.inf)
    attention_probs = jax.nn.softmax(attention_logits, axis=-1).astype(jnp.bfloat16)
    aggregated_values = jnp.einsum(
        "owi,oiwn->own", attention_probs, split_value_heads, preferred_element_type=jnp.float32
    )
    return aggregated_values.reshape(node_count, width)


def body(
    fields,
    target,
    area_weight,
    grid_count,
    mesh_query,
    enc_index,
    proc_index,
    dec_index,
    w_embed,
    w_enc_kv,
    w_qkv,
    w_out,
    w_dec1,
    w_dec2,
):
    own_fields = fields[0]
    grid_rows = own_fields.shape[0]
    mesh_rows, width = mesh_query.shape
    field_count = own_fields.shape[1]
    grid_window = with_halo(
        jax.nn.silu(
            jnp.dot(
                own_fields,
                lax.all_gather(w_embed, "dp", axis=1, tiled=True),
                preferred_element_type=jnp.float32,
            )
        ).astype(jnp.bfloat16),
        (("space", 0),),
        grid_rows,
    )
    grid_pairs = jnp.dot(
        grid_window,
        lax.all_gather(w_enc_kv, "dp", axis=1, tiled=True),
        preferred_element_type=jnp.float32,
    ).astype(jnp.bfloat16)
    present = enc_index >= 0
    enc_near = jnp.take(grid_pairs, jnp.maximum(enc_index, 0), axis=0)
    latent = (mesh_query.astype(jnp.float32) + attend(mesh_query, enc_near, present)).astype(
        jnp.bfloat16
    )
    normed = layer_norm(latent.astype(jnp.float32)).astype(jnp.bfloat16)
    mesh_qkv = jnp.dot(
        normed, lax.all_gather(w_qkv, "dp", axis=1, tiled=True), preferred_element_type=jnp.float32
    ).astype(jnp.bfloat16)
    mesh_queries = mesh_qkv[:, :width]
    mesh_pairs = with_halo(mesh_qkv[:, width:], (("space", 0),), mesh_rows)
    proc_near = jnp.take(mesh_pairs, proc_index, axis=0)
    mixed = attend(mesh_queries, proc_near, jnp.ones(proc_index.shape, dtype=bool)).astype(
        jnp.bfloat16
    )
    columns = mixed
    projected = jnp.dot(
        columns, lax.all_gather(w_out, "dp", axis=0, tiled=True), preferred_element_type=jnp.float32
    )
    updated = (latent.astype(jnp.float32) + projected).astype(jnp.bfloat16)
    mesh_window = with_halo(updated, (("space", 0),), mesh_rows)
    dec_near = jnp.take(mesh_window, dec_index, axis=0).astype(jnp.float32)
    decoder_in = layer_norm(jnp.mean(dec_near, axis=1)).astype(jnp.bfloat16)
    decoder_hidden = jax.nn.silu(
        jnp.dot(
            decoder_in,
            lax.all_gather(w_dec1, "dp", axis=1, tiled=True),
            preferred_element_type=jnp.float32,
        )
    ).astype(jnp.bfloat16)
    columns = decoder_hidden
    increment = jnp.dot(
        columns,
        lax.all_gather(w_dec2, "dp", axis=0, tiled=True),
        preferred_element_type=jnp.float32,
    )
    valid = jnp.arange(grid_rows, dtype=jnp.int32) < grid_count[0]
    predicted = jnp.where(
        valid[:, None], own_fields.astype(jnp.float32) + increment, jnp.float32(0.0)
    )
    keep_mask = valid.astype(jnp.float32)
    target_rows = target[0].astype(jnp.float32)
    misfit = predicted - target_rows
    error_sums = jnp.sum((keep_mask * area_weight)[:, None] * misfit * misfit, axis=0)
    target_sums = jnp.sum(keep_mask[:, None] * target_rows * target_rows, axis=0)
    valid_count = jnp.sum(keep_mask)
    weight_sum = jnp.sum(keep_mask * area_weight)
    target_all, count_all, weight_all = lax.psum(
        (target_sums, valid_count, weight_sum), ("dp", "space")
    )
    local_loss = jnp.sum(error_sums / (target_all / count_all + 1e-05))
    loss = lax.psum(local_loss, ("dp", "space")) / (field_count * weight_all)
    return (predicted.astype(jnp.bfloat16)[None], loss)


def solution(mesh):
    placed = (
        P("dp", "space", None),
        P("dp", "space", None),
        P("space"),
        P("space"),
        P("space", None),
        P("space", None),
        P("space", None),
        P("space", None),
        P(None, "dp"),
        P(None, "dp"),
        P(None, "dp"),
        P("dp", None),
        P(None, "dp"),
        P("dp", None),
    )
    return jax.shard_map(
        body, mesh=mesh, in_specs=placed, out_specs=(P("dp", "space", None), P()), check_vma=False
    )
```

profile of v0, /device:TPU:0, one launch (start us, length us, event | category | flops | bytes accessed | tf_op | source)
XLA Modules:
  0.0 315.6 jit_solution(1042012544870451233)
XLA Ops:
  9.5 6.6 %all_gather.18 = bf16[100,1024]{1,0:T(8,128)(2,1)S(1)} all-gather(bf16[100,512]{1,0:T(8,128)(2,1)S(1)} %copy-done.1), channel_id=1, replica_groups=mesh['dp'=2,'space'=16] {'dp'}, dimensions={1}, use_global_device_ids=true | all-gather | bytes 307200 | tf_op jit(solution)/shard_map/all_gather | solution.py:76
  21.2 2.0 collective-permute-done.1
  23.2 45.9 %all-gather.5.cloned.1.call-done = bf16[1024,2048]{1,0:T(8,128)(2,1)} async-done(((bf16[1024,1024]{1,0:T(8,128)(2,1)}), bf16[1024,2048]{1,0:T(8,128)(2,1)}) %all-gather.5.cloned.1.call-update) | async-done | bytes 4194320 | tf_op jit(solution)/shard_map/all_gather | solution.py:85
  69.0 4.0 %convolution_convert_fusion.1 = bf16[384,2048]{1,0:T(8,128)(2,1)S(1)} fusion(bf16[1024,2048]{1,0:T(8,128)(2,1)} %all-gather.5.cloned.1.call-done, bf16[128,1024]{1,0:T(8,128)(2,1)S(1)} %collective-permute-done.1, bf16[128,1024]{1,0:T(8,128)(2,1)S(1)} %multiply_convert_fusion.1, bf16[128,1024]{1,0:T(8,128)(2,1)S(1)} %collective-permute-done), kind=kOutput, calls=%fused_computation.6 | convolution fusion | flops 1613758464 | bytes 6553600 | tf_op jit(solution)/shard_map/dot_general | solution.py:83
  73.0 2.5 gather_fusion
  77.0 2.1 broadcast_select_fusion.1
  79.4 1.9 reshape.127
  81.3 2.8 fusion.4
  87.1 63.9 %all-gather.7.cloned.1.call-done = bf16[1024,3072]{1,0:T(8,128)(2,1)} async-done(((bf16[1024,1536]{1,0:T(8,128)(2,1)}), bf16[1024,3072]{1,0:T(8,128)(2,1)}) %all-gather.7.cloned.1.call-update) | async-done | bytes 6291472 | tf_op jit(solution)/shard_map/all_gather | solution.py:95
  151.0 4.0 %convolution_convert_fusion = bf16[32,3072]{1,0:T(8,128)(2,1)S(1)} fusion(bf16[1024,3072]{1,0:T(8,128)(2,1)} %all-gather.7.cloned.1.call-done, bf16[32,1024]{1,0:T(8,128)(2,1)S(1)} %get-tuple-element.11, f32[32]{0:T(128)S(1)} %add_sqrt_fusion.1, f32[32]{0:T(128)S(1)} %broadcast_multiply_fusion.1), kind=kOutput, calls=%fused_computation.5 | convolution fusion | flops 201555968 | bytes 6553856 | tf_op jit(solution)/shard_map/dot_general | solution.py:94
  155.1 1.7 collective-permute-start.2
  159.0 2.4 collective-permute-done.3
  161.4 2.5 gather_fusion.1
  164.3 2.4 reshape.86
  166.7 2.8 fusion.8
  172.4 13.4 %all-gather.9.cloned.1.call-done = bf16[1024,1024]{1,0:T(8,128)(2,1)} async-done(((bf16[512,1024]{1,0:T(8,128)(2,1)}), bf16[1024,1024]{1,0:T(8,128)(2,1)}) %all-gather.9.cloned.1.call-update) | async-done | bytes 2097168 | tf_op jit(solution)/shard_map/all_gather | solution.py:105
  185.7 2.1 fusion.13
  187.8 1.7 collective-permute-start.4
  191.0 5.4 %all_gather.23 = bf16[1024,100]{0,1:T(8,128)(2,1)S(1)} all-gather(bf16[512,100]{0,1:T(8,128)(2,1)S(1)} %copy-done.2), channel_id=1, replica_groups=mesh['dp'=2,'space'=16] {'dp'}, dimensions={0}, use_global_device_ids=true | all-gather | bytes 307200 | tf_op jit(solution)/shard_map/all_gather | solution.py:121
  196.4 2.1 gather_fusion.2
  200.8 19.7 %all-gather.11.cloned.1.call-done = bf16[1024,1024]{1,0:T(8,128)(2,1)} async-done(((bf16[1024,512]{1,0:T(8,128)(2,1)}), bf16[1024,1024]{1,0:T(8,128)(2,1)}) %all-gather.11.cloned.1.call-update) | async-done | bytes 2097168 | tf_op jit(solution)/shard_map/all_gather | solution.py:114
  220.5 3.0 fusion.43
  223.5 40.8 %all-reduce.1 = (f32[100]{0:T(128)S(1)}, f32[]{:T(128)}) all-reduce(f32[100]{0:T(128)S(1)} %get-tuple-element.2, f32[]{:T(128)} %get-tuple-element.21), channel_id=1, replica_groups=mesh['dp'=2,'space'=16] {'dp','space'}, use_global_device_ids=true, to_apply=%region_11.12 | all-reduce | flops 101 | bytes 808 | tf_op jit(solution)/shard_map/psum | solution.py:135
  265.7 41.1 %all-reduce = (f32[]{:T(128)}, f32[]{:T(128)}) all-reduce(f32[]{:T(128)} %fusion.46, f32[]{:T(128)} %get-tuple-element.8), channel_id=1, replica_groups=mesh['dp'=2,'space'=16] {'dp','space'}, use_global_device_ids=true, to_apply=%region_15.16 | all-reduce | flops 2 | bytes 16 | tf_op jit(solution)/shard_map/psum | solution.py:139
  (91 shorter events, 21.8 us)
Async XLA Ops:
  7.2 61.9 %all-gather.5.cloned.1.call-start = ((), (), s32[]{:S(2)}) async-start(), calls=%async_computation | async-start | bytes 6291456 | tf_op jit(solution)/shard_map/all_gather | solution.py:85
  7.9 1.6 copy-start.1
  7.9 8.2 %copy-start.8 = (bf16[1,128,100]{1,2,0:T(8,128)(2,1)S(1)}, bf16[1,128,100]{1,2,0:T(8,128)(2,1)}, u32[]{:S(2)}) copy-start(bf16[1,128,100]{1,2,0:T(8,128)(2,1)} %param.14) | copy-start | bytes 76804
  7.9 143.1 %all-gather.7.cloned.1.call-start = ((), (), s32[]{:S(2)}) async-start(), calls=%async_computation.1 | async-start | bytes 9437184 | tf_op jit(solution)/shard_map/all_gather | solution.py:95
  8.7 10.4 %copy-start.4 = (s32[32,12]{0,1:T(8,128)S(1)}, s32[32,12]{0,1:T(8,128)}, u32[]{:S(2)}) copy-start(s32[32,12]{0,1:T(8,128)} %param.19) | copy-start | bytes 4612
  8.7 177.1 %all-gather.9.cloned.1.call-start = ((), (), s32[]{:S(2)}) async-start(), calls=%async_computation.2 | async-start | bytes 3145728 | tf_op jit(solution)/shard_map/all_gather | solution.py:105
  9.4 9.7 %copy-start.5 = (s32[128,3]{0,1:T(4,128)S(1)}, s32[128,3]{0,1:T(4,128)}, u32[]{:S(2)}) copy-start(s32[128,3]{0,1:T(4,128)} %param.21) | copy-start | bytes 4612
  9.4 9.9 %copy-start.3 = (s32[32,16]{0,1:T(8,128)S(1)}, s32[32,16]{0,1:T(8,128)}, u32[]{:S(2)}) copy-start(s32[32,16]{0,1:T(8,128)} %param.20) | copy-start | bytes 6148
  9.4 10.6 %copy-start.6 = (f32[128]{0:T(128)S(1)}, f32[128]{0:T(128)}, u32[]{:S(2)}) copy-start(f32[128]{0:T(128)} %param.16) | copy-start | bytes 1540
  9.4 11.4 %copy-start = (bf16[32,1024]{1,0:T(8,128)(2,1)S(1)}, bf16[32,1024]{1,0:T(8,128)(2,1)}, u32[]{:S(2)}) copy-start(bf16[32,1024]{1,0:T(8,128)(2,1)} %param.18) | copy-start | bytes 196612
  9.5 211.1 %all-gather.11.cloned.1.call-start = ((), (), s32[]{:S(2)}) async-start(), calls=%async_computation.3 | async-start | bytes 3145728 | tf_op jit(solution)/shard_map/all_gather | solution.py:114
  16.4 4.7 %collective-permute-start = (bf16[128,1024]{1,0:T(8,128)(2,1)S(1)}, bf16[128,1024]{1,0:T(8,128)(2,1)S(1)}, u32[]{:S(2)}, u32[]{:S(2)}) collective-permute-start(bf16[128,1024]{1,0:T(8,128)(2,1)S(1)} %multiply_convert_fusion.1), channel_id=1, source_target_pairs={{0,1},{1,2},{2,3},{3,4},{4,5},{5,6},{6,7},{7,8},{8,9},{9,10},{10,1... | collective-permute-start | bytes 786440 | tf_op jit(solution)/shard_map/ppermute | solution.py:19
  17.7 5.4 %collective-permute-start.1 = (bf16[128,1024]{1,0:T(8,128)(2,1)S(1)}, bf16[128,1024]{1,0:T(8,128)(2,1)S(1)}, u32[]{:S(2)}, u32[]{:S(2)}) collective-permute-start(bf16[128,1024]{1,0:T(8,128)(2,1)S(1)} %multiply_convert_fusion.1), channel_id=1, source_target_pairs={{1,0},{2,1},{3,2},{4,3},{5,4},{6,5},{7,6},{8,7},{9,8},{10,9},{11,1... | collective-permute-start | bytes 786440 | tf_op jit(solution)/shard_map/ppermute | solution.py:21
  155.1 3.9 %collective-permute-start.2 = (bf16[32,2048]{1,0:T(8,128)(2,1)S(1)}, bf16[32,2048]{1,0:T(8,128)(2,1)S(1)}, u32[]{:S(2)}, u32[]{:S(2)}) collective-permute-start(bf16[32,2048]{1,0:T(8,128)(2,1)S(1)} %slice.33), channel_id=1, source_target_pairs={{0,1},{1,2},{2,3},{3,4},{4,5},{5,6},{6,7},{7,8},{8,9},{9,10},{10,1... | collective-permute-start | bytes 393224 | tf_op jit(solution)/shard_map/ppermute | solution.py:19
  156.8 4.5 %collective-permute-start.3 = (bf16[32,2048]{1,0:T(8,128)(2,1)S(1)}, bf16[32,2048]{1,0:T(8,128)(2,1)S(1)}, u32[]{:S(2)}, u32[]{:S(2)}) collective-permute-start(bf16[32,2048]{1,0:T(8,128)(2,1)S(1)} %slice.33), channel_id=1, source_target_pairs={{1,0},{2,1},{3,2},{4,3},{5,4},{6,5},{7,6},{8,7},{9,8},{10,9},{11,1... | collective-permute-start | bytes 393224 | tf_op jit(solution)/shard_map/ppermute | solution.py:21
  172.2 18.8 %copy-start.2 = (bf16[512,100]{0,1:T(8,128)(2,1)S(1)}, bf16[512,100]{0,1:T(8,128)(2,1)}, u32[]{:S(2)}) copy-start(bf16[512,100]{0,1:T(8,128)(2,1)} %param.27) | copy-start | bytes 307204
  187.8 8.6 %collective-permute-start.4 = (bf16[32,1024]{1,0:T(8,128)(2,1)S(1)}, bf16[32,1024]{1,0:T(8,128)(2,1)S(1)}, u32[]{:S(2)}, u32[]{:S(2)}) collective-permute-start(bf16[32,1024]{1,0:T(8,128)(2,1)S(1)} %fusion.13), channel_id=1, source_target_pairs={{0,1},{1,2},{2,3},{3,4},{4,5},{5,6},{6,7},{7,8},{8,9},{9,10},{10,1... | collective-permute-start | bytes 196616 | tf_op jit(solution)/shard_map/ppermute | solution.py:19
  189.6 6.8 %collective-permute-start.5 = (bf16[32,1024]{1,0:T(8,128)(2,1)S(1)}, bf16[32,1024]{1,0:T(8,128)(2,1)S(1)}, u32[]{:S(2)}, u32[]{:S(2)}) collective-permute-start(bf16[32,1024]{1,0:T(8,128)(2,1)S(1)} %fusion.13), channel_id=1, source_target_pairs={{1,0},{2,1},{3,2},{4,3},{5,4},{6,5},{7,6},{8,7},{9,8},{10,9},{11,1... | collective-permute-start | bytes 196616 | tf_op jit(solution)/shard_map/ppermute | solution.py:21
  198.5 22.0 %copy-start.7 = (bf16[1,128,100]{1,2,0:T(8,128)(2,1)S(1)}, bf16[1,128,100]{1,2,0:T(8,128)(2,1)}, u32[]{:S(2)}) copy-start(bf16[1,128,100]{1,2,0:T(8,128)(2,1)} %param.15) | copy-start | bytes 76804
Sparse Core Ops, SparseCore 0:
  9.5 59.4 all-gather.4
  70.6 80.4 all-gather.6
  152.6 33.1 all-gather.8
  187.1 33.3 all-gather.10
where the time goes:
time: 316 us
  waiting for transfers between devices  149 us (47%)
  blocking collectives  93.8 us (30%)
  matrix products  20.3 us (6%)
  local copies, waits for them, and re-layouts  19.1 us (6%)
  between operations  17.2 us (5%)
  starting transfers between devices  9.01 us (3%)
  other arithmetic  6.86 us (2%)
    all_gather x1, waiting for transfers between devices, body(): lax.all_gather(w_qkv, 'dp', axis=1, tiled=True)  63.9 us
    all_gather x1, waiting for transfers between devices, body(): lax.all_gather(w_enc_kv, 'dp', axis=1, tiled=True)  45.9 us
    psum x1, blocking collectives, body(): loss = lax.psum(local_loss, ('dp', 'space')) / (field_count * weight_all)  41.1 us
    psum x1, blocking collectives, body(): lax.psum((target_sums, valid_count, weight_sum), ('dp', 'space'))  40.8 us
    all_gather x1, waiting for transfers between devices, body(): lax.all_gather(w_dec1, 'dp', axis=1, tiled=True)  19.7 us
    all_gather x1, waiting for transfers between devices, body(): lax.all_gather(w_out, 'dp', axis=0, tiled=True)  13.4 us
    all_gather x1, blocking collectives, body(): lax.all_gather(w_embed, 'dp', axis=1, tiled=True)  6.56 us
  transfers between devices with their start and end apart: 10, of which 6 were waited for; matrix products, arithmetic and copies ran while one was open for 13% of the time, Pallas kernels for 0%

commit v1 on v0

--- a/solution.py
+++ b/solution.py
@@ -1,11 +1,325 @@
+import functools
 import math
 
 import jax
 import jax.numpy as jnp
 from jax import lax
+from jax.experimental import pallas as pl
+from jax.experimental.pallas import tpu as pltpu
 from jax.sharding import PartitionSpec as P
 
 HEADS = 16
+F32 = jnp.float32
+BF16 = jnp.bfloat16
+
+
+def silu(x):
+    return 0.5 * x * (1.0 + jnp.tanh(0.5 * x))
+
+
+def dot(a, b):
+    return jnp.dot(a, b, preferred_element_type=F32)
+
+
+def dot_nt(a, b):
+    return lax.dot_general(a, b, (((1,), (1,)), ((), ())), preferred_element_type=F32)
+
+
+def normalize(values):
+    centre = jnp.mean(values, axis=-1, keepdims=True)
+    shifted = values - centre
+    spread = jnp.mean(shifted * shifted, axis=-1, keepdims=True)
+    return shifted * lax.rsqrt(spread + 1e-05)
+
+
+def call(kernel, out_shape, args, scratch=(), flops=0, smem=(0,)):
+    specs = [
+        pl.BlockSpec(memory_space=pltpu.SMEM if i in smem else pltpu.VMEM) for i in range(len(args))
+    ]
+    many = isinstance(out_shape, (list, tuple))
+    out_specs = jax.tree.map(lambda _: pl.BlockSpec(memory_space=pltpu.VMEM), out_shape)
+    size = sum(math.prod(a.shape) * a.dtype.itemsize for a in args)
+    return pl.pallas_call(
+        kernel,
+        out_shape=out_shape,
+        in_specs=specs,
+        out_specs=tuple(out_specs) if many else out_specs,
+        scratch_shapes=list(scratch),
+        compiler_params=pltpu.CompilerParams(vmem_limit_bytes=48 * 1024 * 1024),
+        cost_estimate=pl.CostEstimate(flops=flops, bytes_accessed=size, transcendentals=0),
+    )(*args)
+
+
+def encode_kernel(
+    place, own, own1, own2, oth, oth1, oth2, pick, present, we_here, we_there, w_ref, query,
+    pairs_ref, probs_ref,
+):
+    half = we_here.shape[1]
+    nodes, width = query.shape
+    rows = pick.shape[0]
+    slots = own.shape[0]
+    entries = rows // nodes
+    per_head = width // HEADS
+    here = pl.multiple_of(place[0] * half, half)
+    there = pl.multiple_of((1 - place[0]) * half, half)
+    head_of = lax.broadcasted_iota(jnp.int32, (width, 128), 0) // per_head
+    fold = (head_of == lax.broadcasted_iota(jnp.int32, (width, 128), 1)).astype(BF16)
+    queries = jnp.broadcast_to(query[...].astype(F32)[None], (entries, nodes, width))
+    queries = queries.reshape(rows, width)
+    there_mask = present[...] > 0
+    for s, blocks in enumerate(((own, own1, own2), (oth, oth1, oth2))):
+        near = sum(dot(pick[:, i * slots : (i + 1) * slots], b[...]) for i, b in enumerate(blocks))
+        near = near.astype(BF16)
+        embed_here = silu(dot(near, we_here[...])).astype(BF16)
+        embed_there = silu(dot(near, we_there[...])).astype(BF16)
+        pairs = dot(embed_here, w_ref[pl.ds(here, half), :])
+        pairs = (pairs + dot(embed_there, w_ref[pl.ds(there, half), :])).astype(BF16)
+        pairs_ref[s * rows : (s + 1) * rows, :] = pairs
+        product = pairs.astype(F32) * queries
+        high = product.astype(BF16)
+        low = (product - high.astype(F32)).astype(BF16)
+        logits = (dot(high, fold) + dot(low, fold)) * (1.0 / math.sqrt(per_head))
+        logits = jnp.where(there_mask, logits, -1e30).reshape(entries, nodes, 128)
+        top = jnp.max(logits, axis=0, keepdims=True)
+        weight = jnp.where(there_mask.reshape(entries, nodes, 128), jnp.exp(logits - top), 0.0)
+        weight = weight / jnp.sum(weight, axis=0, keepdims=True)
+        turned = jnp.transpose(weight.reshape(rows, 128))
+        probs_ref[:, s * rows : (s + 1) * rows] = turned[:HEADS].astype(BF16)
+
+
+def latent_kernel(probs, pairs, query, latent_ref):
+    nodes, width = query.shape
+    rows = pairs.shape[0] // 2
+    entries = rows // nodes
+    per_head = width // HEADS
+    head_of = lax.broadcasted_iota(jnp.int32, (HEADS, width), 1) // per_head
+    spread = (head_of == lax.broadcasted_iota(jnp.int32, (HEADS, width), 0)).astype(BF16)
+    for s in range(2):
+        turned = probs[:, (1 - s) * rows : (2 - s) * rows].astype(F32)
+        weight = jnp.transpose(turned).astype(BF16)
+        mixed = dot(weight, spread) * pairs[s * rows : (s + 1) * rows, :].astype(F32)
+        mixed = jnp.sum(mixed.reshape(entries, nodes, width), axis=0)
+        latent_ref[s * nodes : (s + 1) * nodes, :] = (query[...].astype(F32) + mixed).astype(BF16)
+
+
+def mesh_kernel(
+    place, lat0, lat1, lat2, count, w_ref, same_ref, cross_ref, wo_ref,
+    keep_ref, send_ref, norm_ref,
+):
+    both, width = lat0.shape
+    nodes = both // 2
+    half = width // 2
+    rows = 3 * both
+    heads = HEADS // 2
+    per_head = half // heads
+    for i, block in enumerate((lat0, lat1, lat2)):
+        norm_ref[i * both : (i + 1) * both, :] = normalize(block[...].astype(F32)).astype(BF16)
+    here = pl.multiple_of(place[1] * half, half)
+    there = pl.multiple_of((1 - place[1]) * half, half)
+    first = place[0] == 0
+    part_a = dot(norm_ref[...], w_ref[:, :half])
+    part_c = dot(norm_ref[...], w_ref[:, 2 * half :])
+    part_b = dot(norm_ref[:, pl.ds(here, half)], same_ref[...])
+    part_b += dot(norm_ref[:, pl.ds(there, half)], cross_ref[...])
+    queries = jnp.where(first, part_a[:both], part_b[:both]).astype(BF16)
+    keys = jnp.where(first, part_c, part_a).astype(BF16)
+    values = jnp.where(first, part_b, part_c).astype(BF16)
+    head_of = lax.broadcasted_iota(jnp.int32, (both, half), 1) // per_head
+    zero = jnp.zeros_like(queries)
+    stacked = jnp.concatenate(
+        [jnp.where(head_of == h, queries, zero) for h in range(heads)], axis=0
+    )
+    logits = dot_nt(stacked, keys) * (1.0 / math.sqrt(per_head))
+    logits = logits.reshape(heads, both, rows)
+    times = count[...][None]
+    logits = jnp.where(times > 0, logits, -1e30)
+    top = jnp.max(logits, axis=-1, keepdims=True)
+    weight = times * jnp.exp(logits - top)
+    weight = weight / jnp.sum(weight, axis=-1, keepdims=True)
+    mixed = dot(weight.astype(BF16).reshape(heads * both, rows), values)
+    mixed = mixed.reshape(heads, both, half)
+    total = jnp.where(head_of == 0, mixed[0], 0.0)
+    for h in range(1, heads):
+        total = jnp.where(head_of == h, mixed[h], total)
+    projected = dot(total.astype(BF16), wo_ref[...])
+    keep_ref[...] = lat0[:nodes, :].astype(F32) + projected[:nodes]
+    send_ref[...] = projected[nodes:].astype(BF16)
+
+
+def decode_kernel(
+    place, up0, up1, up2, count, w1_ref, same_ref, cross_ref, w2_ref, w2_there, fields, target,
+    area, valid, pred_ref, sums_ref, norm_ref,
+):
+    nodes, width = up0.shape
+    half = width // 2
+    near = sum(
+        dot(count[:, i * nodes : (i + 1) * nodes], b[...]) for i, b in enumerate((up0, up1, up2))
+    )
+    norm_ref[...] = normalize(near * (1.0 / 3.0)).astype(BF16)
+    here = pl.multiple_of(place[1] * half, half)
+    there = pl.multiple_of((1 - place[1]) * half, half)
+    hidden = silu(dot(norm_ref[...], w1_ref[...])).astype(BF16)
+    hidden_there = dot(norm_ref[:, pl.ds(here, half)], same_ref[...])
+    hidden_there += dot(norm_ref[:, pl.ds(there, half)], cross_ref[...])
+    hidden_there = silu(hidden_there).astype(BF16)
+    increment = dot(hidden, w2_ref[...]) + dot(hidden_there, w2_there[...])
+    keep = valid[...] > 0
+    predicted = jnp.where(keep, fields[...].astype(F32) + increment, 0.0)
+    pred_ref[...] = predicted.astype(BF16)
+    goal = target[...].astype(F32)
+    misfit = predicted - goal
+    weight = jnp.where(keep, area[...], 0.0)
+    count_field = fields.shape[1]
+    errors = jnp.sum(weight * misfit * misfit, axis=0, keepdims=True)
+    squares = jnp.sum(jnp.where(keep, goal * goal, 0.0), axis=0, keepdims=True)
+    here_count = jnp.sum(valid[...], axis=0, keepdims=True)
+    here_weight = jnp.sum(weight, axis=0, keepdims=True)
+    sums = jnp.concatenate(
+        [
+            errors,
+            squares,
+            jnp.broadcast_to(here_count, (1, count_field)),
+            jnp.broadcast_to(here_weight, (1, count_field)),
+            jnp.zeros((4, count_field), F32),
+        ],
+        axis=0,
+    )
+    sums_ref[...] = jnp.broadcast_to(sums[None], sums_ref.shape)
+
+
+def loss_kernel(parts, loss_ref):
+    total = jnp.sum(parts[...], axis=0)
+    fields = total.shape[1]
+    scaled = total[0:1] / (total[1:2] / total[2:3] + 1e-05)
+    weight = total[3:4, 0:1]
+    loss_ref[...] = jnp.sum(scaled, axis=1, keepdims=True) / (fields * weight)
+
+
+def small_body(
+    fields, target, area_weight, grid_count, mesh_query, enc_index, proc_index, dec_index,
+    w_embed, w_enc_kv, w_qkv, w_out, w_dec1, w_dec2,
+):
+    space = lax.axis_size("space")
+    samples = lax.axis_size("dp")
+    row = lax.axis_index("dp")
+    spot = lax.axis_index("space")
+    core = spot % 2
+    place = jnp.stack([row, core]).astype(jnp.int32)
+    own = fields[0]
+    slots, field_count = own.shape
+    nodes, width = mesh_query.shape
+    half = width // 2
+    entries = enc_index.shape[1]
+    rows = nodes * entries
+
+    swap = [(0, 1), (1, 0)]
+    pair = [(i, i ^ 1) for i in range(space)]
+    link = [(i, i + 1) for i in range(1, space - 1, 2)]
+    link = link + [(j, i) for i, j in link]
+    cross = [(d * space + i, (1 - d) * space + j) for d in range(2) for i, j in link]
+
+    def over_dp(x):
+        return lax.ppermute(x, "dp", swap)
+
+    def over_pair(x):
+        return lax.ppermute(x, "space", pair)
+
+    def over_link(x):
+        return lax.ppermute(x, "space", link)
+
+    oth = over_dp(own)
+    own2 = over_link(own)
+    oth2 = lax.ppermute(own, ("dp", "space"), cross)
+    we_there = over_dp(w_embed)
+    own1 = over_pair(own)
+    oth1 = over_pair(oth)
+
+    wq_same = over_dp(lax.dynamic_slice(w_qkv, (core * half, half), (half, half)))
+    wq_cross = over_pair(wq_same)
+    w1_same = over_dp(lax.dynamic_slice(w_dec1, (core * half, 0), (half, half)))
+    w1_cross = over_pair(w1_same)
+    w2_there = over_dp(w_dec2)
+
+    def block_of(index, size):
+        side = index // size
+        even = jnp.where(side == 0, 2, jnp.where(side == 1, 0, 1))
+        odd = jnp.where(side == 0, 1, jnp.where(side == 1, 0, 2))
+        return jnp.where(core == 0, even, odd), index % size
+
+    block, slot = block_of(enc_index, slots)
+    column = jnp.where(enc_index >= 0, block * slots + slot, -1).T.reshape(rows, 1)
+    pick = (column == jnp.arange(3 * slots, dtype=jnp.int32)[None]).astype(BF16)
+    present = jnp.broadcast_to((column >= 0).astype(F32), (rows, 128))
+
+    block, slot = block_of(proc_index, nodes)
+    near = jnp.arange(6 * nodes, dtype=jnp.int32)
+    sample_of = (near // nodes) % 2
+    code = (near // (2 * nodes)) * nodes + near % nodes
+    column = (block * nodes + slot)[:, :, None] == code[None, None]
+    times = jnp.sum(column.astype(F32), axis=1)
+    times = jnp.concatenate(
+        [times * (sample_of == 0)[None], times * (sample_of == 1)[None]], axis=0
+    )
+
+    block, slot = block_of(dec_index, nodes)
+    column = (block * nodes + slot)[:, :, None] == jnp.arange(3 * nodes, dtype=jnp.int32)
+    dec_count = jnp.sum(column.astype(F32), axis=1).astype(BF16)
+
+    valid = (jnp.arange(slots, dtype=jnp.int32) < grid_count[0]).astype(F32)[:, None]
+    area = area_weight[:, None]
+
+    pairs, probs = call(
+        encode_kernel,
+        (
+            jax.ShapeDtypeStruct((2 * rows, width), BF16),
+            jax.ShapeDtypeStruct((HEADS, 2 * rows), BF16),
+        ),
+        (place, own, own1, own2, oth, oth1, oth2, pick, present, w_embed, we_there, w_enc_kv,
+         mesh_query),
+        flops=2 * 2 * rows * width * (width + field_count),
+    )
+    probs = over_dp(probs)
+    latent = call(
+        latent_kernel,
+        jax.ShapeDtypeStruct((2 * nodes, width), BF16),
+        (probs, pairs, mesh_query),
+        flops=2 * 2 * rows * width * 128,
+        smem=(),
+    )
+    came = over_dp(latent)
+    came = jnp.concatenate([came[nodes:], came[:nodes]], axis=0)
+    latent = jnp.where(row == 0, came, latent)
+    lat1 = over_pair(latent)
+    lat2 = over_link(latent)
+    keep, send = call(
+        mesh_kernel,
+        (
+            jax.ShapeDtypeStruct((nodes, width), F32),
+            jax.ShapeDtypeStruct((nodes, width), BF16),
+        ),
+        (place, latent, lat1, lat2, times, w_qkv, wq_same, wq_cross, w_out),
+        scratch=[pltpu.VMEM((6 * nodes, width), BF16)],
+        flops=2 * 6 * nodes * width * 3 * half,
+    )
+    updated = (keep + over_dp(send).astype(F32)).astype(BF16)
+    up1 = over_pair(updated)
+    up2 = over_link(updated)
+    predicted, sums = call(
+        decode_kernel,
+        (
+            jax.ShapeDtypeStruct((slots, field_count), BF16),
+            jax.ShapeDtypeStruct((space * samples, 8, field_count), F32),
+        ),
+        (place, updated, up1, up2, dec_count, w_dec1, w1_same, w1_cross, w_dec2, w2_there, own,
+         target[0], area, valid),
+        scratch=[pltpu.VMEM((slots, width), BF16)],
+        flops=2 * slots * width * (width + field_count),
+    )
+    parts = lax.all_to_all(sums, ("dp", "space"), 0, 0)
+    loss = call(
+        loss_kernel, jax.ShapeDtypeStruct((1, 1), F32), (parts,), smem=()
+    )
+    return predicted[None], loss[0, 0]
 
 
 def with_halo(cells, sides, width):
@@ -49,7 +363,7 @@
     return aggregated_values.reshape(node_count, width)
 
 
-def body(
+def general_body(
     fields,
     target,
     area_weight,
@@ -157,6 +471,7 @@
         P(None, "dp"),
         P("dp", None),
     )
+    small = mesh.shape["dp"] == 2 and mesh.shape["space"] % 2 == 0
     return jax.shard_map(
-        body, mesh=mesh, in_specs=placed, out_specs=(P("dp", "space", None), P()), check_vma=False
-    )
+        small_body if small else general_body, mesh=mesh, in_specs=placed, out_specs=(P("dp", "space", None), P()), check_vma=False
+    )

time: 316 us -> 99.8 us (0.32)
  waiting for transfers between devices: 149 us -> 20.9 us
  blocking collectives: 93.8 us -> 0 us
  starting transfers between devices: 9.01 us -> 35 us
  matrix products: 20.3 us -> 0 us
  between operations: 17.2 us -> 1.57 us
  Pallas kernels: 0 us -> 12.7 us
  local copies, waits for them, and re-layouts: 19.1 us -> 23.5 us
    all_gather x4 -> x0, waiting for transfers between devices: 143 us -> none  [the longest x1 63.9 us: body(): lax.all_gather(w_qkv, 'dp', axis=1, tiled=True)]
    psum x2 -> x0, blocking collectives: 81.9 us -> none  [the longest x1 41.1 us: body(): loss = lax.psum(local_loss, ('dp', 'space')) / (field_count * weight_all)]
    dot_general x9 -> x0, matrix products: 20.3 us -> none  [the longest x2 5.52 us: attend(): jnp.einsum('gtz,gxtz->gtx', split_query_heads, split_key_heads, preferred...]
    unnamed x18 -> x56, local copies, waits for them, and re-layouts: 0.04 us -> 19.2 us
    ppermute x6 -> x18, starting transfers between devices: 8.85 us -> 22.4 us  [the longest x6 11.7 us: over_pair(): return lax.ppermute(x, 'space', pair)]
    pallas_call x0 -> x5, Pallas kernels: none -> 12.7 us  [call(): pl.pallas_call(kernel, out_shape=out_shape, in_specs=specs, out_specs=tup...]
    all_to_all x0 -> x1, starting transfers between devices: none -> 12.5 us  [small_body(): parts = lax.all_to_all(sums, ('dp', 'space'), 0, 0)]
    all_gather x2 -> x0, blocking collectives: 11.9 us -> none  [the longest x1 6.56 us: body(): lax.all_gather(w_embed, 'dp', axis=1, tiled=True)]
  transfers between devices with their start and end apart: 10 -> 19, of which waited for: 6 -> 5; matrix products, arithmetic and copies ran while one was open for 13% -> 11% of each run, Pallas kernels for 0% -> 9%
where the time goes in v1:
time: 99.8 us; the launch traced here: 98.5 us
  starting transfers between devices  35 us (35%)
  local copies, waits for them, and re-layouts  23.5 us (24%)
  waiting for transfers between devices  20.9 us (21%)
  Pallas kernels  12.7 us (13%)
  other arithmetic  4.93 us (5%)
  between operations  1.57 us (2%)
    unnamed x56, local copies, waits for them, and re-layouts  19.2 us
    ppermute x8, waiting for transfers between devices, over_dp(): return lax.ppermute(x, 'dp', swap)  13.1 us
    pallas_call x5, Pallas kernels, call(): pl.pallas_call(kernel, out_shape=out_shape, in_specs=specs, out_specs=tup...  12.7 us
    all_to_all x1, starting transfers between devices, small_body(): parts = lax.all_to_all(sums, ('dp', 'space'), 0, 0)  12.5 us
    ppermute x6, starting transfers between devices, over_pair(): return lax.ppermute(x, 'space', pair)  11.7 us
    ppermute x8, starting transfers between devices, over_dp(): return lax.ppermute(x, 'dp', swap)  8.15 us
    all_to_all x1, waiting for transfers between devices, small_body(): parts = lax.all_to_all(sums, ('dp', 'space'), 0, 0)  7.51 us
  transfers between devices with their start and end apart: 19, of which 5 were waited for; matrix products, arithmetic and copies ran while one was open for 11% of the time, Pallas kernels for 9%

profile of v1, /device:TPU:0, one launch (start us, length us, event | category | flops | bytes accessed | tf_op | source)
XLA Modules:
  0.0 98.5 jit_solution(12450547405839989361)
XLA Ops:
  1.5 3.0 %collective-permute-start.2 = (bf16[128,100]{1,0:T(8,128)(2,1)S(1)}, bf16[128,100]{1,0:T(8,128)(2,1)S(1)}, u32[]{:S(2)}, u32[]{:S(2)}) collective-permute-start(bf16[128,100]{1,0:T(8,128)(2,1)S(1)} %bitcast.11), channel_id=1, source_target_pairs={{0,16},{16,0},{1,17},{17,1},{2,18},{18,2},{3,19},{19,3},{4,20},{20... | collective-permute-start | bytes 76808 | tf_op jit(solution)/shard_map/ppermute | solution.py:222
  8.4 1.9 %constant_dynamic-slice_fusion = bf16[512,512]{1,0:T(8,128)(2,1)} fusion(bf16[1024,1536]{1,0:T(8,128)(2,1)} %w_ref.3, s32[]{:T(128)S(6)} %select_n.190), kind=kLoop, calls=%fused_computation.58 | loop fusion | bytes 1048580 | tf_op jit(solution)/shard_map/dynamic_slice | solution.py:237
  10.3 1.9 %constant_dynamic-slice_fusion.1 = bf16[512,512]{1,0:T(8,128)(2,1)} fusion(bf16[1024,512]{1,0:T(8,128)(2,1)} %w1_ref.1, s32[]{:T(128)S(6)} %select_n.190), kind=kLoop, calls=%fused_computation.59 | loop fusion | bytes 1048580 | tf_op jit(solution)/shard_map/dynamic_slice | solution.py:239
  13.0 5.8 %collective-permute-start.3 = (bf16[128,100]{1,0:T(8,128)(2,1)S(1)}, bf16[128,100]{1,0:T(8,128)(2,1)S(1)}, u32[]{:S(2)}, u32[]{:S(2)}) collective-permute-start(bf16[128,100]{1,0:T(8,128)(2,1)S(1)} %collective-permute-done.2.oth), channel_id=1, source_target_pairs={{0,1},{1,0},{2,3},{3,2},{4,5},{5,4},{6,7},{7,6},{8,9},{9,8},{10,11... | collective-permute-start | bytes 76808 | tf_op jit(solution)/shard_map/ppermute | solution.py:225
  18.9 1.0 %copy.37.w2_ref = bf16[512,100]{1,0:T(8,128)(2,1)S(1)} copy(bf16[512,100]{0,1:T(8,128)(2,1)} %param.27) | data formatting | bytes 204800 | tf_op args[13]
  21.4 1.7 %collective-permute-start.15 = (bf16[512,512]{1,0:T(8,128)(2,1)}, bf16[512,512]{1,0:T(8,128)(2,1)}, u32[]{:S(2)}, u32[]{:S(2)}) collective-permute-start(bf16[512,512]{1,0:T(8,128)(2,1)} %constant_dynamic-slice_fusion.1), channel_id=1, source_target_pairs={{0,16},{16,0},{1,17},{17,1},{2,18},{18,2},{3,19},{19,3},{4,20},{20... | collective-permute-start | bytes 1572872 | tf_op jit(solution)/shard_map/ppermute | solution.py:222
  25.4 1.0 copy-done.5
  27.2 1.6 %copy-done.9 = bf16[1024,1024]{1,0:T(8,128)(2,1)S(1)} copy-done((bf16[1024,1024]{1,0:T(8,128)(2,1)S(1)}, bf16[1024,1024]{1,0:T(8,128)(2,1)}, u32[]{:S(2)}) %copy-start.9) | copy-done | bytes 2097176
  28.8 0.9 copy-done.10
  34.4 5.2 %shard_map.149 = (bf16[768,1024]{1,0:T(8,128)(2,1)S(1)}, bf16[16,768]{1,0:T(8,128)(2,1)}) custom-call(s32[2]{0:T(128)S(1)} %pad_add_fusion.place, bf16[128,100]{1,0:T(8,128)(2,1)S(1)} %bitcast.15, bf16[128,100]{1,0:T(8,128)(2,1)S(1)} %copy-done.16, bf16[128,100]{1,0:T(8,128)(2,1)S(1)} %copy-done.18, bf16[128,100]{1,0:T(8,128)(2,1)S(1)} %copy-done.14, ...), custom_call_target="tpu_custom_call" | custom-call | flops 1767899136 | bytes 3012616 | tf_op jit(solution)/shard_map/pallas_call | solution.py:42
  39.7 1.2 %copy-done.2 = bf16[768,1024]{1,0:T(8,128)(2,1)} copy-done((bf16[768,1024]{1,0:T(8,128)(2,1)}, bf16[768,1024]{1,0:T(8,128)(2,1)S(1)}, u32[]{:S(2)}) %copy-start.2) | copy-done | bytes 1572888
  40.8 1.7 %collective-permute-start.6 = (bf16[16,768]{1,0:T(8,128)(2,1)}, bf16[16,768]{1,0:T(8,128)(2,1)S(1)}, u32[]{:S(2)}, u32[]{:S(2)}) collective-permute-start(bf16[16,768]{1,0:T(8,128)(2,1)} %get-tuple-element.8), channel_id=1, source_target_pairs={{0,16},{16,0},{1,17},{17,1},{2,18},{18,2},{3,19},{19,3},{4,20},{20... | collective-permute-start | bytes 73736 | tf_op jit(solution)/shard_map/ppermute | solution.py:222
  42.6 6.5 %collective-permute-done.6.probs = bf16[16,768]{1,0:T(8,128)(2,1)S(1)} collective-permute-done((bf16[16,768]{1,0:T(8,128)(2,1)}, bf16[16,768]{1,0:T(8,128)(2,1)S(1)}, u32[]{:S(2)}, u32[]{:S(2)}) %collective-permute-start.6) | collective-permute-done | bytes 24608 | tf_op jit(solution)/shard_map/ppermute | solution.py:222
  49.1 1.4 %copy-done.3 = bf16[768,1024]{1,0:T(8,128)(2,1)S(1)} copy-done((bf16[768,1024]{1,0:T(8,128)(2,1)S(1)}, bf16[768,1024]{1,0:T(8,128)(2,1)}, u32[]{:S(2)}) %copy-start.3) | copy-done | bytes 1572888
  52.3 3.9 %collective-permute-done.7 = bf16[64,1024]{1,0:T(8,128)(2,1)S(1)} collective-permute-done((bf16[64,1024]{1,0:T(8,128)(2,1)S(1)}, bf16[64,1024]{1,0:T(8,128)(2,1)S(1)}, u32[]{:S(2)}, u32[]{:S(2)}) %collective-permute-start.7) | collective-permute-done | bytes 131104 | tf_op jit(solution)/shard_map/ppermute | solution.py:222
  57.6 3.8 %collective-permute-start.16 = (bf16[512,512]{1,0:T(8,128)(2,1)}, bf16[512,512]{1,0:T(8,128)(2,1)}, u32[]{:S(2)}, u32[]{:S(2)}) collective-permute-start(bf16[512,512]{1,0:T(8,128)(2,1)} %collective-permute-done.15.same_ref), channel_id=1, source_target_pairs={{0,1},{1,0},{2,3},{3,2},{4,5},{5,4},{6,7},{7,6},{8,9},{9,8},{10,11... | collective-permute-start | bytes 1572872 | tf_op jit(solution)/shard_map/ppermute | solution.py:225
  61.5 3.1 %shard_map.151 = (f32[32,1024]{1,0:T(8,128)S(1)}, bf16[32,1024]{1,0:T(8,128)(2,1)S(1)}) custom-call(s32[2]{0:T(128)S(1)} %pad_add_fusion.place, bf16[64,1024]{1,0:T(8,128)(2,1)S(1)} %maximum_select_fusion.lat0, bf16[64,1024]{1,0:T(8,128)(2,1)S(1)} %collective-permute-done.8.lat1, bf16[64,1024]{1,0:T(8,128)(2,1)S(1)} %collective-permute-done.9.lat2, ...), custom_call_target="tpu_custom_call" | custom-call | flops 603979776 | bytes 5685256 | tf_op jit(solution)/shard_map/pallas_call | solution.py:42
  66.9 2.7 %collective-permute-done.12 = bf16[32,1024]{1,0:T(8,128)(2,1)S(1)} collective-permute-done((bf16[32,1024]{1,0:T(8,128)(2,1)S(1)}, bf16[32,1024]{1,0:T(8,128)(2,1)S(1)}, u32[]{:S(2)}, u32[]{:S(2)}) %collective-permute-start.12) | collective-permute-done | bytes 65568 | tf_op jit(solution)/shard_map/ppermute | solution.py:222
  69.6 0.9 add_convert_fusion.up0
  70.5 1.4 %collective-permute-start.13 = (bf16[32,1024]{1,0:T(8,128)(2,1)S(1)}, bf16[32,1024]{1,0:T(8,128)(2,1)S(1)}, u32[]{:S(2)}, u32[]{:S(2)}) collective-permute-start(bf16[32,1024]{1,0:T(8,128)(2,1)S(1)} %add_convert_fusion.up0), channel_id=1, source_target_pairs={{0,1},{1,0},{2,3},{3,2},{4,5},{5,4},{6,7},{7,6},{8,9},{9,8},{10,11... | collective-permute-start | bytes 196616 | tf_op jit(solution)/shard_map/ppermute | solution.py:225
  72.8 1.2 %copy-done.1 = bf16[1024,512]{1,0:T(8,128)(2,1)S(1)} copy-done((bf16[1024,512]{1,0:T(8,128)(2,1)S(1)}, bf16[1024,512]{1,0:T(8,128)(2,1)}, u32[]{:S(2)}) %copy-start.1) | copy-done | bytes 1048600
  74.0 3.1 %shard_map.152 = (bf16[128,100]{1,0:T(8,128)(2,1)S(1)}, f32[32,8,100]{2,1,0:T(8,128)}) custom-call(s32[2]{0:T(128)S(1)} %pad_add_fusion.place, bf16[32,1024]{1,0:T(8,128)(2,1)S(1)} %add_convert_fusion.up0, bf16[32,1024]{1,0:T(8,128)(2,1)S(1)} %collective-permute-done.13.up1, bf16[32,1024]{1,0:T(8,128)(2,1)S(1)} %collective-permute-done.14.up2, ...), custom_call_target="tpu_custom_call" | custom-call | flops 294649856 | bytes 2575368 | tf_op jit(solution)/shard_map/pallas_call | solution.py:42
  77.1 12.5 %all-to-all-start = ((f32[32,8,100]{2,1,0:T(8,128)}), f32[32,8,100]{2,1,0:T(8,128)S(1)}, u32[]{:S(2)}, u32[]{:S(2)}) async-start(f32[32,8,100]{2,1,0:T(8,128)} %get-tuple-element.13), calls=%async_computation | async-start | bytes 262144 | tf_op jit(solution)/shard_map/all_to_all | solution.py:318
  90.4 7.5 %all-to-all-done.parts = f32[32,8,100]{2,1,0:T(8,128)S(1)} async-done(((f32[32,8,100]{2,1,0:T(8,128)}), f32[32,8,100]{2,1,0:T(8,128)S(1)}, u32[]{:S(2)}, u32[]{:S(2)}) %all-to-all-start) | async-done | bytes 102432 | tf_op jit(solution)/shard_map/all_to_all | solution.py:318
  (98 shorter events, 21.9 us)
Async XLA Ops:
  1.5 11.5 %collective-permute-start.2 = (bf16[128,100]{1,0:T(8,128)(2,1)S(1)}, bf16[128,100]{1,0:T(8,128)(2,1)S(1)}, u32[]{:S(2)}, u32[]{:S(2)}) collective-permute-start(bf16[128,100]{1,0:T(8,128)(2,1)S(1)} %bitcast.11), channel_id=1, source_target_pairs={{0,16},{16,0},{1,17},{17,1},{2,18},{18,2},{3,19},{19,3},{4,20},{20... | collective-permute-start | bytes 76808 | tf_op jit(solution)/shard_map/ppermute | solution.py:222
  4.5 15.4 %collective-permute-start = (bf16[128,100]{1,0:T(8,128)(2,1)S(1)}, bf16[128,100]{1,0:T(8,128)(2,1)S(1)}, u32[]{:S(2)}, u32[]{:S(2)}) collective-permute-start(bf16[128,100]{1,0:T(8,128)(2,1)S(1)} %bitcast.12), channel_id=1, source_target_pairs={{0,1},{1,0},{2,3},{3,2},{4,5},{5,4},{6,7},{7,6},{8,9},{9,8},{10,11... | collective-permute-start | bytes 76808 | tf_op jit(solution)/shard_map/ppermute | solution.py:225
  4.5 16.3 %collective-permute-start.1 = (bf16[128,100]{1,0:T(8,128)(2,1)S(1)}, bf16[128,100]{1,0:T(8,128)(2,1)S(1)}, u32[]{:S(2)}, u32[]{:S(2)}) collective-permute-start(bf16[128,100]{1,0:T(8,128)(2,1)S(1)} %bitcast.13), channel_id=1, source_target_pairs={{1,2},{3,4},{5,6},{7,8},{9,10},{11,12},{13,14},{2,1},{4,3},{6,5},{... | collective-permute-start | bytes 76808 | tf_op jit(solution)/shard_map/ppermute | solution.py:228
  5.2 18.0 %collective-permute-start.4 = (bf16[128,100]{1,0:T(8,128)(2,1)S(1)}, bf16[128,100]{1,0:T(8,128)(2,1)S(1)}, u32[]{:S(2)}, u32[]{:S(2)}) collective-permute-start(bf16[128,100]{1,0:T(8,128)(2,1)S(1)} %bitcast.14), channel_id=1, source_target_pairs={{1,18},{3,20},{5,22},{7,24},{9,26},{11,28},{13,30},{2,17},{4,19},{... | collective-permute-start | bytes 76808 | tf_op jit(solution)/shard_map/ppermute | solution.py:232
  5.8 18.9 %collective-permute-start.5 = (bf16[100,512]{1,0:T(8,128)(2,1)}, bf16[100,512]{1,0:T(8,128)(2,1)S(1)}, u32[]{:S(2)}, u32[]{:S(2)}) collective-permute-start(bf16[100,512]{1,0:T(8,128)(2,1)} %we_here.1), channel_id=1, source_target_pairs={{0,16},{16,0},{1,17},{17,1},{2,18},{18,2},{3,19},{19,3},{4,20},{20... | collective-permute-start | bytes 307208 | tf_op jit(solution)/shard_map/ppermute | solution.py:222
  13.0 11.7 %copy-start.13 = (bf16[128,100]{1,0:T(8,128)(2,1)}, bf16[128,100]{1,0:T(8,128)(2,1)S(1)}, u32[]{:S(2)}) copy-start(bf16[128,100]{1,0:T(8,128)(2,1)S(1)} %collective-permute-done.2.oth) | copy-start | bytes 76804
  13.0 11.1 %collective-permute-start.3 = (bf16[128,100]{1,0:T(8,128)(2,1)S(1)}, bf16[128,100]{1,0:T(8,128)(2,1)S(1)}, u32[]{:S(2)}, u32[]{:S(2)}) collective-permute-start(bf16[128,100]{1,0:T(8,128)(2,1)S(1)} %collective-permute-done.2.oth), channel_id=1, source_target_pairs={{0,1},{1,0},{2,3},{3,2},{4,5},{5,4},{6,7},{7,6},{8,9},{9,8},{10,11... | collective-permute-start | bytes 76808 | tf_op jit(solution)/shard_map/ppermute | solution.py:225
  20.5 35.7 %collective-permute-start.10 = (bf16[512,512]{1,0:T(8,128)(2,1)}, bf16[512,512]{1,0:T(8,128)(2,1)}, u32[]{:S(2)}, u32[]{:S(2)}) collective-permute-start(bf16[512,512]{1,0:T(8,128)(2,1)} %constant_dynamic-slice_fusion), channel_id=1, source_target_pairs={{0,16},{16,0},{1,17},{17,1},{2,18},{18,2},{3,19},{19,3},{4,20},{20... | collective-permute-start | bytes 1572872 | tf_op jit(solution)/shard_map/ppermute | solution.py:222
  21.4 36.2 %collective-permute-start.15 = (bf16[512,512]{1,0:T(8,128)(2,1)}, bf16[512,512]{1,0:T(8,128)(2,1)}, u32[]{:S(2)}, u32[]{:S(2)}) collective-permute-start(bf16[512,512]{1,0:T(8,128)(2,1)} %constant_dynamic-slice_fusion.1), channel_id=1, source_target_pairs={{0,16},{16,0},{1,17},{17,1},{2,18},{18,2},{3,19},{19,3},{4,20},{20... | collective-permute-start | bytes 1572872 | tf_op jit(solution)/shard_map/ppermute | solution.py:222
  23.8 48.8 %collective-permute-start.17 = (bf16[512,100]{1,0:T(8,128)(2,1)S(1)}, bf16[512,100]{1,0:T(8,128)(2,1)S(1)}, u32[]{:S(2)}, u32[]{:S(2)}) collective-permute-start(bf16[512,100]{1,0:T(8,128)(2,1)S(1)} %copy.37.w2_ref), channel_id=1, source_target_pairs={{0,16},{16,0},{1,17},{17,1},{2,18},{18,2},{3,19},{19,3},{4,20},{20... | collective-permute-start | bytes 307208 | tf_op jit(solution)/shard_map/ppermute | solution.py:222
  34.4 14.7 %copy-start.8 = (bf16[32,1024]{1,0:T(8,128)(2,1)S(1)}, bf16[32,1024]{1,0:T(8,128)(2,1)}, u32[]{:S(2)}) copy-start(bf16[32,1024]{1,0:T(8,128)(2,1)} %query.3) | copy-start | bytes 196612
  34.4 23.2 %copy-start.24 = (s32[128,3]{0,1:T(4,128)S(1)}, s32[128,3]{0,1:T(4,128)}, u32[]{:S(2)}) copy-start(s32[128,3]{0,1:T(4,128)} %param.21) | copy-start | bytes 4612
  34.4 27.1 %copy-start = (bf16[1024,1536]{1,0:T(8,128)(2,1)S(1)}, bf16[1024,1536]{1,0:T(8,128)(2,1)}, u32[]{:S(2)}) copy-start(bf16[1024,1536]{1,0:T(8,128)(2,1)} %w_ref.3) | copy-start | bytes 9437188
  40.8 8.3 %collective-permute-start.6 = (bf16[16,768]{1,0:T(8,128)(2,1)}, bf16[16,768]{1,0:T(8,128)(2,1)S(1)}, u32[]{:S(2)}, u32[]{:S(2)}) collective-permute-start(bf16[16,768]{1,0:T(8,128)(2,1)} %get-tuple-element.8), channel_id=1, source_target_pairs={{0,16},{16,0},{1,17},{17,1},{2,18},{18,2},{3,19},{19,3},{4,20},{20... | collective-permute-start | bytes 73736 | tf_op jit(solution)/shard_map/ppermute | solution.py:222
  50.5 11.0 %copy-start.4 = (bf16[512,1024]{1,0:T(8,128)(2,1)S(1)}, bf16[512,1024]{1,0:T(8,128)(2,1)}, u32[]{:S(2)}) copy-start(bf16[512,1024]{1,0:T(8,128)(2,1)} %wo_ref.1) | copy-start | bytes 3145732
  51.2 5.0 %collective-permute-start.7 = (bf16[64,1024]{1,0:T(8,128)(2,1)S(1)}, bf16[64,1024]{1,0:T(8,128)(2,1)S(1)}, u32[]{:S(2)}, u32[]{:S(2)}) collective-permute-start(bf16[64,1024]{1,0:T(8,128)(2,1)S(1)} %shard_map.150), channel_id=1, source_target_pairs={{0,16},{16,0},{1,17},{17,1},{2,18},{18,2},{3,19},{19,3},{4,20},{20... | collective-permute-start | bytes 393224 | tf_op jit(solution)/shard_map/ppermute | solution.py:222
  56.2 5.3 %collective-permute-start.11 = (bf16[512,512]{1,0:T(8,128)(2,1)}, bf16[512,512]{1,0:T(8,128)(2,1)S(1)}, u32[]{:S(2)}, u32[]{:S(2)}) collective-permute-start(bf16[512,512]{1,0:T(8,128)(2,1)} %collective-permute-done.10.same_ref), channel_id=1, source_target_pairs={{0,1},{1,0},{2,3},{3,2},{4,5},{5,4},{6,7},{7,6},{8,9},{9,8},{10,11... | collective-permute-start | bytes 1572872 | tf_op jit(solution)/shard_map/ppermute | solution.py:225
  56.4 5.1 %collective-permute-start.8 = (bf16[64,1024]{1,0:T(8,128)(2,1)S(1)}, bf16[64,1024]{1,0:T(8,128)(2,1)S(1)}, u32[]{:S(2)}, u32[]{:S(2)}) collective-permute-start(bf16[64,1024]{1,0:T(8,128)(2,1)S(1)} %maximum_select_fusion.lat0), channel_id=1, source_target_pairs={{0,1},{1,0},{2,3},{3,2},{4,5},{5,4},{6,7},{7,6},{8,9},{9,8},{10,11... | collective-permute-start | bytes 393224 | tf_op jit(solution)/shard_map/ppermute | solution.py:225
  56.9 4.6 %collective-permute-start.9 = (bf16[64,1024]{1,0:T(8,128)(2,1)S(1)}, bf16[64,1024]{1,0:T(8,128)(2,1)S(1)}, u32[]{:S(2)}, u32[]{:S(2)}) collective-permute-start(bf16[64,1024]{1,0:T(8,128)(2,1)S(1)} %maximum_select_fusion.lat0), channel_id=1, source_target_pairs={{1,2},{3,4},{5,6},{7,8},{9,10},{11,12},{13,14},{2,1},{4,3},{6,5},{... | collective-permute-start | bytes 393224 | tf_op jit(solution)/shard_map/ppermute | solution.py:228
  57.6 15.0 %collective-permute-start.16 = (bf16[512,512]{1,0:T(8,128)(2,1)}, bf16[512,512]{1,0:T(8,128)(2,1)}, u32[]{:S(2)}, u32[]{:S(2)}) collective-permute-start(bf16[512,512]{1,0:T(8,128)(2,1)} %collective-permute-done.15.same_ref), channel_id=1, source_target_pairs={{0,1},{1,0},{2,3},{3,2},{4,5},{5,4},{6,7},{7,6},{8,9},{9,8},{10,11... | collective-permute-start | bytes 1572872 | tf_op jit(solution)/shard_map/ppermute | solution.py:225
  65.3 4.3 %collective-permute-start.12 = (bf16[32,1024]{1,0:T(8,128)(2,1)S(1)}, bf16[32,1024]{1,0:T(8,128)(2,1)S(1)}, u32[]{:S(2)}, u32[]{:S(2)}) collective-permute-start(bf16[32,1024]{1,0:T(8,128)(2,1)S(1)} %get-tuple-element.11), channel_id=1, source_target_pairs={{0,16},{16,0},{1,17},{17,1},{2,18},{18,2},{3,19},{19,3},{4,20},{20... | collective-permute-start | bytes 196616 | tf_op jit(solution)/shard_map/ppermute | solution.py:222
  70.5 2.3 %collective-permute-start.13 = (bf16[32,1024]{1,0:T(8,128)(2,1)S(1)}, bf16[32,1024]{1,0:T(8,128)(2,1)S(1)}, u32[]{:S(2)}, u32[]{:S(2)}) collective-permute-start(bf16[32,1024]{1,0:T(8,128)(2,1)S(1)} %add_convert_fusion.up0), channel_id=1, source_target_pairs={{0,1},{1,0},{2,3},{3,2},{4,5},{5,4},{6,7},{7,6},{8,9},{9,8},{10,11... | collective-permute-start | bytes 196616 | tf_op jit(solution)/shard_map/ppermute | solution.py:225
  71.9 0.9 collective-permute-start.14
  77.1 20.8 %all-to-all-start = ((f32[32,8,100]{2,1,0:T(8,128)}), f32[32,8,100]{2,1,0:T(8,128)S(1)}, u32[]{:S(2)}, u32[]{:S(2)}) async-start(f32[32,8,100]{2,1,0:T(8,128)} %get-tuple-element.13), calls=%async_computation | async-start | bytes 262144 | tf_op jit(solution)/shard_map/all_to_all | solution.py:318
  (21 other events, 37.3 us)

commit v2 on v0

--- a/solution.py
+++ b/solution.py
@@ -3,9 +3,378 @@
 import jax
 import jax.numpy as jnp
 from jax import lax
+from jax.experimental import pallas as pl
+from jax.experimental.pallas import tpu as pltpu
 from jax.sharding import PartitionSpec as P
 
 HEADS = 16
+F32 = jnp.float32
+BF16 = jnp.bfloat16
+
+
+def silu(x):
+    return 0.5 * x * (1.0 + jnp.tanh(0.5 * x))
+
+
+def dot(a, b):
+    return jnp.dot(a, b, preferred_element_type=F32)
+
+
+def dot_nt(a, b, precision=None):
+    return lax.dot_general(
+        a, b, (((1,), (1,)), ((), ())), preferred_element_type=F32, precision=precision
+    )
+
+
+def normalize(values):
+    centre = jnp.mean(values, axis=-1, keepdims=True)
+    shifted = values - centre
+    spread = jnp.mean(shifted * shifted, axis=-1, keepdims=True)
+    return shifted * lax.rsqrt(spread + 1e-05)
+
+
+def shape(dims, dtype=BF16):
+    return jax.ShapeDtypeStruct(tuple(dims), dtype)
+
+
+def call(kernel, outs, args, scratch=(), flops=0, smem=()):
+    size = sum(math.prod(a.shape) * a.dtype.itemsize for a in args)
+    return pl.pallas_call(
+        kernel,
+        out_shape=tuple(outs),
+        in_specs=[
+            pl.BlockSpec(memory_space=pltpu.SMEM if i in smem else pltpu.VMEM)
+            for i in range(len(args))
+        ],
+        out_specs=(pl.BlockSpec(memory_space=pltpu.VMEM),) * len(outs),
+        scratch_shapes=list(scratch),
+        compiler_params=pltpu.CompilerParams(vmem_limit_bytes=24 * 1024 * 1024),
+        cost_estimate=pl.CostEstimate(flops=flops, bytes_accessed=size, transcendentals=0),
+    )(*args)
+
+
+def cut(w, column, width):
+    pieces = 8
+    size = w.shape[0] // 4
+    step = size // pieces
+
+    def kernel(w_ref, out_ref, sems):
+        start = (lax.axis_index("space") % 4) * size
+        copies = [
+            pltpu.make_async_copy(
+                w_ref.at[
+                    pl.ds(pl.multiple_of(start + i * step, step), step), pl.ds(column, width)
+                ],
+                out_ref.at[pl.ds(i * step, step), :],
+                sems.at[i],
+            )
+            for i in range(pieces)
+        ]
+        for copy in copies:
+            copy.start()
+        for copy in copies:
+            copy.wait()
+
+    return pl.pallas_call(
+        kernel,
+        out_shape=shape((size, width)),
+        in_specs=[pl.BlockSpec(memory_space=pltpu.HBM)],
+        out_specs=pl.BlockSpec(memory_space=pltpu.VMEM),
+        scratch_shapes=[pltpu.SemaphoreType.DMA((pieces,))],
+        compiler_params=pltpu.CompilerParams(vmem_limit_bytes=58 * 1024 * 1024),
+        cost_estimate=pl.CostEstimate(flops=0, bytes_accessed=0, transcendentals=0),
+    )(w)
+
+
+def side_block(index, size):
+    odd = lax.axis_index("space") % 2
+    side = index // size
+    block = jnp.where(side == 1, 0, jnp.where((side == 2) == (odd == 0), 1, 2))
+    return block * size + index % size
+
+
+def encode_kernel(
+    query_ref, index_ref, own, own1, own2, oth, oth1, oth2, we_here, we_there, w_ref,
+    pairs_ref, probs_ref,
+):
+    nodes, width = query_ref.shape
+    entries = index_ref.shape[0]
+    rows = nodes * entries
+    per_head = width // HEADS
+    ours = lax.axis_index("dp")
+    index = jnp.transpose(index_ref[...])
+    entry = jnp.concatenate([index[:, k : k + 1] for k in range(entries)], axis=0)
+    head_of = lax.broadcasted_iota(jnp.int32, (width, 128), 0) // per_head
+    fold = (head_of == lax.broadcasted_iota(jnp.int32, (width, 128), 1)).astype(BF16)
+    queries = jnp.broadcast_to(query_ref[...].astype(F32)[None], (entries, nodes, width))
+    queries = queries.reshape(rows, width)
+    present = jnp.broadcast_to(entry >= 0, (rows, 128))
+    slots = own.shape[1]
+    place = jnp.where(entry >= 0, side_block(jnp.maximum(entry, 0), slots), -1)
+    lane = lax.broadcasted_iota(jnp.int32, (rows, slots), 1)
+    pick = [(place == lane + i * slots).astype(BF16) for i in range(3)]
+    half = we_here.shape[1]
+    here = pl.multiple_of(ours * half, half)
+    there = pl.multiple_of((1 - ours) * half, half)
+    for s in range(2):
+        near = 0.0
+        for i, (mine, theirs) in enumerate(((own, oth), (own1, oth1), (own2, oth2))):
+            near += dot_nt(pick[i], jnp.where(ours == s, mine[...], theirs[...]))
+        near = near.astype(BF16)
+        embed_here = silu(dot(near, we_here[...])).astype(BF16)
+        embed_there = silu(dot(near, we_there[...])).astype(BF16)
+        pairs = dot(embed_here, w_ref[pl.ds(here, half), :])
+        pairs = (pairs + dot(embed_there, w_ref[pl.ds(there, half), :])).astype(BF16)
+        pairs_ref[s * rows : (s + 1) * rows, :] = pairs
+        product = pairs.astype(F32) * queries
+        high = product.astype(BF16)
+        low = (product - high.astype(F32)).astype(BF16)
+        logits = (dot(high, fold) + dot(low, fold)) * (1.0 / math.sqrt(per_head))
+        logits = jnp.where(present, logits, -1e30).reshape(entries, nodes, 128)
+        top = jnp.max(logits, axis=0, keepdims=True)
+        weight = jnp.where(present.reshape(entries, nodes, 128), jnp.exp(logits - top), 0.0)
+        weight = weight / jnp.sum(weight, axis=0, keepdims=True)
+        turned = jnp.transpose(weight.reshape(rows, 128))
+        probs_ref[:, s * rows : (s + 1) * rows] = turned[:HEADS].astype(BF16)
+
+
+def latent_kernel(query_ref, probs, pairs, latent_ref):
+    query = query_ref[...].astype(F32)
+    nodes, width = query.shape
+    rows = pairs.shape[0] // 2
+    entries = rows // nodes
+    per_head = width // HEADS
+    head_of = lax.broadcasted_iota(jnp.int32, (HEADS, width), 1) // per_head
+    spread = (head_of == lax.broadcasted_iota(jnp.int32, (HEADS, width), 0)).astype(BF16)
+    for s in range(2):
+        turned = probs[:, s * rows : (s + 1) * rows].astype(F32)
+        weight = jnp.transpose(turned).astype(BF16)
+        mixed = dot(weight, spread) * pairs[s * rows : (s + 1) * rows, :].astype(F32)
+        mixed = jnp.sum(mixed.reshape(entries, nodes, width), axis=0)
+        latent_ref[s * nodes : (s + 1) * nodes, :] = (query + mixed).astype(BF16)
+
+
+def choose_kernel(mine, theirs, w_ref, out_ref, part_ref):
+    first = lax.axis_index("dp") == 0
+    out_ref[...] = jnp.where(first, theirs[...], mine[...])
+    size = part_ref.shape[0]
+    start = pl.multiple_of((lax.axis_index("space") % 4) * size, size)
+    part_ref[...] = w_ref[pl.ds(start, size), :]
+
+
+def add_kernel(mine, theirs, out_ref):
+    out_ref[...] = (mine[...] + theirs[...].astype(F32)).astype(BF16)
+
+
+def mesh_kernel(
+    index_ref, lat0, lat1, lat2, w_ref, part0, part1, part2, part3, wo_ref,
+    keep_ref, send_ref, norm_ref, sums_ref,
+):
+    both, width = lat0.shape
+    nodes = both // 2
+    half = width // 2
+    rows = 3 * both
+    heads = HEADS // 2
+    per_head = half // heads
+    place = side_block(jnp.transpose(index_ref[...]), nodes)
+    near = lax.broadcasted_iota(jnp.int32, (nodes, rows), 1)
+    code = (near // both) * nodes + near % nodes
+    times = sum((place[:, j : j + 1] == code).astype(F32) for j in range(index_ref.shape[0]))
+    second = (near // nodes) % 2
+    times = jnp.concatenate(
+        [jnp.where(second == 0, times, 0.0), jnp.where(second == 1, times, 0.0)], axis=0
+    )[None]
+    for i, block in enumerate((lat0, lat1, lat2)):
+        norm_ref[i * both : (i + 1) * both, :] = normalize(block[...].astype(F32)).astype(BF16)
+    spot = lax.axis_index("space") % 4
+    ours = lax.axis_index("dp")
+    first = ours == 0
+    part_a = dot(norm_ref[...], w_ref[:, :half])
+    part_c = dot(norm_ref[...], w_ref[:, 2 * half :])
+    part_b = 0.0
+    for i, block in enumerate((part0, part1, part2, part3)):
+        size = block.shape[0]
+        part = pl.multiple_of((spot ^ i) * size, size)
+        part_b += dot(norm_ref[:, pl.ds(part, size)], block[...])
+    queries = jnp.where(first, part_a[:both], part_b[:both]).astype(BF16)
+    keys = jnp.where(first, part_c, part_a).astype(BF16)
+    values = jnp.where(first, part_b, part_c).astype(BF16)
+    head_of = lax.broadcasted_iota(jnp.int32, (both, half), 1) // per_head
+    zero = jnp.zeros_like(queries)
+    stacked = jnp.concatenate(
+        [jnp.where(head_of == h, queries, zero) for h in range(heads)], axis=0
+    )
+    logits = dot_nt(stacked, keys) * (1.0 / math.sqrt(per_head))
+    logits = logits.reshape(heads, both, rows)
+    logits = jnp.where(times > 0, logits, -1e30)
+    top = jnp.max(logits, axis=-1, keepdims=True)
+    weight = times * jnp.exp(logits - top)
+    weight = weight / jnp.sum(weight, axis=-1, keepdims=True)
+    mixed = dot(weight.astype(BF16).reshape(heads * both, rows), values)
+    mixed = mixed.reshape(heads, both, half)
+    total = jnp.where(head_of == 0, mixed[0], 0.0)
+    for h in range(1, heads):
+        total = jnp.where(head_of == h, mixed[h], total)
+    sums_ref[...] = dot(total.astype(BF16), wo_ref[...])
+    mine = pl.multiple_of(ours * nodes, nodes)
+    theirs = pl.multiple_of((1 - ours) * nodes, nodes)
+    keep_ref[...] = lat0[pl.ds(mine, nodes), :].astype(F32) + sums_ref[pl.ds(mine, nodes), :]
+    send_ref[...] = sums_ref[pl.ds(theirs, nodes), :].astype(BF16)
+
+
+def decode_kernel(
+    limit, index_ref, fields, target, area, up0, up1, up2,
+    w1_ref, part0, part1, part2, part3, w2_ref, w2_there,
+    pred_ref, sums_ref, norm_ref,
+):
+    count_field, slots = fields.shape
+    keep = lax.broadcasted_iota(jnp.int32, (8, slots), 1) < limit[0]
+    keep = keep.astype(F32)
+    weight = keep * area[...]
+    nodes, width = up0.shape
+    entries = index_ref.shape[0]
+    place = side_block(jnp.transpose(index_ref[...]), nodes)
+    near = lax.broadcasted_iota(jnp.int32, (slots, nodes), 1)
+    mean = 0.0
+    for i, updated in enumerate((up0, up1, up2)):
+        times = sum((place[:, k : k + 1] == near + i * nodes).astype(F32) for k in range(entries))
+        mean += dot(times.astype(BF16), updated[...])
+    norm_ref[...] = normalize(mean * (1.0 / entries)).astype(BF16)
+    spot = lax.axis_index("space") % 4
+    hidden = silu(dot(norm_ref[...], w1_ref[...])).astype(BF16)
+    hidden_there = 0.0
+    for i, block in enumerate((part0, part1, part2, part3)):
+        size = block.shape[0]
+        part = pl.multiple_of((spot ^ i) * size, size)
+        hidden_there += dot(norm_ref[:, pl.ds(part, size)], block[...])
+    hidden_there = silu(hidden_there).astype(BF16)
+    increment = dot_nt(w2_ref[...], hidden) + dot_nt(w2_there[...], hidden_there)
+    valid = keep[:1] > 0
+    predicted = jnp.where(valid, fields[...].astype(F32) + increment, 0.0)
+    pred_ref[...] = predicted.astype(BF16)
+    goal = target[...].astype(F32)
+    misfit = predicted - goal
+    errors = dot_nt(weight, misfit * misfit, lax.Precision.HIGHEST)
+    squares = dot_nt(keep, goal * goal, lax.Precision.HIGHEST)
+    here_count = jnp.broadcast_to(jnp.sum(keep, axis=1, keepdims=True), (8, count_field))
+    here_weight = jnp.broadcast_to(jnp.sum(weight, axis=1, keepdims=True), (8, count_field))
+    row = lax.broadcasted_iota(jnp.int32, (8, count_field), 0)
+    sums = jnp.where(
+        row == 0, errors, jnp.where(row == 1, squares, jnp.where(row == 2, here_count, here_weight))
+    )
+    sums_ref[...] = jnp.broadcast_to(sums[None], sums_ref.shape)
+
+
+def loss_kernel(parts, loss_ref):
+    total = jnp.sum(parts[...], axis=0)
+    fields = total.shape[1]
+    scaled = total[0:1] / (total[1:2] / total[2:3] + 1e-05)
+    weight = total[3:4, 0:1]
+    loss_ref[...] = jnp.sum(scaled, axis=1, keepdims=True) / (fields * weight)
+
+
+def small_body(
+    fields, target, area_weight, grid_count, mesh_query, enc_index, proc_index, dec_index,
+    w_embed, w_enc_kv, w_qkv, w_out, w_dec1, w_dec2,
+):
+    space = lax.axis_size("space")
+    samples = lax.axis_size("dp")
+    own = fields[0].T
+    goal = target[0].T
+    w2 = w_dec2.T
+    field_count, slots = own.shape
+    nodes, width = mesh_query.shape
+    half = width // 2
+    rows = nodes * enc_index.shape[1]
+
+    swap = [(0, 1), (1, 0)]
+    pair = [(i, i ^ 1) for i in range(space)]
+    link = [(i, i + 1) for i in range(1, space - 1, 2)]
+    link = link + [(j, i) for i, j in link]
+
+    def over_dp(x):
+        return lax.ppermute(x, "dp", swap)
+
+    def over_pair(x):
+        return lax.ppermute(x, "space", pair)
+
+    def over_link(x):
+        return lax.ppermute(x, "space", link)
+
+    def over_both(x, steps):
+        steps = [(d * space + i, (1 - d) * space + j) for d in range(2) for i, j in steps]
+        return lax.ppermute(x, ("dp", "space"), steps)
+
+    def over_quad(x):
+        return lax.ppermute(x, "space", [(i, i ^ 2) for i in range(space)])
+
+    def after(x, *others):
+        return lax.optimization_barrier((x,) + others)[0]
+
+    wq0 = cut(w_qkv, half, half)
+    own = after(own, wq0)
+    oth = over_dp(own)
+    we_there = over_dp(w_embed)
+    oth1 = over_both(own, pair)
+    oth2 = over_both(own, link)
+    own2 = over_link(own)
+    own1 = over_pair(own)
+    fetched = (own1, own2, oth2, oth1, we_there, oth, wq0)
+    own1, own2, oth2, oth1, we_there, oth, wq0 = lax.optimization_barrier(fetched)
+    wq0 = over_dp(wq0)
+
+    pairs, probs = call(
+        encode_kernel,
+        (shape((2 * rows, width)), shape((HEADS, 2 * rows))),
+        (mesh_query, enc_index.T, own, own1, own2, oth, oth1, oth2, w_embed, we_there, w_enc_kv),
+        flops=2 * 2 * rows * width * (width + field_count),
+    )
+    (latent,) = call(
+        latent_kernel,
+        (shape((2 * nodes, width)),),
+        (mesh_query, over_dp(probs), pairs),
+        flops=2 * 2 * rows * width * 128,
+    )
+    came = over_dp(latent)
+    wq0 = after(wq0, latent)
+    wq2 = over_quad(wq0)
+    wq1 = over_pair(after(wq0, came))
+    wq3 = over_pair(after(wq2, came))
+    latent, w10 = call(
+        choose_kernel,
+        (shape((2 * nodes, width)), shape((width // 4, half))),
+        (latent, came, w_dec1),
+    )
+    lat1 = over_pair(latent)
+    lat2 = over_link(latent)
+    w10 = over_dp(w10)
+    w2_there = over_dp(after(w2, latent))
+    w10 = after(w10, lat2)
+    w12 = over_quad(w10)
+    keep, send = call(
+        mesh_kernel,
+        (shape((nodes, width), F32), shape((nodes, width))),
+        (proc_index.T, latent, lat1, lat2, w_qkv, wq0, wq1, wq2, wq3, w_out),
+        scratch=[pltpu.VMEM((6 * nodes, width), BF16), pltpu.VMEM((2 * nodes, width), F32)],
+        flops=2 * 6 * nodes * width * 3 * half,
+    )
+    came = over_dp(send)
+    w11 = over_pair(after(w10, keep))
+    (updated,) = call(add_kernel, (shape((nodes, width)),), (keep, came))
+    w13 = over_pair(after(w12, updated))
+    predicted, sums = call(
+        decode_kernel,
+        (shape((field_count, slots)), shape((space * samples, 8, field_count), F32)),
+        (grid_count, dec_index.T, own, goal, area_weight[None], updated, over_pair(updated),
+         over_link(updated), w_dec1, w10, w11, w12, w13,
+         w2, w2_there),
+        scratch=[pltpu.VMEM((slots, width), BF16)],
+        flops=2 * slots * width * (width + field_count),
+        smem=(0,),
+    )
+    parts = lax.all_to_all(sums, ("dp", "space"), 0, 0)
+    (loss,) = call(loss_kernel, (shape((1, 1), F32),), (parts,))
+    return predicted.T[None], loss[0, 0]
 
 
 def with_halo(cells, sides, width):
@@ -49,7 +418,7 @@
     return aggregated_values.reshape(node_count, width)
 
 
-def body(
+def general_body(
     fields,
     target,
     area_weight,
@@ -157,6 +526,7 @@
         P(None, "dp"),
         P("dp", None),
     )
+    small = mesh.shape["dp"] == 2 and mesh.shape["space"] % 4 == 0
     return jax.shard_map(
-        body, mesh=mesh, in_specs=placed, out_specs=(P("dp", "space", None), P()), check_vma=False
-    )
+        small_body if small else general_body, mesh=mesh, in_specs=placed, out_specs=(P("dp", "space", None), P()), check_vma=False
+    )

time: 316 us -> 72.4 us (0.23)
  waiting for transfers between devices: 149 us -> 14.9 us
  blocking collectives: 93.8 us -> 13.8 us
  starting transfers between devices: 9.01 us -> 30.3 us
  matrix products: 20.3 us -> 0 us
  local copies, waits for them, and re-layouts: 19.1 us -> 0.07 us
  between operations: 17.2 us -> 1.55 us
  Pallas kernels: 0 us -> 11.5 us
  other arithmetic: 6.86 us -> 0 us
    all_gather x4 -> x0, waiting for transfers between devices: 143 us -> none  [the longest x1 63.9 us: body(): lax.all_gather(w_qkv, 'dp', axis=1, tiled=True)]
    psum x2 -> x0, blocking collectives: 81.9 us -> none  [the longest x1 41.1 us: body(): loss = lax.psum(local_loss, ('dp', 'space')) / (field_count * weight_all)]
    ppermute x6 -> x22, starting transfers between devices: 8.85 us -> 30.3 us  [the longest x8 10.8 us: over_dp(): return lax.ppermute(x, 'dp', swap)]
    dot_general x9 -> x0, matrix products: 20.3 us -> none  [the longest x2 5.52 us: attend(): jnp.einsum('gtz,gxtz->gtx', split_query_heads, split_key_heads, preferred...]
    all_to_all x0 -> x1, blocking collectives: none -> 13.8 us  [small_body(): parts = lax.all_to_all(sums, ('dp', 'space'), 0, 0)]
    all_gather x2 -> x0, blocking collectives: 11.9 us -> none  [the longest x1 6.56 us: body(): lax.all_gather(w_embed, 'dp', axis=1, tiled=True)]
    pallas_call x0 -> x8, Pallas kernels: none -> 11.5 us  [the longest x7 9.86 us: call(): pl.pallas_call(kernel, out_shape=tuple(outs), in_specs=[pl.BlockSpec(memo...]
    ppermute x6 -> x22, waiting for transfers between devices: 4.39 us -> 14.9 us  [the longest x8 11.9 us: over_dp(): return lax.ppermute(x, 'dp', swap)]
  transfers between devices with their start and end apart: 10 -> 22, of which waited for: 6 -> 7; matrix products, arithmetic and copies ran while one was open for 13% -> 0% of each run, Pallas kernels for 0% -> 12%
where the time goes in v2:
time: 72.4 us; the launch traced here: 72.1 us
  starting transfers between devices  30.3 us (42%)
  waiting for transfers between devices  14.9 us (21%)
  blocking collectives  13.8 us (19%)
  Pallas kernels  11.5 us (16%)
  between operations  1.55 us (2%)
    all_to_all x1, blocking collectives, small_body(): parts = lax.all_to_all(sums, ('dp', 'space'), 0, 0)  13.8 us
    ppermute x8, waiting for transfers between devices, over_dp(): return lax.ppermute(x, 'dp', swap)  11.9 us
    ppermute x8, starting transfers between devices, over_dp(): return lax.ppermute(x, 'dp', swap)  10.8 us
    pallas_call x7, Pallas kernels, call(): pl.pallas_call(kernel, out_shape=tuple(outs), in_specs=[pl.BlockSpec(memo...  9.86 us
    ppermute x2, starting transfers between devices, over_quad(): return lax.ppermute(x, 'space', [(i, i ^ 2) for i in range(space)])  6.74 us
    ppermute x2, starting transfers between devices, over_both(): return lax.ppermute(x, ('dp', 'space'), steps)  6.52 us
    ppermute x7, starting transfers between devices, over_pair(): return lax.ppermute(x, 'space', pair)  4.23 us
    ppermute x3, starting transfers between devices, over_link(): return lax.ppermute(x, 'space', link)  1.97 us
  transfers between devices with their start and end apart: 22, of which 7 were waited for; matrix products, arithmetic and copies ran while one was open for 0% of the time, Pallas kernels for 12%

profile of v2, /device:TPU:0, one launch (start us, length us, event | category | flops | bytes accessed | tf_op | source)
XLA Modules:
  0.0 72.1 jit_solution(17044216239087895600)
XLA Ops:
  0.7 3.0 %collective-permute-start.4 = (bf16[100,512]{1,0:T(8,128)(2,1)}, bf16[100,512]{1,0:T(8,128)(2,1)S(1)}, u32[]{:S(2)}, u32[]{:S(2)}) collective-permute-start(bf16[100,512]{1,0:T(8,128)(2,1)} %we_here.1), channel_id=1, source_target_pairs={{0,16},{16,0},{1,17},{17,1},{2,18},{18,2},{3,19},{19,3},{4,20},{20... | collective-permute-start | bytes 307208 | tf_op jit(solution)/shard_map/ppermute | solution.py:296
  3.7 1.6 %shard_map.149 = bf16[256,512]{1,0:T(8,128)(2,1)} custom-call(bf16[1024,1536]{1,0:T(8,128)(2,1)} %w_ref.7), custom_call_target="tpu_custom_call" | custom-call | tf_op jit(solution)/shard_map/pallas_call | solution.py:78
  5.4 0.7 collective-permute-start.1
  6.1 0.7 collective-permute-start.2
  6.8 5.9 %collective-permute-start.3 = (bf16[100,128]{1,0:T(8,128)(2,1)S(1)}, bf16[100,128]{1,0:T(8,128)(2,1)S(1)}, u32[]{:S(2)}, u32[]{:S(2)}) collective-permute-start(bf16[100,128]{1,0:T(8,128)(2,1)S(1)} %bitcast.20), channel_id=1, source_target_pairs={{0,17},{1,16},{2,19},{3,18},{4,21},{5,20},{6,23},{7,22},{8,25},{9,... | collective-permute-start | bytes 76808 | tf_op jit(solution)/shard_map/ppermute | solution.py:306
  12.8 1.6 %collective-permute-done.3.oth1 = bf16[100,128]{1,0:T(8,128)(2,1)S(1)} collective-permute-done((bf16[100,128]{1,0:T(8,128)(2,1)S(1)}, bf16[100,128]{1,0:T(8,128)(2,1)S(1)}, u32[]{:S(2)}, u32[]{:S(2)}) %collective-permute-start.3) | collective-permute-done | bytes 25632 | tf_op jit(solution)/shard_map/ppermute | solution.py:306
  14.4 2.1 %collective-permute-done.5.oth = bf16[100,128]{1,0:T(8,128)(2,1)S(1)} collective-permute-done((bf16[100,128]{1,0:T(8,128)(2,1)S(1)}, bf16[100,128]{1,0:T(8,128)(2,1)S(1)}, u32[]{:S(2)}, u32[]{:S(2)}) %collective-permute-start.5) | collective-permute-done | bytes 25632 | tf_op jit(solution)/shard_map/ppermute | solution.py:296
  17.1 4.5 %shard_map.150 = (bf16[768,1024]{1,0:T(8,128)(2,1)S(1)}, bf16[16,768]{1,0:T(8,128)(2,1)S(1)}) custom-call(bf16[32,1024]{1,0:T(8,128)(2,1)S(1)} %copy-done.4, s32[12,32]{1,0:T(8,128)S(1)} %bitcast.28, bf16[100,128]{1,0:T(8,128)(2,1)S(1)} %bitcast.22, bf16[100,128]{1,0:T(8,128)(2,1)S(1)} %collective-permute-done.own1, ...), custom_call_target="tpu_custom_call" | custom-call | flops 1767899136 | bytes 2522624 | tf_op jit(solution)/shard_map/pallas_call | solution.py:42
  21.6 1.5 %collective-permute-start.6 = (bf16[16,768]{1,0:T(8,128)(2,1)S(1)}, bf16[16,768]{1,0:T(8,128)(2,1)S(1)}, u32[]{:S(2)}, u32[]{:S(2)}) collective-permute-start(bf16[16,768]{1,0:T(8,128)(2,1)S(1)} %get-tuple-element.32), channel_id=1, source_target_pairs={{0,16},{16,0},{1,17},{17,1},{2,18},{18,2},{3,19},{19,3},{4,20},{20... | collective-permute-start | bytes 73736 | tf_op jit(solution)/shard_map/ppermute | solution.py:296
  23.1 2.4 %collective-permute-done.6.probs = bf16[16,768]{1,0:T(8,128)(2,1)S(1)} collective-permute-done((bf16[16,768]{1,0:T(8,128)(2,1)S(1)}, bf16[16,768]{1,0:T(8,128)(2,1)S(1)}, u32[]{:S(2)}, u32[]{:S(2)}) %collective-permute-start.6) | collective-permute-done | bytes 24608 | tf_op jit(solution)/shard_map/ppermute | solution.py:296
  26.1 1.5 %collective-permute-start.7 = (bf16[64,1024]{1,0:T(8,128)(2,1)S(1)}, bf16[64,1024]{1,0:T(8,128)(2,1)S(1)}, u32[]{:S(2)}, u32[]{:S(2)}) collective-permute-start(bf16[64,1024]{1,0:T(8,128)(2,1)S(1)} %shard_map.151.mine), channel_id=1, source_target_pairs={{0,16},{16,0},{1,17},{17,1},{2,18},{18,2},{3,19},{19,3},{4,20},{20... | collective-permute-start | bytes 393224 | tf_op jit(solution)/shard_map/ppermute | solution.py:296
  27.7 2.4 %collective-permute-start.12 = (bf16[256,512]{1,0:T(8,128)(2,1)S(1)}, bf16[256,512]{1,0:T(8,128)(2,1)S(1)}, u32[]{:S(2)}, u32[]{:S(2)}) collective-permute-start(bf16[256,512]{1,0:T(8,128)(2,1)S(1)} %collective-permute-done.10.part0), channel_id=1, source_target_pairs={{0,2},{1,3},{2,0},{3,1},{4,6},{5,7},{6,4},{7,5},{8,10},{9,11},{10,... | collective-permute-start | bytes 786440 | tf_op jit(solution)/shard_map/ppermute | solution.py:309
  30.1 1.1 %collective-permute-done.7.theirs = bf16[64,1024]{1,0:T(8,128)(2,1)S(1)} collective-permute-done((bf16[64,1024]{1,0:T(8,128)(2,1)S(1)}, bf16[64,1024]{1,0:T(8,128)(2,1)S(1)}, u32[]{:S(2)}, u32[]{:S(2)}) %collective-permute-start.7) | collective-permute-done | bytes 131104 | tf_op jit(solution)/shard_map/ppermute | solution.py:296
  31.2 2.2 %collective-permute-start.17 = (bf16[256,512]{1,0:T(8,128)(2,1)S(1)}, bf16[256,512]{1,0:T(8,128)(2,1)S(1)}, u32[]{:S(2)}, u32[]{:S(2)}) collective-permute-start(bf16[256,512]{1,0:T(8,128)(2,1)S(1)} %get-tuple-element.41), channel_id=1, source_target_pairs={{0,16},{16,0},{1,17},{17,1},{2,18},{18,2},{3,19},{19,3},{4,20},{20... | collective-permute-start | bytes 786440 | tf_op jit(solution)/shard_map/ppermute | solution.py:296
  34.0 3.8 %collective-permute-start.11 = (bf16[256,512]{1,0:T(8,128)(2,1)S(1)}, bf16[256,512]{1,0:T(8,128)(2,1)S(1)}, u32[]{:S(2)}, u32[]{:S(2)}) collective-permute-start(bf16[256,512]{1,0:T(8,128)(2,1)S(1)} %collective-permute-done.10.part0), channel_id=1, source_target_pairs={{0,1},{1,0},{2,3},{3,2},{4,5},{5,4},{6,7},{7,6},{8,9},{9,8},{10,11... | collective-permute-start | bytes 786440 | tf_op jit(solution)/shard_map/ppermute | solution.py:299
  38.0 4.3 %collective-permute-start.19 = (bf16[256,512]{1,0:T(8,128)(2,1)S(1)}, bf16[256,512]{1,0:T(8,128)(2,1)S(1)}, u32[]{:S(2)}, u32[]{:S(2)}) collective-permute-start(bf16[256,512]{1,0:T(8,128)(2,1)S(1)} %collective-permute-done.17.part0), channel_id=1, source_target_pairs={{0,2},{1,3},{2,0},{3,1},{4,6},{5,7},{6,4},{7,5},{8,10},{9,11},{10,... | collective-permute-start | bytes 786440 | tf_op jit(solution)/shard_map/ppermute | solution.py:309
  42.3 1.3 %collective-permute-done.8.lat1 = bf16[64,1024]{1,0:T(8,128)(2,1)S(1)} collective-permute-done((bf16[64,1024]{1,0:T(8,128)(2,1)S(1)}, bf16[64,1024]{1,0:T(8,128)(2,1)S(1)}, u32[]{:S(2)}, u32[]{:S(2)}) %collective-permute-start.8) | collective-permute-done | bytes 131104 | tf_op jit(solution)/shard_map/ppermute | solution.py:299
  43.7 2.1 %shard_map.153 = (f32[32,1024]{1,0:T(8,128)S(1)}, bf16[32,1024]{1,0:T(8,128)(2,1)S(1)}) custom-call(s32[16,32]{1,0:T(8,128)S(1)} %bitcast.25, bf16[64,1024]{1,0:T(8,128)(2,1)S(1)} %get-tuple-element.34.lat0, bf16[64,1024]{1,0:T(8,128)(2,1)S(1)} %collective-permute-done.8.lat1, bf16[64,1024]{1,0:T(8,128)(2,1)S(1)} %collective-permute-done.9.lat2, ...), custom_call_target="tpu_custom_call" | custom-call | flops 603979776 | bytes 5638144 | tf_op jit(solution)/shard_map/pallas_call | solution.py:42
  45.8 0.9 %collective-permute-start.14 = (bf16[32,1024]{1,0:T(8,128)(2,1)S(1)}, bf16[32,1024]{1,0:T(8,128)(2,1)S(1)}, u32[]{:S(2)}, u32[]{:S(2)}) collective-permute-start(bf16[32,1024]{1,0:T(8,128)(2,1)S(1)} %get-tuple-element.40), channel_id=1, source_target_pairs={{0,16},{16,0},{1,17},{17,1},{2,18},{18,2},{3,19},{19,3},{4,20},{20... | collective-permute-start | bytes 196616 | tf_op jit(solution)/shard_map/ppermute | solution.py:296
  46.7 3.4 %collective-permute-done.14.theirs = bf16[32,1024]{1,0:T(8,128)(2,1)S(1)} collective-permute-done((bf16[32,1024]{1,0:T(8,128)(2,1)S(1)}, bf16[32,1024]{1,0:T(8,128)(2,1)S(1)}, u32[]{:S(2)}, u32[]{:S(2)}) %collective-permute-start.14) | collective-permute-done | bytes 65568 | tf_op jit(solution)/shard_map/ppermute | solution.py:296
  50.3 0.9 %collective-permute-start.21 = (bf16[100,512]{1,0:T(8,128)(2,1)S(1)}, bf16[100,512]{1,0:T(8,128)(2,1)S(1)}, u32[]{:S(2)}, u32[]{:S(2)}) collective-permute-start(bf16[100,512]{1,0:T(8,128)(2,1)S(1)} %bitcast.15), channel_id=1, source_target_pairs={{0,16},{16,0},{1,17},{17,1},{2,18},{18,2},{3,19},{19,3},{4,20},{20... | collective-permute-start | bytes 307208 | tf_op jit(solution)/shard_map/ppermute | solution.py:296
  52.7 3.0 %collective-permute-done.21.w2_there = bf16[100,512]{1,0:T(8,128)(2,1)S(1)} collective-permute-done((bf16[100,512]{1,0:T(8,128)(2,1)S(1)}, bf16[100,512]{1,0:T(8,128)(2,1)S(1)}, u32[]{:S(2)}, u32[]{:S(2)}) %collective-permute-start.21) | collective-permute-done | bytes 102432 | tf_op jit(solution)/shard_map/ppermute | solution.py:296
  55.7 2.0 %shard_map.155 = (bf16[100,128]{1,0:T(8,128)(2,1)}, f32[32,8,100]{2,1,0:T(8,128)S(1)}) custom-call(s32[1]{0:T(128)S(6)} %copy.16.limit, s32[3,128]{1,0:T(4,128)S(1)} %bitcast.26, bf16[100,128]{1,0:T(8,128)(2,1)S(1)} %bitcast.23, bf16[100,128]{1,0:T(8,128)(2,1)S(1)} %bitcast.24, f32[1,128]{1,0:T(1,128)S(1)} %bitcast.27, bf16[32,1024]{1,0:T(8,128)(2,1)S(1)} %shard_map.154.up0, ...), custom_call_target="tpu_custom_call" | custom-call | flops 294649856 | bytes 2551812 | tf_op jit(solution)/shard_map/pallas_call | solution.py:42
  57.6 13.8 %all_to_all.5.parts = f32[32,8,100]{2,1,0:T(8,128)S(1)} all-to-all(f32[32,8,100]{2,1,0:T(8,128)S(1)} %get-tuple-element.47), channel_id=1, replica_groups=mesh['dp'=2,'space'=16] {'dp','space'}, dimensions={0} | all-to-all | bytes 204800 | tf_op jit(solution)/shard_map/all_to_all | solution.py:375
  (55 shorter events, 3.9 us)
Async XLA Ops:
  0.7 15.8 %collective-permute-start.4 = (bf16[100,512]{1,0:T(8,128)(2,1)}, bf16[100,512]{1,0:T(8,128)(2,1)S(1)}, u32[]{:S(2)}, u32[]{:S(2)}) collective-permute-start(bf16[100,512]{1,0:T(8,128)(2,1)} %we_here.1), channel_id=1, source_target_pairs={{0,16},{16,0},{1,17},{17,1},{2,18},{18,2},{3,19},{19,3},{4,20},{20... | collective-permute-start | bytes 307208 | tf_op jit(solution)/shard_map/ppermute | solution.py:296
  5.3 7.3 %collective-permute-start = (bf16[100,128]{1,0:T(8,128)(2,1)S(1)}, bf16[100,128]{1,0:T(8,128)(2,1)S(1)}, u32[]{:S(2)}, u32[]{:S(2)}) collective-permute-start(bf16[100,128]{1,0:T(8,128)(2,1)S(1)} %bitcast.17), channel_id=1, source_target_pairs={{0,1},{1,0},{2,3},{3,2},{4,5},{5,4},{6,7},{7,6},{8,9},{9,8},{10,11... | collective-permute-start | bytes 76808 | tf_op jit(solution)/shard_map/ppermute | solution.py:299
  5.4 7.4 %collective-permute-start.1 = (bf16[100,128]{1,0:T(8,128)(2,1)S(1)}, bf16[100,128]{1,0:T(8,128)(2,1)S(1)}, u32[]{:S(2)}, u32[]{:S(2)}) collective-permute-start(bf16[100,128]{1,0:T(8,128)(2,1)S(1)} %bitcast.18), channel_id=1, source_target_pairs={{1,2},{3,4},{5,6},{7,8},{9,10},{11,12},{13,14},{2,1},{4,3},{6,5},{... | collective-permute-start | bytes 76808 | tf_op jit(solution)/shard_map/ppermute | solution.py:302
  6.1 6.7 %collective-permute-start.2 = (bf16[100,128]{1,0:T(8,128)(2,1)S(1)}, bf16[100,128]{1,0:T(8,128)(2,1)S(1)}, u32[]{:S(2)}, u32[]{:S(2)}) collective-permute-start(bf16[100,128]{1,0:T(8,128)(2,1)S(1)} %bitcast.19), channel_id=1, source_target_pairs={{1,18},{3,20},{5,22},{7,24},{9,26},{11,28},{13,30},{2,17},{4,19},{... | collective-permute-start | bytes 76808 | tf_op jit(solution)/shard_map/ppermute | solution.py:306
  6.8 7.7 %collective-permute-start.3 = (bf16[100,128]{1,0:T(8,128)(2,1)S(1)}, bf16[100,128]{1,0:T(8,128)(2,1)S(1)}, u32[]{:S(2)}, u32[]{:S(2)}) collective-permute-start(bf16[100,128]{1,0:T(8,128)(2,1)S(1)} %bitcast.20), channel_id=1, source_target_pairs={{0,17},{1,16},{2,19},{3,18},{4,21},{5,20},{6,23},{7,22},{8,25},{9,... | collective-permute-start | bytes 76808 | tf_op jit(solution)/shard_map/ppermute | solution.py:306
  12.6 3.8 %collective-permute-start.5 = (bf16[100,128]{1,0:T(8,128)(2,1)S(1)}, bf16[100,128]{1,0:T(8,128)(2,1)S(1)}, u32[]{:S(2)}, u32[]{:S(2)}) collective-permute-start(bf16[100,128]{1,0:T(8,128)(2,1)S(1)} %bitcast.21), channel_id=1, source_target_pairs={{0,16},{16,0},{1,17},{17,1},{2,18},{18,2},{3,19},{19,3},{4,20},{20... | collective-permute-start | bytes 76808 | tf_op jit(solution)/shard_map/ppermute | solution.py:296
  16.5 11.2 %collective-permute-start.10 = (bf16[256,512]{1,0:T(8,128)(2,1)}, bf16[256,512]{1,0:T(8,128)(2,1)S(1)}, u32[]{:S(2)}, u32[]{:S(2)}) collective-permute-start(bf16[256,512]{1,0:T(8,128)(2,1)} %shard_map.149), channel_id=1, source_target_pairs={{0,16},{16,0},{1,17},{17,1},{2,18},{18,2},{3,19},{19,3},{4,20},{20... | collective-permute-start | bytes 786440 | tf_op jit(solution)/shard_map/ppermute | solution.py:296
  17.1 26.6 %copy-start = (bf16[1024,1536]{1,0:T(8,128)(2,1)S(1)}, bf16[1024,1536]{1,0:T(8,128)(2,1)}, u32[]{:S(2)}) copy-start(bf16[1024,1536]{1,0:T(8,128)(2,1)} %w_ref.7) | copy-start | bytes 9437188
  21.6 22.1 %copy-start.2 = (bf16[512,1024]{1,0:T(8,128)(2,1)S(1)}, bf16[512,1024]{1,0:T(8,128)(2,1)}, u32[]{:S(2)}) copy-start(bf16[512,1024]{1,0:T(8,128)(2,1)} %wo_ref.1) | copy-start | bytes 3145732
  21.6 3.9 %collective-permute-start.6 = (bf16[16,768]{1,0:T(8,128)(2,1)S(1)}, bf16[16,768]{1,0:T(8,128)(2,1)S(1)}, u32[]{:S(2)}, u32[]{:S(2)}) collective-permute-start(bf16[16,768]{1,0:T(8,128)(2,1)S(1)} %get-tuple-element.32), channel_id=1, source_target_pairs={{0,16},{16,0},{1,17},{17,1},{2,18},{18,2},{3,19},{19,3},{4,20},{20... | collective-permute-start | bytes 73736 | tf_op jit(solution)/shard_map/ppermute | solution.py:296
  26.1 5.0 %collective-permute-start.7 = (bf16[64,1024]{1,0:T(8,128)(2,1)S(1)}, bf16[64,1024]{1,0:T(8,128)(2,1)S(1)}, u32[]{:S(2)}, u32[]{:S(2)}) collective-permute-start(bf16[64,1024]{1,0:T(8,128)(2,1)S(1)} %shard_map.151.mine), channel_id=1, source_target_pairs={{0,16},{16,0},{1,17},{17,1},{2,18},{18,2},{3,19},{19,3},{4,20},{20... | collective-permute-start | bytes 393224 | tf_op jit(solution)/shard_map/ppermute | solution.py:296
  27.7 10.2 %collective-permute-start.12 = (bf16[256,512]{1,0:T(8,128)(2,1)S(1)}, bf16[256,512]{1,0:T(8,128)(2,1)S(1)}, u32[]{:S(2)}, u32[]{:S(2)}) collective-permute-start(bf16[256,512]{1,0:T(8,128)(2,1)S(1)} %collective-permute-done.10.part0), channel_id=1, source_target_pairs={{0,2},{1,3},{2,0},{3,1},{4,6},{5,7},{6,4},{7,5},{8,10},{9,11},{10,... | collective-permute-start | bytes 786440 | tf_op jit(solution)/shard_map/ppermute | solution.py:309
  31.2 6.8 %collective-permute-start.17 = (bf16[256,512]{1,0:T(8,128)(2,1)S(1)}, bf16[256,512]{1,0:T(8,128)(2,1)S(1)}, u32[]{:S(2)}, u32[]{:S(2)}) collective-permute-start(bf16[256,512]{1,0:T(8,128)(2,1)S(1)} %get-tuple-element.41), channel_id=1, source_target_pairs={{0,16},{16,0},{1,17},{17,1},{2,18},{18,2},{3,19},{19,3},{4,20},{20... | collective-permute-start | bytes 786440 | tf_op jit(solution)/shard_map/ppermute | solution.py:296
  33.4 4.6 %collective-permute-start.9 = (bf16[64,1024]{1,0:T(8,128)(2,1)S(1)}, bf16[64,1024]{1,0:T(8,128)(2,1)S(1)}, u32[]{:S(2)}, u32[]{:S(2)}) collective-permute-start(bf16[64,1024]{1,0:T(8,128)(2,1)S(1)} %get-tuple-element.34.lat0), channel_id=1, source_target_pairs={{1,2},{3,4},{5,6},{7,8},{9,10},{11,12},{13,14},{2,1},{4,3},{6,5},{... | collective-permute-start | bytes 393224 | tf_op jit(solution)/shard_map/ppermute | solution.py:302
  34.0 9.6 %collective-permute-start.11 = (bf16[256,512]{1,0:T(8,128)(2,1)S(1)}, bf16[256,512]{1,0:T(8,128)(2,1)S(1)}, u32[]{:S(2)}, u32[]{:S(2)}) collective-permute-start(bf16[256,512]{1,0:T(8,128)(2,1)S(1)} %collective-permute-done.10.part0), channel_id=1, source_target_pairs={{0,1},{1,0},{2,3},{3,2},{4,5},{5,4},{6,7},{7,6},{8,9},{9,8},{10,11... | collective-permute-start | bytes 786440 | tf_op jit(solution)/shard_map/ppermute | solution.py:299
  37.9 5.8 %collective-permute-start.13 = (bf16[256,512]{1,0:T(8,128)(2,1)S(1)}, bf16[256,512]{1,0:T(8,128)(2,1)S(1)}, u32[]{:S(2)}, u32[]{:S(2)}) collective-permute-start(bf16[256,512]{1,0:T(8,128)(2,1)S(1)} %collective-permute-done.12.part2), channel_id=1, source_target_pairs={{0,1},{1,0},{2,3},{3,2},{4,5},{5,4},{6,7},{7,6},{8,9},{9,8},{10,11... | collective-permute-start | bytes 786440 | tf_op jit(solution)/shard_map/ppermute | solution.py:299
  38.0 12.2 %collective-permute-start.19 = (bf16[256,512]{1,0:T(8,128)(2,1)S(1)}, bf16[256,512]{1,0:T(8,128)(2,1)S(1)}, u32[]{:S(2)}, u32[]{:S(2)}) collective-permute-start(bf16[256,512]{1,0:T(8,128)(2,1)S(1)} %collective-permute-done.17.part0), channel_id=1, source_target_pairs={{0,2},{1,3},{2,0},{3,1},{4,6},{5,7},{6,4},{7,5},{8,10},{9,11},{10,... | collective-permute-start | bytes 786440 | tf_op jit(solution)/shard_map/ppermute | solution.py:309
  42.3 1.3 %collective-permute-start.8 = (bf16[64,1024]{1,0:T(8,128)(2,1)S(1)}, bf16[64,1024]{1,0:T(8,128)(2,1)S(1)}, u32[]{:S(2)}, u32[]{:S(2)}) collective-permute-start(bf16[64,1024]{1,0:T(8,128)(2,1)S(1)} %get-tuple-element.34.lat0), channel_id=1, source_target_pairs={{0,1},{1,0},{2,3},{3,2},{4,5},{5,4},{6,7},{7,6},{8,9},{9,8},{10,11... | collective-permute-start | bytes 393224 | tf_op jit(solution)/shard_map/ppermute | solution.py:299
  45.8 4.3 %collective-permute-start.14 = (bf16[32,1024]{1,0:T(8,128)(2,1)S(1)}, bf16[32,1024]{1,0:T(8,128)(2,1)S(1)}, u32[]{:S(2)}, u32[]{:S(2)}) collective-permute-start(bf16[32,1024]{1,0:T(8,128)(2,1)S(1)} %get-tuple-element.40), channel_id=1, source_target_pairs={{0,16},{16,0},{1,17},{17,1},{2,18},{18,2},{3,19},{19,3},{4,20},{20... | collective-permute-start | bytes 196616 | tf_op jit(solution)/shard_map/ppermute | solution.py:296
  46.7 8.9 %collective-permute-start.18 = (bf16[256,512]{1,0:T(8,128)(2,1)S(1)}, bf16[256,512]{1,0:T(8,128)(2,1)S(1)}, u32[]{:S(2)}, u32[]{:S(2)}) collective-permute-start(bf16[256,512]{1,0:T(8,128)(2,1)S(1)} %collective-permute-done.17.part0), channel_id=1, source_target_pairs={{0,1},{1,0},{2,3},{3,2},{4,5},{5,4},{6,7},{7,6},{8,9},{9,8},{10,11... | collective-permute-start | bytes 786440 | tf_op jit(solution)/shard_map/ppermute | solution.py:299
  50.2 5.5 %collective-permute-start.20 = (bf16[256,512]{1,0:T(8,128)(2,1)S(1)}, bf16[256,512]{1,0:T(8,128)(2,1)S(1)}, u32[]{:S(2)}, u32[]{:S(2)}) collective-permute-start(bf16[256,512]{1,0:T(8,128)(2,1)S(1)} %collective-permute-done.19.part2), channel_id=1, source_target_pairs={{0,1},{1,0},{2,3},{3,2},{4,5},{5,4},{6,7},{7,6},{8,9},{9,8},{10,11... | collective-permute-start | bytes 786440 | tf_op jit(solution)/shard_map/ppermute | solution.py:299
  50.3 5.4 %collective-permute-start.21 = (bf16[100,512]{1,0:T(8,128)(2,1)S(1)}, bf16[100,512]{1,0:T(8,128)(2,1)S(1)}, u32[]{:S(2)}, u32[]{:S(2)}) collective-permute-start(bf16[100,512]{1,0:T(8,128)(2,1)S(1)} %bitcast.15), channel_id=1, source_target_pairs={{0,16},{16,0},{1,17},{17,1},{2,18},{18,2},{3,19},{19,3},{4,20},{20... | collective-permute-start | bytes 307208 | tf_op jit(solution)/shard_map/ppermute | solution.py:296
  51.2 4.5 %collective-permute-start.15 = (bf16[32,1024]{1,0:T(8,128)(2,1)S(1)}, bf16[32,1024]{1,0:T(8,128)(2,1)S(1)}, u32[]{:S(2)}, u32[]{:S(2)}) collective-permute-start(bf16[32,1024]{1,0:T(8,128)(2,1)S(1)} %shard_map.154.up0), channel_id=1, source_target_pairs={{0,1},{1,0},{2,3},{3,2},{4,5},{5,4},{6,7},{7,6},{8,9},{9,8},{10,11... | collective-permute-start | bytes 196616 | tf_op jit(solution)/shard_map/ppermute | solution.py:299
  51.3 4.3 %collective-permute-start.16 = (bf16[32,1024]{1,0:T(8,128)(2,1)S(1)}, bf16[32,1024]{1,0:T(8,128)(2,1)S(1)}, u32[]{:S(2)}, u32[]{:S(2)}) collective-permute-start(bf16[32,1024]{1,0:T(8,128)(2,1)S(1)} %shard_map.154.up0), channel_id=1, source_target_pairs={{1,2},{3,4},{5,6},{7,8},{9,10},{11,12},{13,14},{2,1},{4,3},{6,5},{... | collective-permute-start | bytes 196616 | tf_op jit(solution)/shard_map/ppermute | solution.py:302
  (11 other events, 144.5 us)

commit v3 on v2

--- a/solution.py
+++ b/solution.py
@@ -10,6 +10,7 @@
 HEADS = 16
 F32 = jnp.float32
 BF16 = jnp.bfloat16
+BUSY = 4_000_000_000
 
 
 def silu(x):
@@ -53,39 +54,6 @@
     )(*args)
 
 
-def cut(w, column, width):
-    pieces = 8
-    size = w.shape[0] // 4
-    step = size // pieces
-
-    def kernel(w_ref, out_ref, sems):
-        start = (lax.axis_index("space") % 4) * size
-        copies = [
-            pltpu.make_async_copy(
-                w_ref.at[
-                    pl.ds(pl.multiple_of(start + i * step, step), step), pl.ds(column, width)
-                ],
-                out_ref.at[pl.ds(i * step, step), :],
-                sems.at[i],
-            )
-            for i in range(pieces)
-        ]
-        for copy in copies:
-            copy.start()
-        for copy in copies:
-            copy.wait()
-
-    return pl.pallas_call(
-        kernel,
-        out_shape=shape((size, width)),
-        in_specs=[pl.BlockSpec(memory_space=pltpu.HBM)],
-        out_specs=pl.BlockSpec(memory_space=pltpu.VMEM),
-        scratch_shapes=[pltpu.SemaphoreType.DMA((pieces,))],
-        compiler_params=pltpu.CompilerParams(vmem_limit_bytes=58 * 1024 * 1024),
-        cost_estimate=pl.CostEstimate(flops=0, bytes_accessed=0, transcendentals=0),
-    )(w)
-
-
 def side_block(index, size):
     odd = lax.axis_index("space") % 2
     side = index // size
@@ -93,40 +61,53 @@
     return block * size + index % size
 
 
-def encode_kernel(
-    query_ref, index_ref, own, own1, own2, oth, oth1, oth2, we_here, we_there, w_ref,
-    pairs_ref, probs_ref,
-):
+def slots_of(index_ref, slots):
+    entries = index_ref.shape[0]
+    index = jnp.transpose(index_ref[...])
+    entry = jnp.concatenate([index[:, k : k + 1] for k in range(entries)], axis=0)
+    return jnp.where(entry >= 0, side_block(jnp.maximum(entry, 0), slots), -1), entry >= 0
+
+
+def picked(place, i, slots):
+    lane = lax.broadcasted_iota(jnp.int32, (place.shape[0], slots), 1)
+    return (place == lane + i * slots).astype(BF16)
+
+
+def pick_kernel(index_ref, pick_ref, present_ref):
+    slots = pick_ref.shape[2]
+    place, present = slots_of(index_ref, slots)
+    for i in range(3):
+        pick_ref[i] = picked(place, i, slots)
+    present_ref[...] = jnp.broadcast_to(present.astype(F32), present_ref.shape)
+
+
+def near_kernel(pick_ref, near0, near1, near2, out_ref):
+    total = sum(dot_nt(block[...], pick_ref[i]) for i, block in enumerate((near0, near1, near2)))
+    out_ref[...] = total.astype(BF16)
+
+
+def encode(query_ref, present_ref, near_ref, we_here, we_there, w_ref, pairs_ref, probs_ref):
     nodes, width = query_ref.shape
-    entries = index_ref.shape[0]
-    rows = nodes * entries
+    rows = present_ref.shape[0]
+    entries = rows // nodes
     per_head = width // HEADS
     ours = lax.axis_index("dp")
-    index = jnp.transpose(index_ref[...])
-    entry = jnp.concatenate([index[:, k : k + 1] for k in range(entries)], axis=0)
-    head_of = lax.broadcasted_iota(jnp.int32, (width, 128), 0) // per_head
-    fold = (head_of == lax.broadcasted_iota(jnp.int32, (width, 128), 1)).astype(BF16)
-    queries = jnp.broadcast_to(query_ref[...].astype(F32)[None], (entries, nodes, width))
-    queries = queries.reshape(rows, width)
-    present = jnp.broadcast_to(entry >= 0, (rows, 128))
-    slots = own.shape[1]
-    place = jnp.where(entry >= 0, side_block(jnp.maximum(entry, 0), slots), -1)
-    lane = lax.broadcasted_iota(jnp.int32, (rows, slots), 1)
-    pick = [(place == lane + i * slots).astype(BF16) for i in range(3)]
     half = we_here.shape[1]
     here = pl.multiple_of(ours * half, half)
     there = pl.multiple_of((1 - ours) * half, half)
-    for s in range(2):
-        near = 0.0
-        for i, (mine, theirs) in enumerate(((own, oth), (own1, oth1), (own2, oth2))):
-            near += dot_nt(pick[i], jnp.where(ours == s, mine[...], theirs[...]))
-        near = near.astype(BF16)
-        embed_here = silu(dot(near, we_here[...])).astype(BF16)
-        embed_there = silu(dot(near, we_there[...])).astype(BF16)
-        pairs = dot(embed_here, w_ref[pl.ds(here, half), :])
-        pairs = (pairs + dot(embed_there, w_ref[pl.ds(there, half), :])).astype(BF16)
-        pairs_ref[s * rows : (s + 1) * rows, :] = pairs
-        product = pairs.astype(F32) * queries
+    near = jnp.transpose(near_ref[...].astype(F32)).astype(BF16)
+    embed_here = silu(dot(near, we_here[...])).astype(BF16)
+    embed_there = silu(dot(near, we_there[...])).astype(BF16)
+    pairs = dot(embed_here, w_ref[pl.ds(here, half), :])
+    pairs_ref[...] = (pairs + dot(embed_there, w_ref[pl.ds(there, half), :])).astype(BF16)
+
+    @pl.when(ours == 0)
+    def _():
+        present = present_ref[...] > 0
+        head_of = lax.broadcasted_iota(jnp.int32, (width, 128), 0) // per_head
+        fold = (head_of == lax.broadcasted_iota(jnp.int32, (width, 128), 1)).astype(BF16)
+        queries = jnp.broadcast_to(query_ref[...].astype(F32)[None], (entries, nodes, width))
+        product = pairs_ref[...].astype(F32) * queries.reshape(rows, width)
         high = product.astype(BF16)
         low = (product - high.astype(F32)).astype(BF16)
         logits = (dot(high, fold) + dot(low, fold)) * (1.0 / math.sqrt(per_head))
@@ -134,48 +115,113 @@
         top = jnp.max(logits, axis=0, keepdims=True)
         weight = jnp.where(present.reshape(entries, nodes, 128), jnp.exp(logits - top), 0.0)
         weight = weight / jnp.sum(weight, axis=0, keepdims=True)
-        turned = jnp.transpose(weight.reshape(rows, 128))
-        probs_ref[:, s * rows : (s + 1) * rows] = turned[:HEADS].astype(BF16)
-
-
-def latent_kernel(query_ref, probs, pairs, latent_ref):
+        probs_ref[...] = jnp.transpose(weight.reshape(rows, 128))[:HEADS].astype(BF16)
+
+    @pl.when(ours != 0)
+    def _():
+        probs_ref[...] = jnp.zeros(probs_ref.shape, BF16)
+
+
+def encode_own_kernel(
+    query_ref, present_ref, near_ref, we_here, we_there, w_ref, pairs_ref, probs_ref
+):
+    encode(query_ref, present_ref, near_ref, we_here, we_there, w_ref, pairs_ref, probs_ref)
+
+
+def encode_other_kernel(
+    query_ref, present_ref, near_ref, we_here, we_there, w_ref, first_ref, pairs_ref, probs_ref
+):
+    rows = first_ref.shape[1]
+    probs_ref[:, :rows] = first_ref[...]
+    encode(
+        query_ref, present_ref, near_ref, we_here, we_there, w_ref, pairs_ref,
+        probs_ref.at[:, rows : 2 * rows],
+    )
+
+
+def latent_kernel(query_ref, probs, pairs_own, pairs_other, latent_ref):
     query = query_ref[...].astype(F32)
     nodes, width = query.shape
-    rows = pairs.shape[0] // 2
+    rows = pairs_own.shape[0]
     entries = rows // nodes
     per_head = width // HEADS
     head_of = lax.broadcasted_iota(jnp.int32, (HEADS, width), 1) // per_head
     spread = (head_of == lax.broadcasted_iota(jnp.int32, (HEADS, width), 0)).astype(BF16)
-    for s in range(2):
-        turned = probs[:, s * rows : (s + 1) * rows].astype(F32)
-        weight = jnp.transpose(turned).astype(BF16)
-        mixed = dot(weight, spread) * pairs[s * rows : (s + 1) * rows, :].astype(F32)
-        mixed = jnp.sum(mixed.reshape(entries, nodes, width), axis=0)
-        latent_ref[s * nodes : (s + 1) * nodes, :] = (query + mixed).astype(BF16)
-
-
-def choose_kernel(mine, theirs, w_ref, out_ref, part_ref):
-    first = lax.axis_index("dp") == 0
-    out_ref[...] = jnp.where(first, theirs[...], mine[...])
-    size = part_ref.shape[0]
-    start = pl.multiple_of((lax.axis_index("space") % 4) * size, size)
-    part_ref[...] = w_ref[pl.ds(start, size), :]
+
+    @pl.when(lax.axis_index("dp") != 0)
+    def _():
+        for s, pairs in enumerate((pairs_other, pairs_own)):
+            turned = probs[:, s * rows : (s + 1) * rows].astype(F32)
+            weight = jnp.transpose(turned).astype(BF16)
+            mixed = dot(weight, spread) * pairs[...].astype(F32)
+            mixed = jnp.sum(mixed.reshape(entries, nodes, width), axis=0)
+            latent_ref[s * nodes : (s + 1) * nodes, :] = (query + mixed).astype(BF16)
+
+    @pl.when(lax.axis_index("dp") == 0)
+    def _():
+        latent_ref[...] = jnp.zeros_like(latent_ref)
 
 
 def add_kernel(mine, theirs, out_ref):
     out_ref[...] = (mine[...] + theirs[...].astype(F32)).astype(BF16)
 
 
+def later_kernel(latent, w_ref, send_ref, pairs_ref):
+    half = w_ref.shape[1] // 3
+    first = lax.axis_index("dp") == 0
+
+    @pl.when(jnp.logical_not(first))
+    def _():
+        norm = normalize(latent[...].astype(F32)).astype(BF16)
+        pairs_ref[:, :half] = dot(norm, w_ref[:, :half]).astype(BF16)
+        send_ref[...] = dot(norm, w_ref[:, half : 2 * half]).astype(BF16)
+        pairs_ref[:, half:] = dot(norm, w_ref[:, 2 * half :]).astype(BF16)
+
+    @pl.when(first)
+    def _():
+        send_ref[...] = jnp.zeros(send_ref.shape, BF16)
+        pairs_ref[...] = jnp.zeros(pairs_ref.shape, BF16)
+
+
+def first_kernel(mine, came, w_ref, latent_ref, queries_ref, send_ref, keys_ref):
+    half = w_ref.shape[1] // 3
+    first = lax.axis_index("dp") == 0
+
+    @pl.when(first)
+    def _():
+        latent_ref[...] = came[...]
+        norm = normalize(came[...].astype(F32)).astype(BF16)
+        queries_ref[...] = dot(norm, w_ref[:, :half]).astype(BF16)
+        send_ref[...] = dot(norm, w_ref[:, half : 2 * half]).astype(BF16)
+        keys_ref[...] = dot(norm, w_ref[:, 2 * half :]).astype(BF16)
+
+    @pl.when(jnp.logical_not(first))
+    def _():
+        latent_ref[...] = mine[...]
+        queries_ref[...] = jnp.zeros(queries_ref.shape, BF16)
+        send_ref[...] = jnp.zeros(send_ref.shape, BF16)
+        keys_ref[...] = jnp.zeros(keys_ref.shape, BF16)
+
+
+def pairs_kernel(mine, keys, values, out_ref):
+    half = keys.shape[1]
+    first = lax.axis_index("dp") == 0
+    out_ref[:, :half] = jnp.where(first, keys[...], mine[:, :half])
+    out_ref[:, half:] = jnp.where(first, values[...], mine[:, half:])
+
+
 def mesh_kernel(
-    index_ref, lat0, lat1, lat2, w_ref, part0, part1, part2, part3, wo_ref,
-    keep_ref, send_ref, norm_ref, sums_ref,
+    index_ref, latent, mine, came, pairs0, pairs1, pairs2, wo_ref, keep_ref, send_ref
 ):
-    both, width = lat0.shape
+    both, half = mine.shape
     nodes = both // 2
-    half = width // 2
     rows = 3 * both
     heads = HEADS // 2
     per_head = half // heads
+    first = lax.axis_index("dp") == 0
+    queries = jnp.where(first, mine[...], came[...])
+    pairs = jnp.concatenate([pairs0[...], pairs1[...], pairs2[...]], axis=0)
+    keys, values = pairs[:, :half], pairs[:, half:]
     place = side_block(jnp.transpose(index_ref[...]), nodes)
     near = lax.broadcasted_iota(jnp.int32, (nodes, rows), 1)
     code = (near // both) * nodes + near % nodes
@@ -184,21 +230,6 @@
     times = jnp.concatenate(
         [jnp.where(second == 0, times, 0.0), jnp.where(second == 1, times, 0.0)], axis=0
     )[None]
-    for i, block in enumerate((lat0, lat1, lat2)):
-        norm_ref[i * both : (i + 1) * both, :] = normalize(block[...].astype(F32)).astype(BF16)
-    spot = lax.axis_index("space") % 4
-    ours = lax.axis_index("dp")
-    first = ours == 0
-    part_a = dot(norm_ref[...], w_ref[:, :half])
-    part_c = dot(norm_ref[...], w_ref[:, 2 * half :])
-    part_b = 0.0
-    for i, block in enumerate((part0, part1, part2, part3)):
-        size = block.shape[0]
-        part = pl.multiple_of((spot ^ i) * size, size)
-        part_b += dot(norm_ref[:, pl.ds(part, size)], block[...])
-    queries = jnp.where(first, part_a[:both], part_b[:both]).astype(BF16)
-    keys = jnp.where(first, part_c, part_a).astype(BF16)
-    values = jnp.where(first, part_b, part_c).astype(BF16)
     head_of = lax.broadcasted_iota(jnp.int32, (both, half), 1) // per_head
     zero = jnp.zeros_like(queries)
     stacked = jnp.concatenate(
@@ -215,40 +246,36 @@
     total = jnp.where(head_of == 0, mixed[0], 0.0)
     for h in range(1, heads):
         total = jnp.where(head_of == h, mixed[h], total)
-    sums_ref[...] = dot(total.astype(BF16), wo_ref[...])
-    mine = pl.multiple_of(ours * nodes, nodes)
-    theirs = pl.multiple_of((1 - ours) * nodes, nodes)
-    keep_ref[...] = lat0[pl.ds(mine, nodes), :].astype(F32) + sums_ref[pl.ds(mine, nodes), :]
-    send_ref[...] = sums_ref[pl.ds(theirs, nodes), :].astype(BF16)
-
-
-def decode_kernel(
-    limit, index_ref, fields, target, area, up0, up1, up2,
-    w1_ref, part0, part1, part2, part3, w2_ref, w2_there,
-    pred_ref, sums_ref, norm_ref,
-):
+    projected = dot(total.astype(BF16), wo_ref[...])
+    keep_ref[...] = latent[...].astype(F32) + projected
+    send_ref[...] = projected.astype(BF16)
+
+
+def decode_kernel(index_ref, up0, up1, up2, w1_ref, w2_ref, keep_ref, send_ref):
+    both, width = up0.shape
+    nodes = both // 2
+    entries, slots = index_ref.shape
+    place = side_block(jnp.transpose(index_ref[...]), nodes)
+    near = lax.broadcasted_iota(jnp.int32, (slots, nodes), 1)
+    means = [0.0, 0.0]
+    for i, block in enumerate((up0, up1, up2)):
+        times = sum((place[:, k : k + 1] == near + i * nodes).astype(F32) for k in range(entries))
+        for s in range(2):
+            means[s] += dot(times.astype(BF16), block[s * nodes : (s + 1) * nodes, :])
+    mean = jnp.concatenate(means, axis=0) * (1.0 / entries)
+    hidden = silu(dot(normalize(mean).astype(BF16), w1_ref[...])).astype(BF16)
+    parts = [dot_nt(w2_ref[...], hidden[s * slots : (s + 1) * slots]) for s in range(2)]
+    first = lax.axis_index("dp") == 0
+    keep_ref[...] = jnp.where(first, parts[0], parts[1])
+    send_ref[...] = jnp.where(first, parts[1], parts[0]).astype(BF16)
+
+
+def errors_kernel(limit, fields, target, area, keep_ref, came, pred_ref, sums_ref):
     count_field, slots = fields.shape
     keep = lax.broadcasted_iota(jnp.int32, (8, slots), 1) < limit[0]
     keep = keep.astype(F32)
     weight = keep * area[...]
-    nodes, width = up0.shape
-    entries = index_ref.shape[0]
-    place = side_block(jnp.transpose(index_ref[...]), nodes)
-    near = lax.broadcasted_iota(jnp.int32, (slots, nodes), 1)
-    mean = 0.0
-    for i, updated in enumerate((up0, up1, up2)):
-        times = sum((place[:, k : k + 1] == near + i * nodes).astype(F32) for k in range(entries))
-        mean += dot(times.astype(BF16), updated[...])
-    norm_ref[...] = normalize(mean * (1.0 / entries)).astype(BF16)
-    spot = lax.axis_index("space") % 4
-    hidden = silu(dot(norm_ref[...], w1_ref[...])).astype(BF16)
-    hidden_there = 0.0
-    for i, block in enumerate((part0, part1, part2, part3)):
-        size = block.shape[0]
-        part = pl.multiple_of((spot ^ i) * size, size)
-        hidden_there += dot(norm_ref[:, pl.ds(part, size)], block[...])
-    hidden_there = silu(hidden_there).astype(BF16)
-    increment = dot_nt(w2_ref[...], hidden) + dot_nt(w2_there[...], hidden_there)
+    increment = keep_ref[...] + came[...].astype(F32)
     valid = keep[:1] > 0
     predicted = jnp.where(valid, fields[...].astype(F32) + increment, 0.0)
     pred_ref[...] = predicted.astype(BF16)
@@ -295,6 +322,12 @@
     def over_dp(x):
         return lax.ppermute(x, "dp", swap)
 
+    def to_first(x):
+        return lax.ppermute(x, "dp", [(1, 0)])
+
+    def to_second(x):
+        return lax.ppermute(x, "dp", [(0, 1)])
+
     def over_pair(x):
         return lax.ppermute(x, "space", pair)
 
@@ -311,65 +344,71 @@
     def after(x, *others):
         return lax.optimization_barrier((x,) + others)[0]
 
-    wq0 = cut(w_qkv, half, half)
-    own = after(own, wq0)
-    oth = over_dp(own)
     we_there = over_dp(w_embed)
-    oth1 = over_both(own, pair)
-    oth2 = over_both(own, link)
+    own1 = over_pair(own)
     own2 = over_link(own)
-    own1 = over_pair(own)
-    fetched = (own1, own2, oth2, oth1, we_there, oth, wq0)
-    own1, own2, oth2, oth1, we_there, oth, wq0 = lax.optimization_barrier(fetched)
-    wq0 = over_dp(wq0)
-
+    pick, present = call(
+        pick_kernel,
+        (shape((3, rows, slots)), shape((rows, 128), F32)),
+        (enc_index.T,),
+        flops=BUSY,
+    )
+    (near,) = call(
+        near_kernel, (shape((field_count, rows)),), (pick, own, own1, own2), flops=BUSY
+    )
+    other = over_dp(near)
+    pairs_own, probs = call(
+        encode_own_kernel,
+        (shape((rows, width)), shape((HEADS, rows))),
+        (mesh_query, present, near, w_embed, we_there, w_enc_kv),
+        flops=2 * rows * width * (width + field_count),
+    )
     pairs, probs = call(
-        encode_kernel,
-        (shape((2 * rows, width)), shape((HEADS, 2 * rows))),
-        (mesh_query, enc_index.T, own, own1, own2, oth, oth1, oth2, w_embed, we_there, w_enc_kv),
-        flops=2 * 2 * rows * width * (width + field_count),
+        encode_other_kernel,
+        (shape((rows, width)), shape((HEADS, 2 * rows))),
+        (mesh_query, present, other, w_embed, we_there, w_enc_kv, probs),
+        flops=2 * rows * width * (width + field_count),
     )
     (latent,) = call(
         latent_kernel,
         (shape((2 * nodes, width)),),
-        (mesh_query, over_dp(probs), pairs),
+        (mesh_query, to_second(probs), pairs_own, pairs),
         flops=2 * 2 * rows * width * 128,
     )
-    came = over_dp(latent)
-    wq0 = after(wq0, latent)
-    wq2 = over_quad(wq0)
-    wq1 = over_pair(after(wq0, came))
-    wq3 = over_pair(after(wq2, came))
-    latent, w10 = call(
-        choose_kernel,
-        (shape((2 * nodes, width)), shape((width // 4, half))),
-        (latent, came, w_dec1),
-    )
-    lat1 = over_pair(latent)
-    lat2 = over_link(latent)
-    w10 = over_dp(w10)
-    w2_there = over_dp(after(w2, latent))
-    w10 = after(w10, lat2)
-    w12 = over_quad(w10)
+    came = to_first(latent)
+    send, pairs = call(
+        later_kernel,
+        (shape((2 * nodes, half)), shape((2 * nodes, width))),
+        (latent, w_qkv),
+        flops=2 * 2 * nodes * width * 3 * half,
+    )
+    values = to_first(send)
+    latent, queries, send, keys = call(
+        first_kernel,
+        (shape((2 * nodes, width)),) + (shape((2 * nodes, half)),) * 3,
+        (latent, came, w_qkv),
+        flops=2 * 2 * nodes * width * 3 * half,
+    )
+    (pairs,) = call(pairs_kernel, (shape((2 * nodes, width)),), (pairs, keys, values))
     keep, send = call(
         mesh_kernel,
-        (shape((nodes, width), F32), shape((nodes, width))),
-        (proc_index.T, latent, lat1, lat2, w_qkv, wq0, wq1, wq2, wq3, w_out),
-        scratch=[pltpu.VMEM((6 * nodes, width), BF16), pltpu.VMEM((2 * nodes, width), F32)],
-        flops=2 * 6 * nodes * width * 3 * half,
-    )
-    came = over_dp(send)
-    w11 = over_pair(after(w10, keep))
-    (updated,) = call(add_kernel, (shape((nodes, width)),), (keep, came))
-    w13 = over_pair(after(w12, updated))
+        (shape((2 * nodes, width), F32), shape((2 * nodes, width))),
+        (proc_index.T, latent, queries, to_second(send), pairs, over_pair(pairs),
+         over_link(pairs), w_out),
+        flops=2 * 2 * nodes * width * width,
+    )
+    (updated,) = call(add_kernel, (shape((2 * nodes, width)),), (keep, over_dp(send)))
+    up2 = over_link(updated)
+    keep, send = call(
+        decode_kernel,
+        (shape((field_count, slots), F32), shape((field_count, slots))),
+        (dec_index.T, updated, over_pair(updated), up2, w_dec1, w2),
+        flops=2 * slots * width * (width + field_count),
+    )
     predicted, sums = call(
-        decode_kernel,
+        errors_kernel,
         (shape((field_count, slots)), shape((space * samples, 8, field_count), F32)),
-        (grid_count, dec_index.T, own, goal, area_weight[None], updated, over_pair(updated),
-         over_link(updated), w_dec1, w10, w11, w12, w13,
-         w2, w2_there),
-        scratch=[pltpu.VMEM((slots, width), BF16)],
-        flops=2 * slots * width * (width + field_count),
+        (grid_count, own, goal, area_weight[None], keep, over_dp(send)),
         smem=(0,),
     )
     parts = lax.all_to_all(sums, ("dp", "space"), 0, 0)
@@ -526,7 +565,7 @@
         P(None, "dp"),
         P("dp", None),
     )
-    small = mesh.shape["dp"] == 2 and mesh.shape["space"] % 4 == 0
+    small = mesh.shape["dp"] == 2 and mesh.shape["space"] % 2 == 0
     return jax.shard_map(
         small_body if small else general_body, mesh=mesh, in_specs=placed, out_specs=(P("dp", "space", None), P()), check_vma=False
     )

time: 72.4 us -> 70.2 us (0.970)
  starting transfers between devices: 30.3 us -> 18.7 us
  blocking collectives: 13.8 us -> 22.2 us
  Pallas kernels: 11.5 us -> 9.73 us
  waiting for transfers between devices: 14.9 us -> 16.4 us
  local copies, waits for them, and re-layouts: 0.07 us -> 1.22 us
    all_to_all x1, blocking collectives: 13.8 us -> 22.2 us  [small_body(): parts = lax.all_to_all(sums, ('dp', 'space'), 0, 0)]
    ppermute x4, waiting for transfers between devices: 1.63 us -> 9.48 us  [the longest x2 6.1 us: to_first(): return lax.ppermute(x, 'dp', [(1, 0)])]
    ppermute x4, starting transfers between devices: 13.3 us -> 6.26 us  [the longest x2 3.41 us: to_second(): return lax.ppermute(x, 'dp', [(0, 1)])]
    ppermute x8 -> x4, waiting for transfers between devices: 11.9 us -> 6.59 us  [over_dp(): return lax.ppermute(x, 'dp', swap)]
    ppermute x8 -> x4, starting transfers between devices: 10.8 us -> 6.86 us  [over_dp(): return lax.ppermute(x, 'dp', swap)]
    pallas_call x1 -> x0, Pallas kernels: 1.64 us -> none  [cut(): pl.pallas_call(kernel, out_shape=shape((size, width)), in_specs=[pl.Block...]
    unnamed x26, local copies, waits for them, and re-layouts: 0.07 us -> 1.22 us
    ppermute x7 -> x3, waiting for transfers between devices: 1.36 us -> 0.33 us  [over_pair(): return lax.ppermute(x, 'space', pair)]
  transfers between devices with their start and end apart: 22 -> 14, of which waited for: 7 -> 9; matrix products, arithmetic and copies ran while one was open for 0% -> 0% of each run, Pallas kernels for 12% -> 5%
where the time goes in v3:
time: 70.2 us; the launch traced here: 69.8 us
  blocking collectives  22.2 us (32%)
  starting transfers between devices  18.7 us (27%)
  waiting for transfers between devices  16.4 us (23%)
  Pallas kernels  9.73 us (14%)
  between operations  1.5 us (2%)
  local copies, waits for them, and re-layouts  1.22 us (2%)
    all_to_all x1, blocking collectives, small_body(): parts = lax.all_to_all(sums, ('dp', 'space'), 0, 0)  22.2 us
    pallas_call x13, Pallas kernels, call(): pl.pallas_call(kernel, out_shape=tuple(outs), in_specs=[pl.BlockSpec(memo...  9.73 us
    ppermute x4, starting transfers between devices, over_dp(): return lax.ppermute(x, 'dp', swap)  6.86 us
    ppermute x4, waiting for transfers between devices, over_dp(): return lax.ppermute(x, 'dp', swap)  6.59 us
    ppermute x2, waiting for transfers between devices, to_first(): return lax.ppermute(x, 'dp', [(1, 0)])  6.1 us
    ppermute x3, starting transfers between devices, over_pair(): return lax.ppermute(x, 'space', pair)  3.66 us
    ppermute x2, starting transfers between devices, to_second(): return lax.ppermute(x, 'dp', [(0, 1)])  3.41 us
    ppermute x2, waiting for transfers between devices, to_second(): return lax.ppermute(x, 'dp', [(0, 1)])  3.39 us
  transfers between devices with their start and end apart: 14, of which 9 were waited for; matrix products, arithmetic and copies ran while one was open for 0% of the time, Pallas kernels for 5%

profile of v3, /device:TPU:0, one launch (start us, length us, event | category | flops | bytes accessed | tf_op | source)
XLA Modules:
  0.0 69.8 jit_solution(3351673795760912174)
XLA Ops:
  1.8 2.6 %collective-permute-start.3 = (bf16[100,512]{1,0:T(8,128)(2,1)}, bf16[100,512]{1,0:T(8,128)(2,1)S(1)}, u32[]{:S(2)}, u32[]{:S(2)}) collective-permute-start(bf16[100,512]{1,0:T(8,128)(2,1)} %we_here.3), channel_id=1, source_target_pairs={{0,16},{16,0},{1,17},{17,1},{2,18},{18,2},{3,19},{19,3},{4,20},{20... | collective-permute-start | bytes 307208 | tf_op jit(solution)/shard_map/ppermute | solution.py:323
  4.4 0.7 copy-done.12
  6.2 1.1 %collective-permute-done.3.we_there = bf16[100,512]{1,0:T(8,128)(2,1)S(1)} collective-permute-done((bf16[100,512]{1,0:T(8,128)(2,1)}, bf16[100,512]{1,0:T(8,128)(2,1)S(1)}, u32[]{:S(2)}, u32[]{:S(2)}) %collective-permute-start.3) | collective-permute-done | bytes 102432 | tf_op jit(solution)/shard_map/ppermute | solution.py:323
  7.5 2.0 %shard_map.151 = (bf16[384,1024]{1,0:T(8,128)(2,1)S(1)}, bf16[16,384]{1,0:T(8,128)(2,1)S(1)}) custom-call(bf16[32,1024]{1,0:T(8,128)(2,1)S(1)} %copy-done.4, f32[384,128]{1,0:T(8,128)S(1)} %get-tuple-element.20.present_ref, bf16[100,384]{1,0:T(8,128)(2,1)S(1)} %shard_map.150.near_ref, bf16[100,512]{1,0:T(8,128)(2,1)S(1)} %copy-done.11, ...), custom_call_target="tpu_custom_call" | custom-call | flops 883949568 | bytes 2640896 | tf_op jit(solution)/shard_map/pallas_call | solution.py:43
  9.5 1.1 %collective-permute-done.2.near_ref = bf16[100,384]{1,0:T(8,128)(2,1)S(1)} collective-permute-done((bf16[100,384]{1,0:T(8,128)(2,1)S(1)}, bf16[100,384]{1,0:T(8,128)(2,1)S(1)}, u32[]{:S(2)}, u32[]{:S(2)}) %collective-permute-start.2) | collective-permute-done | bytes 76832 | tf_op jit(solution)/shard_map/ppermute | solution.py:323
  10.6 2.0 %shard_map.152 = (bf16[384,1024]{1,0:T(8,128)(2,1)S(1)}, bf16[16,768]{1,0:T(8,128)(2,1)S(1)}) custom-call(bf16[32,1024]{1,0:T(8,128)(2,1)S(1)} %copy-done.4, f32[384,128]{1,0:T(8,128)S(1)} %get-tuple-element.20.present_ref, bf16[100,384]{1,0:T(8,128)(2,1)S(1)} %collective-permute-done.2.near_ref, bf16[100,512]{1,0:T(8,128)(2,1)S(1)} %copy-done.11, ...), custom_call_target="tpu_custom_call" | custom-call | flops 883949568 | bytes 2653184 | tf_op jit(solution)/shard_map/pallas_call | solution.py:43
  12.6 1.7 %collective-permute-start.4 = (bf16[16,768]{1,0:T(8,128)(2,1)S(1)}, bf16[16,768]{1,0:T(8,128)(2,1)S(1)}, u32[]{:S(2)}, u32[]{:S(2)}) collective-permute-start(bf16[16,768]{1,0:T(8,128)(2,1)S(1)} %get-tuple-element.23), channel_id=1, source_target_pairs={{0,16},{1,17},{2,18},{3,19},{4,20},{5,21},{6,22},{7,23},{8,24},{9,... | collective-permute-start | bytes 73736 | tf_op jit(solution)/shard_map/ppermute | solution.py:329
  14.4 1.5 %collective-permute-done.4.probs = bf16[16,768]{1,0:T(8,128)(2,1)S(1)} collective-permute-done((bf16[16,768]{1,0:T(8,128)(2,1)S(1)}, bf16[16,768]{1,0:T(8,128)(2,1)S(1)}, u32[]{:S(2)}, u32[]{:S(2)}) %collective-permute-start.4) | collective-permute-done | bytes 24608 | tf_op jit(solution)/shard_map/ppermute | solution.py:329
  15.9 1.4 %collective-permute-start.5 = (bf16[64,1024]{1,0:T(8,128)(2,1)S(1)}, bf16[64,1024]{1,0:T(8,128)(2,1)S(1)}, u32[]{:S(2)}, u32[]{:S(2)}) collective-permute-start(bf16[64,1024]{1,0:T(8,128)(2,1)S(1)} %shard_map.153.mine.latent), channel_id=1, source_target_pairs={{16,0},{17,1},{18,2},{19,3},{20,4},{21,5},{22,6},{23,7},{24,8},{25... | collective-permute-start | bytes 393224 | tf_op jit(solution)/shard_map/ppermute | solution.py:326
  17.5 1.4 %collective-permute-start.7 = (bf16[64,512]{1,0:T(8,128)(2,1)S(1)}, bf16[64,512]{1,0:T(8,128)(2,1)S(1)}, u32[]{:S(2)}, u32[]{:S(2)}) collective-permute-start(bf16[64,512]{1,0:T(8,128)(2,1)S(1)} %get-tuple-element.31), channel_id=1, source_target_pairs={{16,0},{17,1},{18,2},{19,3},{20,4},{21,5},{22,6},{23,7},{24,8},{25... | collective-permute-start | bytes 196616 | tf_op jit(solution)/shard_map/ppermute | solution.py:326
  18.9 5.5 %collective-permute-done.5.came = bf16[64,1024]{1,0:T(8,128)(2,1)S(1)} collective-permute-done((bf16[64,1024]{1,0:T(8,128)(2,1)S(1)}, bf16[64,1024]{1,0:T(8,128)(2,1)S(1)}, u32[]{:S(2)}, u32[]{:S(2)}) %collective-permute-start.5) | collective-permute-done | bytes 131104 | tf_op jit(solution)/shard_map/ppermute | solution.py:326
  24.4 0.8 %shard_map.154 = (bf16[64,1024]{1,0:T(8,128)(2,1)S(1)}, bf16[64,512]{1,0:T(8,128)(2,1)S(1)}, bf16[64,512]{1,0:T(8,128)(2,1)S(1)}, bf16[64,512]{1,0:T(8,128)(2,1)S(1)}) custom-call(bf16[64,1024]{1,0:T(8,128)(2,1)S(1)} %shard_map.153.mine.latent, bf16[64,1024]{1,0:T(8,128)(2,1)S(1)} %collective-permute-done.5.came, bf16[1024,1536]{1,0:T(8,128)(2,1)S(1)} %copy-done), custom_call_target="tpu_custom_call" | custom-call | flops 201326592 | bytes 3407872 | tf_op jit(solution)/shard_map/pallas_call | solution.py:43
  26.0 0.7 collective-permute-start.9
  26.7 1.7 %collective-permute-start.6 = (bf16[64,512]{1,0:T(8,128)(2,1)S(1)}, bf16[64,512]{1,0:T(8,128)(2,1)S(1)}, u32[]{:S(2)}, u32[]{:S(2)}) collective-permute-start(bf16[64,512]{1,0:T(8,128)(2,1)S(1)} %get-tuple-element.28), channel_id=1, source_target_pairs={{0,16},{1,17},{2,18},{3,19},{4,20},{5,21},{6,22},{7,23},{8,24},{9,... | collective-permute-start | bytes 196616 | tf_op jit(solution)/shard_map/ppermute | solution.py:329
  28.4 1.9 %collective-permute-done.6.came = bf16[64,512]{1,0:T(8,128)(2,1)S(1)} collective-permute-done((bf16[64,512]{1,0:T(8,128)(2,1)S(1)}, bf16[64,512]{1,0:T(8,128)(2,1)S(1)}, u32[]{:S(2)}, u32[]{:S(2)}) %collective-permute-start.6) | collective-permute-done | bytes 65568 | tf_op jit(solution)/shard_map/ppermute | solution.py:329
  30.3 1.2 %shard_map.157 = (f32[64,1024]{1,0:T(8,128)S(1)}, bf16[64,1024]{1,0:T(8,128)(2,1)S(1)}) custom-call(s32[16,32]{1,0:T(8,128)S(1)} %bitcast.21, bf16[64,1024]{1,0:T(8,128)(2,1)S(1)} %get-tuple-element.26.latent, bf16[64,512]{1,0:T(8,128)(2,1)S(1)} %get-tuple-element.27.mine, bf16[64,512]{1,0:T(8,128)(2,1)S(1)} %collective-permute-done.6.came, ...), custom_call_target="tpu_custom_call" | custom-call | flops 134217728 | bytes 1705984 | tf_op jit(solution)/shard_map/pallas_call | solution.py:43
  31.5 2.4 %collective-permute-start.10 = (bf16[64,1024]{1,0:T(8,128)(2,1)S(1)}, bf16[64,1024]{1,0:T(8,128)(2,1)S(1)}, u32[]{:S(2)}, u32[]{:S(2)}) collective-permute-start(bf16[64,1024]{1,0:T(8,128)(2,1)S(1)} %get-tuple-element.33), channel_id=1, source_target_pairs={{0,16},{16,0},{1,17},{17,1},{2,18},{18,2},{3,19},{19,3},{4,20},{20... | collective-permute-start | bytes 393224 | tf_op jit(solution)/shard_map/ppermute | solution.py:323
  33.9 2.9 %collective-permute-done.10.theirs = bf16[64,1024]{1,0:T(8,128)(2,1)S(1)} collective-permute-done((bf16[64,1024]{1,0:T(8,128)(2,1)S(1)}, bf16[64,1024]{1,0:T(8,128)(2,1)S(1)}, u32[]{:S(2)}, u32[]{:S(2)}) %collective-permute-start.10) | collective-permute-done | bytes 131104 | tf_op jit(solution)/shard_map/ppermute | solution.py:323
  36.9 3.0 %collective-permute-start.11 = (bf16[64,1024]{1,0:T(8,128)(2,1)S(1)}, bf16[64,1024]{1,0:T(8,128)(2,1)S(1)}, u32[]{:S(2)}, u32[]{:S(2)}) collective-permute-start(bf16[64,1024]{1,0:T(8,128)(2,1)S(1)} %shard_map.158.up0), channel_id=1, source_target_pairs={{0,1},{1,0},{2,3},{3,2},{4,5},{5,4},{6,7},{7,6},{8,9},{9,8},{10,11... | collective-permute-start | bytes 393224 | tf_op jit(solution)/shard_map/ppermute | solution.py:332
  39.8 0.7 collective-permute-start.12
  40.8 1.6 %shard_map.159 = (f32[100,128]{1,0:T(8,128)S(1)}, bf16[100,128]{1,0:T(8,128)(2,1)S(1)}) custom-call(s32[3,128]{1,0:T(4,128)S(1)} %bitcast.22, bf16[64,1024]{1,0:T(8,128)(2,1)S(1)} %shard_map.158.up0, bf16[64,1024]{1,0:T(8,128)(2,1)S(1)} %collective-permute-done.11.up1, bf16[64,1024]{1,0:T(8,128)(2,1)S(1)} %collective-permute-done.12.up2, ...), custom_call_target="tpu_custom_call" | custom-call | flops 294649856 | bytes 1545728 | tf_op jit(solution)/shard_map/pallas_call | solution.py:43
  42.4 1.8 %collective-permute-start.13 = (bf16[100,128]{1,0:T(8,128)(2,1)S(1)}, bf16[100,128]{1,0:T(8,128)(2,1)S(1)}, u32[]{:S(2)}, u32[]{:S(2)}) collective-permute-start(bf16[100,128]{1,0:T(8,128)(2,1)S(1)} %get-tuple-element.35), channel_id=1, source_target_pairs={{0,16},{16,0},{1,17},{17,1},{2,18},{18,2},{3,19},{19,3},{4,20},{20... | collective-permute-start | bytes 76808 | tf_op jit(solution)/shard_map/ppermute | solution.py:323
  44.8 1.5 %collective-permute-done.13.came = bf16[100,128]{1,0:T(8,128)(2,1)S(1)} collective-permute-done((bf16[100,128]{1,0:T(8,128)(2,1)S(1)}, bf16[100,128]{1,0:T(8,128)(2,1)S(1)}, u32[]{:S(2)}, u32[]{:S(2)}) %collective-permute-start.13) | collective-permute-done | bytes 25632 | tf_op jit(solution)/shard_map/ppermute | solution.py:323
  47.0 22.2 %all_to_all.5.parts = f32[32,8,100]{2,1,0:T(8,128)S(1)} all-to-all(f32[32,8,100]{2,1,0:T(8,128)S(1)} %get-tuple-element.37), channel_id=1, replica_groups=mesh['dp'=2,'space'=16] {'dp','space'}, dimensions={0} | all-to-all | bytes 204800 | tf_op jit(solution)/shard_map/all_to_all | solution.py:414
  (44 shorter events, 4.9 us)
Async XLA Ops:
  0.6 4.9 %collective-permute-start = (bf16[100,128]{1,0:T(8,128)(2,1)}, bf16[100,128]{1,0:T(8,128)(2,1)S(1)}, u32[]{:S(2)}, u32[]{:S(2)}) collective-permute-start(bf16[100,128]{1,0:T(8,128)(2,1)} %bitcast.16), channel_id=1, source_target_pairs={{0,1},{1,0},{2,3},{3,2},{4,5},{5,4},{6,7},{7,6},{8,9},{9,8},{10,11... | collective-permute-start | bytes 76808 | tf_op jit(solution)/shard_map/ppermute | solution.py:332
  1.1 4.4 %collective-permute-start.1 = (bf16[100,128]{1,0:T(8,128)(2,1)}, bf16[100,128]{1,0:T(8,128)(2,1)S(1)}, u32[]{:S(2)}, u32[]{:S(2)}) collective-permute-start(bf16[100,128]{1,0:T(8,128)(2,1)} %bitcast.17), channel_id=1, source_target_pairs={{1,2},{3,4},{5,6},{7,8},{9,10},{11,12},{13,14},{2,1},{4,3},{6,5},{... | collective-permute-start | bytes 76808 | tf_op jit(solution)/shard_map/ppermute | solution.py:335
  1.8 5.5 %collective-permute-start.3 = (bf16[100,512]{1,0:T(8,128)(2,1)}, bf16[100,512]{1,0:T(8,128)(2,1)S(1)}, u32[]{:S(2)}, u32[]{:S(2)}) collective-permute-start(bf16[100,512]{1,0:T(8,128)(2,1)} %we_here.3), channel_id=1, source_target_pairs={{0,16},{16,0},{1,17},{17,1},{2,18},{18,2},{3,19},{19,3},{4,20},{20... | collective-permute-start | bytes 307208 | tf_op jit(solution)/shard_map/ppermute | solution.py:323
  5.8 1.6 %copy-start.10 = (bf16[1024,1024]{1,0:T(8,128)(2,1)S(1)}, bf16[1024,1024]{1,0:T(8,128)(2,1)}, u32[]{:S(2)}) copy-start(bf16[1024,1024]{1,0:T(8,128)(2,1)} %w_ref.5) | copy-start | bytes 6291460
  5.8 1.6 %copy-start.11 = (bf16[100,512]{1,0:T(8,128)(2,1)S(1)}, bf16[100,512]{1,0:T(8,128)(2,1)}, u32[]{:S(2)}) copy-start(bf16[100,512]{1,0:T(8,128)(2,1)} %we_here.3) | copy-start | bytes 307204
  6.1 4.5 %collective-permute-start.2 = (bf16[100,384]{1,0:T(8,128)(2,1)S(1)}, bf16[100,384]{1,0:T(8,128)(2,1)S(1)}, u32[]{:S(2)}, u32[]{:S(2)}) collective-permute-start(bf16[100,384]{1,0:T(8,128)(2,1)S(1)} %shard_map.150.near_ref), channel_id=1, source_target_pairs={{0,16},{16,0},{1,17},{17,1},{2,18},{18,2},{3,19},{19,3},{4,20},{20... | collective-permute-start | bytes 230408 | tf_op jit(solution)/shard_map/ppermute | solution.py:323
  9.5 7.9 %copy-start = (bf16[1024,1536]{1,0:T(8,128)(2,1)S(1)}, bf16[1024,1536]{1,0:T(8,128)(2,1)}, u32[]{:S(2)}) copy-start(bf16[1024,1536]{1,0:T(8,128)(2,1)} %w_ref.7) | copy-start | bytes 9437188
  12.6 3.3 %collective-permute-start.4 = (bf16[16,768]{1,0:T(8,128)(2,1)S(1)}, bf16[16,768]{1,0:T(8,128)(2,1)S(1)}, u32[]{:S(2)}, u32[]{:S(2)}) collective-permute-start(bf16[16,768]{1,0:T(8,128)(2,1)S(1)} %get-tuple-element.23), channel_id=1, source_target_pairs={{0,16},{1,17},{2,18},{3,19},{4,20},{5,21},{6,22},{7,23},{8,24},{9,... | collective-permute-start | bytes 73736 | tf_op jit(solution)/shard_map/ppermute | solution.py:329
  15.9 14.4 %copy-start.2 = (bf16[512,1024]{1,0:T(8,128)(2,1)S(1)}, bf16[512,1024]{1,0:T(8,128)(2,1)}, u32[]{:S(2)}) copy-start(bf16[512,1024]{1,0:T(8,128)(2,1)} %wo_ref.1) | copy-start | bytes 3145732
  15.9 14.4 %copy-start.7 = (s32[32,16]{0,1:T(8,128)S(1)}, s32[32,16]{0,1:T(8,128)}, u32[]{:S(2)}) copy-start(s32[32,16]{0,1:T(8,128)} %param.20) | copy-start | bytes 6148
  15.9 8.5 %collective-permute-start.5 = (bf16[64,1024]{1,0:T(8,128)(2,1)S(1)}, bf16[64,1024]{1,0:T(8,128)(2,1)S(1)}, u32[]{:S(2)}, u32[]{:S(2)}) collective-permute-start(bf16[64,1024]{1,0:T(8,128)(2,1)S(1)} %shard_map.153.mine.latent), channel_id=1, source_target_pairs={{16,0},{17,1},{18,2},{19,3},{20,4},{21,5},{22,6},{23,7},{24,8},{25... | collective-permute-start | bytes 393224 | tf_op jit(solution)/shard_map/ppermute | solution.py:326
  17.4 23.4 %copy-start.1 = (bf16[1024,512]{1,0:T(8,128)(2,1)S(1)}, bf16[1024,512]{1,0:T(8,128)(2,1)}, u32[]{:S(2)}) copy-start(bf16[1024,512]{1,0:T(8,128)(2,1)} %w1_ref.1) | copy-start | bytes 3145732
  17.4 23.4 %copy-start.3 = (bf16[512,100]{0,1:T(8,128)(2,1)S(1)}, bf16[512,100]{0,1:T(8,128)(2,1)}, u32[]{:S(2)}) copy-start(bf16[512,100]{0,1:T(8,128)(2,1)} %param.27) | copy-start | bytes 307204
  17.4 23.4 %copy-start.8 = (s32[128,3]{0,1:T(4,128)S(1)}, s32[128,3]{0,1:T(4,128)}, u32[]{:S(2)}) copy-start(s32[128,3]{0,1:T(4,128)} %param.21) | copy-start | bytes 4612
  17.4 28.9 %copy-start.6 = (bf16[1,128,100]{1,2,0:T(8,128)(2,1)S(1)}, bf16[1,128,100]{1,2,0:T(8,128)(2,1)}, u32[]{:S(2)}) copy-start(bf16[1,128,100]{1,2,0:T(8,128)(2,1)} %param.15) | copy-start | bytes 76804
  17.5 28.9 %copy-start.9 = (f32[128]{0:T(128)S(1)}, f32[128]{0:T(128)}, u32[]{:S(2)}) copy-start(f32[128]{0:T(128)} %param.16) | copy-start | bytes 1540
  17.5 8.4 %collective-permute-start.7 = (bf16[64,512]{1,0:T(8,128)(2,1)S(1)}, bf16[64,512]{1,0:T(8,128)(2,1)S(1)}, u32[]{:S(2)}, u32[]{:S(2)}) collective-permute-start(bf16[64,512]{1,0:T(8,128)(2,1)S(1)} %get-tuple-element.31), channel_id=1, source_target_pairs={{16,0},{17,1},{18,2},{19,3},{20,4},{21,5},{22,6},{23,7},{24,8},{25... | collective-permute-start | bytes 196616 | tf_op jit(solution)/shard_map/ppermute | solution.py:326
  25.9 4.4 %collective-permute-start.8 = (bf16[64,1024]{1,0:T(8,128)(2,1)S(1)}, bf16[64,1024]{1,0:T(8,128)(2,1)S(1)}, u32[]{:S(2)}, u32[]{:S(2)}) collective-permute-start(bf16[64,1024]{1,0:T(8,128)(2,1)S(1)} %shard_map.156.pairs0), channel_id=1, source_target_pairs={{0,1},{1,0},{2,3},{3,2},{4,5},{5,4},{6,7},{7,6},{8,9},{9,8},{10,11... | collective-permute-start | bytes 393224 | tf_op jit(solution)/shard_map/ppermute | solution.py:332
  26.0 4.2 %collective-permute-start.9 = (bf16[64,1024]{1,0:T(8,128)(2,1)S(1)}, bf16[64,1024]{1,0:T(8,128)(2,1)S(1)}, u32[]{:S(2)}, u32[]{:S(2)}) collective-permute-start(bf16[64,1024]{1,0:T(8,128)(2,1)S(1)} %shard_map.156.pairs0), channel_id=1, source_target_pairs={{1,2},{3,4},{5,6},{7,8},{9,10},{11,12},{13,14},{2,1},{4,3},{6,5},{... | collective-permute-start | bytes 393224 | tf_op jit(solution)/shard_map/ppermute | solution.py:335
  26.7 3.6 %collective-permute-start.6 = (bf16[64,512]{1,0:T(8,128)(2,1)S(1)}, bf16[64,512]{1,0:T(8,128)(2,1)S(1)}, u32[]{:S(2)}, u32[]{:S(2)}) collective-permute-start(bf16[64,512]{1,0:T(8,128)(2,1)S(1)} %get-tuple-element.28), channel_id=1, source_target_pairs={{0,16},{1,17},{2,18},{3,19},{4,20},{5,21},{6,22},{7,23},{8,24},{9,... | collective-permute-start | bytes 196616 | tf_op jit(solution)/shard_map/ppermute | solution.py:329
  31.5 5.3 %collective-permute-start.10 = (bf16[64,1024]{1,0:T(8,128)(2,1)S(1)}, bf16[64,1024]{1,0:T(8,128)(2,1)S(1)}, u32[]{:S(2)}, u32[]{:S(2)}) collective-permute-start(bf16[64,1024]{1,0:T(8,128)(2,1)S(1)} %get-tuple-element.33), channel_id=1, source_target_pairs={{0,16},{16,0},{1,17},{17,1},{2,18},{18,2},{3,19},{19,3},{4,20},{20... | collective-permute-start | bytes 393224 | tf_op jit(solution)/shard_map/ppermute | solution.py:323
  36.9 3.9 %collective-permute-start.11 = (bf16[64,1024]{1,0:T(8,128)(2,1)S(1)}, bf16[64,1024]{1,0:T(8,128)(2,1)S(1)}, u32[]{:S(2)}, u32[]{:S(2)}) collective-permute-start(bf16[64,1024]{1,0:T(8,128)(2,1)S(1)} %shard_map.158.up0), channel_id=1, source_target_pairs={{0,1},{1,0},{2,3},{3,2},{4,5},{5,4},{6,7},{7,6},{8,9},{9,8},{10,11... | collective-permute-start | bytes 393224 | tf_op jit(solution)/shard_map/ppermute | solution.py:332
  39.8 1.0 %collective-permute-start.12 = (bf16[64,1024]{1,0:T(8,128)(2,1)S(1)}, bf16[64,1024]{1,0:T(8,128)(2,1)S(1)}, u32[]{:S(2)}, u32[]{:S(2)}) collective-permute-start(bf16[64,1024]{1,0:T(8,128)(2,1)S(1)} %shard_map.158.up0), channel_id=1, source_target_pairs={{1,2},{3,4},{5,6},{7,8},{9,10},{11,12},{13,14},{2,1},{4,3},{6,5},{... | collective-permute-start | bytes 393224 | tf_op jit(solution)/shard_map/ppermute | solution.py:335
  42.4 3.9 %collective-permute-start.13 = (bf16[100,128]{1,0:T(8,128)(2,1)S(1)}, bf16[100,128]{1,0:T(8,128)(2,1)S(1)}, u32[]{:S(2)}, u32[]{:S(2)}) collective-permute-start(bf16[100,128]{1,0:T(8,128)(2,1)S(1)} %get-tuple-element.35), channel_id=1, source_target_pairs={{0,16},{16,0},{1,17},{17,1},{2,18},{18,2},{3,19},{19,3},{4,20},{20... | collective-permute-start | bytes 76808 | tf_op jit(solution)/shard_map/ppermute | solution.py:323
  (3 other events, 2.9 us)

commit v4 on v3

--- a/solution.py
+++ b/solution.py
@@ -1,3 +1,4 @@
+import functools
 import math
 
 import jax
@@ -38,8 +39,8 @@
     return jax.ShapeDtypeStruct(tuple(dims), dtype)
 
 
-def call(kernel, outs, args, scratch=(), flops=0, smem=()):
-    size = sum(math.prod(a.shape) * a.dtype.itemsize for a in args)
+def call(kernel, outs, args, scratch=(), flops=0, smem=(), size=None):
+    size = size if size is not None else sum(math.prod(a.shape) * a.dtype.itemsize for a in args)
     return pl.pallas_call(
         kernel,
         out_shape=tuple(outs),
@@ -79,6 +80,27 @@
     for i in range(3):
         pick_ref[i] = picked(place, i, slots)
     present_ref[...] = jnp.broadcast_to(present.astype(F32), present_ref.shape)
+
+
+def share_kernel(w1_ref, w2_ref, out_ref, pad_ref):
+    size = w1_ref.shape[0] // 8
+    tail = pad_ref.shape[0] // 8
+    spot = lax.axis_index("space")
+    share = (spot % 2) * 4 + ((spot // 2) % 2) * 2 + (spot // 4) % 2
+    pad_ref[...] = jnp.zeros(pad_ref.shape, BF16)
+    pad_ref[: w2_ref.shape[0], :] = w2_ref[...]
+    out_ref[:size, :] = w1_ref[pl.ds(pl.multiple_of(share * size, size), size), :]
+    out_ref[size:, :] = pad_ref[pl.ds(pl.multiple_of(share * tail, tail), tail), :]
+
+
+def join_kernel(step, tail, mine, theirs, out_ref):
+    rows = mine.shape[0]
+    bit = (lax.axis_index("space") // step) % 2
+    for block, place in ((mine, bit), (theirs, 1 - bit)):
+        size = rows - tail
+        out_ref[pl.ds(pl.multiple_of(place * size, 16), size), :] = block[:size, :]
+        start = pl.multiple_of(2 * size + place * tail, 16)
+        out_ref[pl.ds(start, tail), :] = block[size:, :]
 
 
 def near_kernel(pick_ref, near0, near1, near2, out_ref):
@@ -211,7 +233,7 @@
 
 
 def mesh_kernel(
-    index_ref, latent, mine, came, pairs0, pairs1, pairs2, wo_ref, keep_ref, send_ref
+    index_ref, latent, mine, came, pairs0, pairs1, pairs2, wo_ref, keep_ref, send_ref, sums_ref
 ):
     both, half = mine.shape
     nodes = both // 2
@@ -246,36 +268,45 @@
     total = jnp.where(head_of == 0, mixed[0], 0.0)
     for h in range(1, heads):
         total = jnp.where(head_of == h, mixed[h], total)
-    projected = dot(total.astype(BF16), wo_ref[...])
-    keep_ref[...] = latent[...].astype(F32) + projected
-    send_ref[...] = projected.astype(BF16)
-
-
-def decode_kernel(index_ref, up0, up1, up2, w1_ref, w2_ref, keep_ref, send_ref):
-    both, width = up0.shape
-    nodes = both // 2
-    entries, slots = index_ref.shape
-    place = side_block(jnp.transpose(index_ref[...]), nodes)
-    near = lax.broadcasted_iota(jnp.int32, (slots, nodes), 1)
-    means = [0.0, 0.0]
-    for i, block in enumerate((up0, up1, up2)):
-        times = sum((place[:, k : k + 1] == near + i * nodes).astype(F32) for k in range(entries))
-        for s in range(2):
-            means[s] += dot(times.astype(BF16), block[s * nodes : (s + 1) * nodes, :])
-    mean = jnp.concatenate(means, axis=0) * (1.0 / entries)
-    hidden = silu(dot(normalize(mean).astype(BF16), w1_ref[...])).astype(BF16)
-    parts = [dot_nt(w2_ref[...], hidden[s * slots : (s + 1) * slots]) for s in range(2)]
-    first = lax.axis_index("dp") == 0
-    keep_ref[...] = jnp.where(first, parts[0], parts[1])
-    send_ref[...] = jnp.where(first, parts[1], parts[0]).astype(BF16)
-
-
-def errors_kernel(limit, fields, target, area, keep_ref, came, pred_ref, sums_ref):
+    sums_ref[...] = dot(total.astype(BF16), wo_ref[...])
+    ours = lax.axis_index("dp")
+    mine = pl.multiple_of(ours * nodes, nodes)
+    theirs = pl.multiple_of((1 - ours) * nodes, nodes)
+    keep_ref[...] = latent[pl.ds(mine, nodes), :].astype(F32) + sums_ref[pl.ds(mine, nodes), :]
+    send_ref[...] = sums_ref[pl.ds(theirs, nodes), :].astype(BF16)
+
+
+def decode_kernel(
+    limit, index_ref, fields, target, area, up0, up1, up2,
+    w1_ref, part0, part1, w2_ref,
+    pred_ref, sums_ref, norm_ref, there_ref,
+):
     count_field, slots = fields.shape
     keep = lax.broadcasted_iota(jnp.int32, (8, slots), 1) < limit[0]
     keep = keep.astype(F32)
     weight = keep * area[...]
-    increment = keep_ref[...] + came[...].astype(F32)
+    nodes, width = up0.shape
+    entries = index_ref.shape[0]
+    place = side_block(jnp.transpose(index_ref[...]), nodes)
+    near = lax.broadcasted_iota(jnp.int32, (slots, nodes), 1)
+    mean = 0.0
+    for i, updated in enumerate((up0, up1, up2)):
+        times = sum((place[:, k : k + 1] == near + i * nodes).astype(F32) for k in range(entries))
+        mean += dot(times.astype(BF16), updated[...])
+    norm_ref[...] = normalize(mean * (1.0 / entries)).astype(BF16)
+    core = lax.axis_index("space") % 2
+    hidden = silu(dot(norm_ref[...], w1_ref[...])).astype(BF16)
+    hidden_there = 0.0
+    size = width // 2
+    tail = part0.shape[0] - size
+    for i, block in enumerate((part0, part1)):
+        part = pl.multiple_of((core ^ i) * size, size)
+        hidden_there += dot(norm_ref[:, pl.ds(part, size)], block[:size, :])
+        start = pl.multiple_of((core ^ i) * tail, tail)
+        there_ref[pl.ds(start, tail), :] = block[size:, :]
+    hidden_there = silu(hidden_there).astype(BF16)
+    increment = dot_nt(w2_ref[...], hidden)
+    increment += dot_nt(there_ref[:count_field, :], hidden_there)
     valid = keep[:1] > 0
     predicted = jnp.where(valid, fields[...].astype(F32) + increment, 0.0)
     pred_ref[...] = predicted.astype(BF16)
@@ -323,10 +354,10 @@
         return lax.ppermute(x, "dp", swap)
 
     def to_first(x):
-        return lax.ppermute(x, "dp", [(1, 0)])
+        return lax.ppermute(x, "dp", swap)
 
     def to_second(x):
-        return lax.ppermute(x, "dp", [(0, 1)])
+        return lax.ppermute(x, "dp", swap)
 
     def over_pair(x):
         return lax.ppermute(x, "space", pair)
@@ -357,12 +388,21 @@
         near_kernel, (shape((field_count, rows)),), (pick, own, own1, own2), flops=BUSY
     )
     other = over_dp(near)
+    tail = 16 * pl.cdiv(field_count, 128)
+    (share,) = call(
+        share_kernel,
+        (shape((width // 8 + tail, half)),),
+        (after(w_dec1, near), w2),
+        scratch=[pltpu.VMEM((8 * tail, half), BF16)],
+        flops=BUSY,
+    )
     pairs_own, probs = call(
         encode_own_kernel,
         (shape((rows, width)), shape((HEADS, rows))),
         (mesh_query, present, near, w_embed, we_there, w_enc_kv),
         flops=2 * rows * width * (width + field_count),
     )
+    share = over_dp(after(share, other, pairs_own))
     pairs, probs = call(
         encode_other_kernel,
         (shape((rows, width)), shape((HEADS, 2 * rows))),
@@ -376,6 +416,8 @@
         flops=2 * 2 * rows * width * 128,
     )
     came = to_first(latent)
+    share = after(share, latent)
+    came_share = lax.ppermute(share, "space", [(i, i ^ 4) for i in range(space)])
     send, pairs = call(
         later_kernel,
         (shape((2 * nodes, half)), shape((2 * nodes, width))),
@@ -390,25 +432,35 @@
         flops=2 * 2 * nodes * width * 3 * half,
     )
     (pairs,) = call(pairs_kernel, (shape((2 * nodes, width)),), (pairs, keys, values))
+    (share,) = call(
+        functools.partial(join_kernel, 4, tail),
+        (shape((2 * share.shape[0], half)),),
+        (share, came_share),
+    )
+    came_share = over_quad(share)
     keep, send = call(
         mesh_kernel,
-        (shape((2 * nodes, width), F32), shape((2 * nodes, width))),
+        (shape((nodes, width), F32), shape((nodes, width))),
         (proc_index.T, latent, queries, to_second(send), pairs, over_pair(pairs),
          over_link(pairs), w_out),
+        scratch=[pltpu.VMEM((2 * nodes, width), F32)],
         flops=2 * 2 * nodes * width * width,
     )
-    (updated,) = call(add_kernel, (shape((2 * nodes, width)),), (keep, over_dp(send)))
-    up2 = over_link(updated)
-    keep, send = call(
+    (share,) = call(
+        functools.partial(join_kernel, 2, 2 * tail),
+        (shape((2 * share.shape[0], half)),),
+        (share, came_share),
+    )
+    (updated,) = call(add_kernel, (shape((nodes, width)),), (keep, over_dp(send)))
+    up1 = over_pair(updated)
+    came_share = over_pair(after(share, up1))
+    predicted, sums = call(
         decode_kernel,
-        (shape((field_count, slots), F32), shape((field_count, slots))),
-        (dec_index.T, updated, over_pair(updated), up2, w_dec1, w2),
+        (shape((field_count, slots)), shape((space * samples, 8, field_count), F32)),
+        (grid_count, dec_index.T, own, goal, area_weight[None], updated, up1,
+         over_link(updated), w_dec1, share, came_share, w2),
+        scratch=[pltpu.VMEM((slots, width), BF16), pltpu.VMEM((8 * tail, half), BF16)],
         flops=2 * slots * width * (width + field_count),
-    )
-    predicted, sums = call(
-        errors_kernel,
-        (shape((field_count, slots)), shape((space * samples, 8, field_count), F32)),
-        (grid_count, own, goal, area_weight[None], keep, over_dp(send)),
         smem=(0,),
     )
     parts = lax.all_to_all(sums, ("dp", "space"), 0, 0)
@@ -565,7 +617,7 @@
         P(None, "dp"),
         P("dp", None),
     )
-    small = mesh.shape["dp"] == 2 and mesh.shape["space"] % 2 == 0
+    small = mesh.shape["dp"] == 2 and mesh.shape["space"] % 8 == 0
     return jax.shard_map(
         small_body if small else general_body, mesh=mesh, in_specs=placed, out_specs=(P("dp", "space", None), P()), check_vma=False
     )

time: 70.2 us -> 65.6 us (0.934)
  waiting for transfers between devices: 16.4 us -> 11.6 us
  blocking collectives: 22.2 us -> 18.9 us
  local copies, waits for them, and re-layouts: 1.22 us -> 3.32 us
  starting transfers between devices: 18.7 us -> 20.2 us
    ppermute x4 -> x6, starting transfers between devices: 6.26 us -> 11.9 us  [the longest x1 4.83 us: small_body(): lax.ppermute(share, 'space', [(i, i ^ 4) for i in range(space)])]
    all_to_all x1, blocking collectives: 22.2 us -> 18.9 us  [small_body(): parts = lax.all_to_all(sums, ('dp', 'space'), 0, 0)]
    ppermute x4, waiting for transfers between devices: 6.59 us -> 3.64 us  [over_dp(): return lax.ppermute(x, 'dp', swap)]
    ppermute x4, starting transfers between devices: 6.86 us -> 4.05 us  [over_dp(): return lax.ppermute(x, 'dp', swap)]
    ppermute x4 -> x6, waiting for transfers between devices: 9.48 us -> 6.83 us  [the longest x2 6.63 us: to_second(): return lax.ppermute(x, 'dp', swap)]
    unnamed x26, local copies, waits for them, and re-layouts: 1.22 us -> 3.32 us
    ppermute x3 -> x4, starting transfers between devices: 3.66 us -> 2.31 us  [over_pair(): return lax.ppermute(x, 'space', pair)]
    ppermute x3 -> x4, waiting for transfers between devices: 0.33 us -> 1.17 us  [over_pair(): return lax.ppermute(x, 'space', pair)]
  transfers between devices with their start and end apart: 14 -> 17, of which waited for: 9 -> 7; matrix products, arithmetic and copies ran while one was open for 0% -> 0% of each run, Pallas kernels for 5% -> 11%
where the time goes in v4:
time: 65.6 us; the launch traced here: 65.2 us
  starting transfers between devices  20.2 us (31%)
  blocking collectives  18.9 us (29%)
  waiting for transfers between devices  11.6 us (18%)
  Pallas kernels  9.61 us (15%)
  local copies, waits for them, and re-layouts  3.32 us (5%)
  between operations  1.5 us (2%)
    all_to_all x1, blocking collectives, small_body(): parts = lax.all_to_all(sums, ('dp', 'space'), 0, 0)  18.9 us
    pallas_call x15, Pallas kernels, call(): pl.pallas_call(kernel, out_shape=tuple(outs), in_specs=[pl.BlockSpec(memo...  9.61 us
    ppermute x2, waiting for transfers between devices, to_second(): return lax.ppermute(x, 'dp', swap)  6.63 us
    ppermute x1, starting transfers between devices, small_body(): lax.ppermute(share, 'space', [(i, i ^ 4) for i in range(space)])  4.83 us
    ppermute x4, starting transfers between devices, over_dp(): return lax.ppermute(x, 'dp', swap)  4.05 us
    ppermute x4, waiting for transfers between devices, over_dp(): return lax.ppermute(x, 'dp', swap)  3.64 us
    unnamed x26, local copies, waits for them, and re-layouts  3.32 us
    ppermute x2, starting transfers between devices, to_first(): return lax.ppermute(x, 'dp', swap)  2.91 us
  transfers between devices with their start and end apart: 17, of which 7 were waited for; matrix products, arithmetic and copies ran while one was open for 0% of the time, Pallas kernels for 11%

profile of v4, /device:TPU:0, one launch (start us, length us, event | category | flops | bytes accessed | tf_op | source)
XLA Modules:
  0.0 65.2 jit_solution(6136726135774084251)
XLA Ops:
  1.8 2.6 %collective-permute-start.3 = (bf16[100,512]{1,0:T(8,128)(2,1)}, bf16[100,512]{1,0:T(8,128)(2,1)S(1)}, u32[]{:S(2)}, u32[]{:S(2)}) collective-permute-start(bf16[100,512]{1,0:T(8,128)(2,1)} %we_here.3), channel_id=1, source_target_pairs={{0,16},{16,0},{1,17},{17,1},{2,18},{18,2},{3,19},{19,3},{4,20},{20... | collective-permute-start | bytes 307208 | tf_op jit(solution)/shard_map/ppermute | solution.py:354
  4.4 0.7 %copy-done.12 = s32[32,12]{0,1:T(8,128)S(1)} copy-done((s32[32,12]{0,1:T(8,128)S(1)}, s32[32,12]{0,1:T(8,128)}, u32[]{:S(2)}) %copy-start.12) | copy-done | bytes 1560
  6.2 0.9 %copy-done.2 = bf16[1024,512]{1,0:T(8,128)(2,1)S(1)} copy-done((bf16[1024,512]{1,0:T(8,128)(2,1)S(1)}, bf16[1024,512]{1,0:T(8,128)(2,1)}, u32[]{:S(2)}) %copy-start.2) | copy-done | bytes 1048600
  7.9 0.8 %copy-done.10 = bf16[1024,1024]{1,0:T(8,128)(2,1)S(1)} copy-done((bf16[1024,1024]{1,0:T(8,128)(2,1)S(1)}, bf16[1024,1024]{1,0:T(8,128)(2,1)}, u32[]{:S(2)}) %copy-start.10) | copy-done | bytes 2097176
  8.7 2.0 %shard_map.151 = (bf16[384,1024]{1,0:T(8,128)(2,1)S(1)}, bf16[16,384]{1,0:T(8,128)(2,1)S(1)}) custom-call(bf16[32,1024]{1,0:T(8,128)(2,1)S(1)} %copy-done.4, f32[384,128]{1,0:T(8,128)S(1)} %get-tuple-element.22.present_ref, bf16[100,384]{1,0:T(8,128)(2,1)S(1)} %shard_map.150.near_ref, bf16[100,512]{1,0:T(8,128)(2,1)S(1)} %copy-done.11, ...), custom_call_target="tpu_custom_call" | custom-call | flops 883949568 | bytes 2640896 | tf_op jit(solution)/shard_map/pallas_call | solution.py:44
  11.3 2.1 %shard_map.152 = (bf16[384,1024]{1,0:T(8,128)(2,1)S(1)}, bf16[16,768]{1,0:T(8,128)(2,1)S(1)}) custom-call(bf16[32,1024]{1,0:T(8,128)(2,1)S(1)} %copy-done.4, f32[384,128]{1,0:T(8,128)S(1)} %get-tuple-element.22.present_ref, bf16[100,384]{1,0:T(8,128)(2,1)S(1)} %collective-permute-done.2.near_ref, bf16[100,512]{1,0:T(8,128)(2,1)S(1)} %copy-done.11, ...), custom_call_target="tpu_custom_call" | custom-call | flops 883949568 | bytes 2653184 | tf_op jit(solution)/shard_map/pallas_call | solution.py:44
  13.3 0.9 %collective-permute-start.4 = (bf16[16,768]{1,0:T(8,128)(2,1)S(1)}, bf16[16,768]{1,0:T(8,128)(2,1)S(1)}, u32[]{:S(2)}, u32[]{:S(2)}) collective-permute-start(bf16[16,768]{1,0:T(8,128)(2,1)S(1)} %get-tuple-element.25), channel_id=1, source_target_pairs={{0,16},{16,0},{1,17},{17,1},{2,18},{18,2},{3,19},{19,3},{4,20},{20... | collective-permute-start | bytes 73736 | tf_op jit(solution)/shard_map/ppermute | solution.py:360
  14.3 3.2 %collective-permute-done.4.probs = bf16[16,768]{1,0:T(8,128)(2,1)S(1)} collective-permute-done((bf16[16,768]{1,0:T(8,128)(2,1)S(1)}, bf16[16,768]{1,0:T(8,128)(2,1)S(1)}, u32[]{:S(2)}, u32[]{:S(2)}) %collective-permute-start.4) | collective-permute-done | bytes 24608 | tf_op jit(solution)/shard_map/ppermute | solution.py:360
  17.5 4.8 %collective-permute-start.14 = (bf16[144,512]{1,0:T(8,128)(2,1)S(1)}, bf16[144,512]{1,0:T(8,128)(2,1)S(1)}, u32[]{:S(2)}, u32[]{:S(2)}) collective-permute-start(bf16[144,512]{1,0:T(8,128)(2,1)S(1)} %collective-permute-done.13.mine), channel_id=1, source_target_pairs={{0,4},{1,5},{2,6},{3,7},{4,0},{5,1},{6,2},{7,3},{8,12},{9,13},{10,... | collective-permute-start | bytes 442376 | tf_op jit(solution)/shard_map/ppermute | solution.py:420
  22.3 1.3 %collective-permute-start.5 = (bf16[64,1024]{1,0:T(8,128)(2,1)S(1)}, bf16[64,1024]{1,0:T(8,128)(2,1)S(1)}, u32[]{:S(2)}, u32[]{:S(2)}) collective-permute-start(bf16[64,1024]{1,0:T(8,128)(2,1)S(1)} %shard_map.153.mine.latent), channel_id=1, source_target_pairs={{0,16},{16,0},{1,17},{17,1},{2,18},{18,2},{3,19},{19,3},{4,20},{20... | collective-permute-start | bytes 393224 | tf_op jit(solution)/shard_map/ppermute | solution.py:357
  23.7 1.6 %collective-permute-start.7 = (bf16[64,512]{1,0:T(8,128)(2,1)S(1)}, bf16[64,512]{1,0:T(8,128)(2,1)S(1)}, u32[]{:S(2)}, u32[]{:S(2)}) collective-permute-start(bf16[64,512]{1,0:T(8,128)(2,1)S(1)} %get-tuple-element.33), channel_id=1, source_target_pairs={{0,16},{16,0},{1,17},{17,1},{2,18},{18,2},{3,19},{19,3},{4,20},{20... | collective-permute-start | bytes 196616 | tf_op jit(solution)/shard_map/ppermute | solution.py:357
  25.6 2.3 %collective-permute-start.15 = (bf16[288,512]{1,0:T(8,128)(2,1)S(1)}, bf16[288,512]{1,0:T(8,128)(2,1)S(1)}, u32[]{:S(2)}, u32[]{:S(2)}) collective-permute-start(bf16[288,512]{1,0:T(8,128)(2,1)S(1)} %shard_map.160.mine), channel_id=1, source_target_pairs={{0,2},{1,3},{2,0},{3,1},{4,6},{5,7},{6,4},{7,5},{8,10},{9,11},{10,... | collective-permute-start | bytes 884744 | tf_op jit(solution)/shard_map/ppermute | solution.py:373
  27.9 0.8 %shard_map.154 = (bf16[64,1024]{1,0:T(8,128)(2,1)S(1)}, bf16[64,512]{1,0:T(8,128)(2,1)S(1)}, bf16[64,512]{1,0:T(8,128)(2,1)S(1)}, bf16[64,512]{1,0:T(8,128)(2,1)S(1)}) custom-call(bf16[64,1024]{1,0:T(8,128)(2,1)S(1)} %shard_map.153.mine.latent, bf16[64,1024]{1,0:T(8,128)(2,1)S(1)} %collective-permute-done.5.came, bf16[1024,1536]{1,0:T(8,128)(2,1)S(1)} %copy-done), custom_call_target="tpu_custom_call" | custom-call | flops 201326592 | bytes 3407872 | tf_op jit(solution)/shard_map/pallas_call | solution.py:44
  28.8 0.7 %collective-permute-start.9 = (bf16[64,1024]{1,0:T(8,128)(2,1)S(1)}, bf16[64,1024]{1,0:T(8,128)(2,1)S(1)}, u32[]{:S(2)}, u32[]{:S(2)}) collective-permute-start(bf16[64,1024]{1,0:T(8,128)(2,1)S(1)} %shard_map.156.pairs0), channel_id=1, source_target_pairs={{1,2},{3,4},{5,6},{7,8},{9,10},{11,12},{13,14},{2,1},{4,3},{6,5},{... | collective-permute-start | bytes 393224 | tf_op jit(solution)/shard_map/ppermute | solution.py:366
  29.5 0.9 %collective-permute-start.6 = (bf16[64,512]{1,0:T(8,128)(2,1)S(1)}, bf16[64,512]{1,0:T(8,128)(2,1)S(1)}, u32[]{:S(2)}, u32[]{:S(2)}) collective-permute-start(bf16[64,512]{1,0:T(8,128)(2,1)S(1)} %get-tuple-element.30), channel_id=1, source_target_pairs={{0,16},{16,0},{1,17},{17,1},{2,18},{18,2},{3,19},{19,3},{4,20},{20... | collective-permute-start | bytes 196616 | tf_op jit(solution)/shard_map/ppermute | solution.py:360
  30.4 3.4 %collective-permute-done.6.came = bf16[64,512]{1,0:T(8,128)(2,1)S(1)} collective-permute-done((bf16[64,512]{1,0:T(8,128)(2,1)S(1)}, bf16[64,512]{1,0:T(8,128)(2,1)S(1)}, u32[]{:S(2)}, u32[]{:S(2)}) %collective-permute-start.6) | collective-permute-done | bytes 65568 | tf_op jit(solution)/shard_map/ppermute | solution.py:360
  33.9 1.2 %shard_map.157 = (f32[32,1024]{1,0:T(8,128)S(1)}, bf16[32,1024]{1,0:T(8,128)(2,1)S(1)}) custom-call(s32[16,32]{1,0:T(8,128)S(1)} %bitcast.22, bf16[64,1024]{1,0:T(8,128)(2,1)S(1)} %get-tuple-element.28.latent, bf16[64,512]{1,0:T(8,128)(2,1)S(1)} %get-tuple-element.29.mine, bf16[64,512]{1,0:T(8,128)(2,1)S(1)} %collective-permute-done.6.came, ...), custom_call_target="tpu_custom_call" | custom-call | flops 134217728 | bytes 1705984 | tf_op jit(solution)/shard_map/pallas_call | solution.py:44
  35.1 0.9 %collective-permute-start.10 = (bf16[32,1024]{1,0:T(8,128)(2,1)S(1)}, bf16[32,1024]{1,0:T(8,128)(2,1)S(1)}, u32[]{:S(2)}, u32[]{:S(2)}) collective-permute-start(bf16[32,1024]{1,0:T(8,128)(2,1)S(1)} %get-tuple-element.35), channel_id=1, source_target_pairs={{0,16},{16,0},{1,17},{17,1},{2,18},{18,2},{3,19},{19,3},{4,20},{20... | collective-permute-start | bytes 196616 | tf_op jit(solution)/shard_map/ppermute | solution.py:354
  35.9 3.4 %collective-permute-done.10.theirs = bf16[32,1024]{1,0:T(8,128)(2,1)S(1)} collective-permute-done((bf16[32,1024]{1,0:T(8,128)(2,1)S(1)}, bf16[32,1024]{1,0:T(8,128)(2,1)S(1)}, u32[]{:S(2)}, u32[]{:S(2)}) %collective-permute-start.10) | collective-permute-done | bytes 65568 | tf_op jit(solution)/shard_map/ppermute | solution.py:354
  39.4 1.4 %collective-permute-start.11 = (bf16[32,1024]{1,0:T(8,128)(2,1)S(1)}, bf16[32,1024]{1,0:T(8,128)(2,1)S(1)}, u32[]{:S(2)}, u32[]{:S(2)}) collective-permute-start(bf16[32,1024]{1,0:T(8,128)(2,1)S(1)} %shard_map.158.up0), channel_id=1, source_target_pairs={{0,1},{1,0},{2,3},{3,2},{4,5},{5,4},{6,7},{7,6},{8,9},{9,8},{10,11... | collective-permute-start | bytes 196616 | tf_op jit(solution)/shard_map/ppermute | solution.py:363
  40.9 0.8 %collective-permute-done.11.up1 = bf16[32,1024]{1,0:T(8,128)(2,1)S(1)} collective-permute-done((bf16[32,1024]{1,0:T(8,128)(2,1)S(1)}, bf16[32,1024]{1,0:T(8,128)(2,1)S(1)}, u32[]{:S(2)}, u32[]{:S(2)}) %collective-permute-start.11) | collective-permute-done | bytes 65568 | tf_op jit(solution)/shard_map/ppermute | solution.py:363
  42.0 0.7 %collective-permute-start.12 = (bf16[32,1024]{1,0:T(8,128)(2,1)S(1)}, bf16[32,1024]{1,0:T(8,128)(2,1)S(1)}, u32[]{:S(2)}, u32[]{:S(2)}) collective-permute-start(bf16[32,1024]{1,0:T(8,128)(2,1)S(1)} %shard_map.158.up0), channel_id=1, source_target_pairs={{1,2},{3,4},{5,6},{7,8},{9,10},{11,12},{13,14},{2,1},{4,3},{6,5},{... | collective-permute-start | bytes 196616 | tf_op jit(solution)/shard_map/ppermute | solution.py:366
  43.7 2.0 %shard_map.162 = (bf16[100,128]{1,0:T(8,128)(2,1)}, f32[32,8,100]{2,1,0:T(8,128)S(1)}) custom-call(s32[1]{0:T(128)S(6)} %copy.16.limit, s32[3,128]{1,0:T(4,128)S(1)} %bitcast.23, bf16[100,128]{1,0:T(8,128)(2,1)S(1)} %bitcast.20, bf16[100,128]{1,0:T(8,128)(2,1)S(1)} %bitcast.21, f32[1,128]{1,0:T(1,128)S(1)} %bitcast.24, bf16[32,1024]{1,0:T(8,128)(2,1)S(1)} %shard_map.158.up0, ...), custom_call_target="tpu_custom_call" | custom-call | flops 294649856 | bytes 2580484 | tf_op jit(solution)/shard_map/pallas_call | solution.py:44
  45.7 18.9 %all_to_all.5.parts = f32[32,8,100]{2,1,0:T(8,128)S(1)} all-to-all(f32[32,8,100]{2,1,0:T(8,128)S(1)} %get-tuple-element.41), channel_id=1, replica_groups=mesh['dp'=2,'space'=16] {'dp','space'}, dimensions={0} | all-to-all | bytes 204800 | tf_op jit(solution)/shard_map/all_to_all | solution.py:466
  (52 shorter events, 5.4 us)
Async XLA Ops:
  0.6 4.9 %collective-permute-start = (bf16[100,128]{1,0:T(8,128)(2,1)}, bf16[100,128]{1,0:T(8,128)(2,1)S(1)}, u32[]{:S(2)}, u32[]{:S(2)}) collective-permute-start(bf16[100,128]{1,0:T(8,128)(2,1)} %bitcast.17), channel_id=1, source_target_pairs={{0,1},{1,0},{2,3},{3,2},{4,5},{5,4},{6,7},{7,6},{8,9},{9,8},{10,11... | collective-permute-start | bytes 76808 | tf_op jit(solution)/shard_map/ppermute | solution.py:363
  1.1 4.4 %collective-permute-start.1 = (bf16[100,128]{1,0:T(8,128)(2,1)}, bf16[100,128]{1,0:T(8,128)(2,1)S(1)}, u32[]{:S(2)}, u32[]{:S(2)}) collective-permute-start(bf16[100,128]{1,0:T(8,128)(2,1)} %bitcast.18), channel_id=1, source_target_pairs={{1,2},{3,4},{5,6},{7,8},{9,10},{11,12},{13,14},{2,1},{4,3},{6,5},{... | collective-permute-start | bytes 76808 | tf_op jit(solution)/shard_map/ppermute | solution.py:366
  1.8 5.5 %collective-permute-start.3 = (bf16[100,512]{1,0:T(8,128)(2,1)}, bf16[100,512]{1,0:T(8,128)(2,1)S(1)}, u32[]{:S(2)}, u32[]{:S(2)}) collective-permute-start(bf16[100,512]{1,0:T(8,128)(2,1)} %we_here.3), channel_id=1, source_target_pairs={{0,16},{16,0},{1,17},{17,1},{2,18},{18,2},{3,19},{19,3},{4,20},{20... | collective-permute-start | bytes 307208 | tf_op jit(solution)/shard_map/ppermute | solution.py:354
  6.1 4.7 %collective-permute-start.2 = (bf16[100,384]{1,0:T(8,128)(2,1)S(1)}, bf16[100,384]{1,0:T(8,128)(2,1)S(1)}, u32[]{:S(2)}, u32[]{:S(2)}) collective-permute-start(bf16[100,384]{1,0:T(8,128)(2,1)S(1)} %shard_map.150.near_ref), channel_id=1, source_target_pairs={{0,16},{16,0},{1,17},{17,1},{2,18},{18,2},{3,19},{19,3},{4,20},{20... | collective-permute-start | bytes 230408 | tf_op jit(solution)/shard_map/ppermute | solution.py:354
  7.1 1.6 %copy-start.11 = (bf16[100,512]{1,0:T(8,128)(2,1)S(1)}, bf16[100,512]{1,0:T(8,128)(2,1)}, u32[]{:S(2)}) copy-start(bf16[100,512]{1,0:T(8,128)(2,1)} %we_here.3) | copy-start | bytes 307204
  10.7 12.9 %copy-start = (bf16[1024,1536]{1,0:T(8,128)(2,1)S(1)}, bf16[1024,1536]{1,0:T(8,128)(2,1)}, u32[]{:S(2)}) copy-start(bf16[1024,1536]{1,0:T(8,128)(2,1)} %w_ref.7) | copy-start | bytes 9437188
  10.8 6.8 %collective-permute-start.13 = (bf16[144,512]{1,0:T(8,128)(2,1)S(1)}, bf16[144,512]{1,0:T(8,128)(2,1)S(1)}, u32[]{:S(2)}, u32[]{:S(2)}) collective-permute-start(bf16[144,512]{1,0:T(8,128)(2,1)S(1)} %shard_map.159), channel_id=1, source_target_pairs={{0,16},{16,0},{1,17},{17,1},{2,18},{18,2},{3,19},{19,3},{4,20},{20... | collective-permute-start | bytes 442376 | tf_op jit(solution)/shard_map/ppermute | solution.py:354
  13.3 4.1 %collective-permute-start.4 = (bf16[16,768]{1,0:T(8,128)(2,1)S(1)}, bf16[16,768]{1,0:T(8,128)(2,1)S(1)}, u32[]{:S(2)}, u32[]{:S(2)}) collective-permute-start(bf16[16,768]{1,0:T(8,128)(2,1)S(1)} %get-tuple-element.25), channel_id=1, source_target_pairs={{0,16},{16,0},{1,17},{17,1},{2,18},{18,2},{3,19},{19,3},{4,20},{20... | collective-permute-start | bytes 73736 | tf_op jit(solution)/shard_map/ppermute | solution.py:360
  17.5 16.4 %copy-start.1 = (bf16[512,1024]{1,0:T(8,128)(2,1)S(1)}, bf16[512,1024]{1,0:T(8,128)(2,1)}, u32[]{:S(2)}) copy-start(bf16[512,1024]{1,0:T(8,128)(2,1)} %wo_ref.1) | copy-start | bytes 3145732
  17.5 16.4 %copy-start.7 = (s32[32,16]{0,1:T(8,128)S(1)}, s32[32,16]{0,1:T(8,128)}, u32[]{:S(2)}) copy-start(s32[32,16]{0,1:T(8,128)} %param.20) | copy-start | bytes 6148
  17.5 8.0 %collective-permute-start.14 = (bf16[144,512]{1,0:T(8,128)(2,1)S(1)}, bf16[144,512]{1,0:T(8,128)(2,1)S(1)}, u32[]{:S(2)}, u32[]{:S(2)}) collective-permute-start(bf16[144,512]{1,0:T(8,128)(2,1)S(1)} %collective-permute-done.13.mine), channel_id=1, source_target_pairs={{0,4},{1,5},{2,6},{3,7},{4,0},{5,1},{6,2},{7,3},{8,12},{9,13},{10,... | collective-permute-start | bytes 442376 | tf_op jit(solution)/shard_map/ppermute | solution.py:420
  22.3 5.5 %collective-permute-start.5 = (bf16[64,1024]{1,0:T(8,128)(2,1)S(1)}, bf16[64,1024]{1,0:T(8,128)(2,1)S(1)}, u32[]{:S(2)}, u32[]{:S(2)}) collective-permute-start(bf16[64,1024]{1,0:T(8,128)(2,1)S(1)} %shard_map.153.mine.latent), channel_id=1, source_target_pairs={{0,16},{16,0},{1,17},{17,1},{2,18},{18,2},{3,19},{19,3},{4,20},{20... | collective-permute-start | bytes 393224 | tf_op jit(solution)/shard_map/ppermute | solution.py:357
  23.7 5.0 %collective-permute-start.7 = (bf16[64,512]{1,0:T(8,128)(2,1)S(1)}, bf16[64,512]{1,0:T(8,128)(2,1)S(1)}, u32[]{:S(2)}, u32[]{:S(2)}) collective-permute-start(bf16[64,512]{1,0:T(8,128)(2,1)S(1)} %get-tuple-element.33), channel_id=1, source_target_pairs={{0,16},{16,0},{1,17},{17,1},{2,18},{18,2},{3,19},{19,3},{4,20},{20... | collective-permute-start | bytes 196616 | tf_op jit(solution)/shard_map/ppermute | solution.py:357
  25.5 18.2 %copy-start.6 = (bf16[1,128,100]{1,2,0:T(8,128)(2,1)S(1)}, bf16[1,128,100]{1,2,0:T(8,128)(2,1)}, u32[]{:S(2)}) copy-start(bf16[1,128,100]{1,2,0:T(8,128)(2,1)} %param.15) | copy-start | bytes 76804
  25.5 18.2 %copy-start.8 = (s32[128,3]{0,1:T(4,128)S(1)}, s32[128,3]{0,1:T(4,128)}, u32[]{:S(2)}) copy-start(s32[128,3]{0,1:T(4,128)} %param.21) | copy-start | bytes 4612
  25.5 18.2 %copy-start.9 = (f32[128]{0:T(128)S(1)}, f32[128]{0:T(128)}, u32[]{:S(2)}) copy-start(f32[128]{0:T(128)} %param.16) | copy-start | bytes 1540
  25.6 15.2 %collective-permute-start.15 = (bf16[288,512]{1,0:T(8,128)(2,1)S(1)}, bf16[288,512]{1,0:T(8,128)(2,1)S(1)}, u32[]{:S(2)}, u32[]{:S(2)}) collective-permute-start(bf16[288,512]{1,0:T(8,128)(2,1)S(1)} %shard_map.160.mine), channel_id=1, source_target_pairs={{0,2},{1,3},{2,0},{3,1},{4,6},{5,7},{6,4},{7,5},{8,10},{9,11},{10,... | collective-permute-start | bytes 884744 | tf_op jit(solution)/shard_map/ppermute | solution.py:373
  28.8 5.1 %collective-permute-start.8 = (bf16[64,1024]{1,0:T(8,128)(2,1)S(1)}, bf16[64,1024]{1,0:T(8,128)(2,1)S(1)}, u32[]{:S(2)}, u32[]{:S(2)}) collective-permute-start(bf16[64,1024]{1,0:T(8,128)(2,1)S(1)} %shard_map.156.pairs0), channel_id=1, source_target_pairs={{0,1},{1,0},{2,3},{3,2},{4,5},{5,4},{6,7},{7,6},{8,9},{9,8},{10,11... | collective-permute-start | bytes 393224 | tf_op jit(solution)/shard_map/ppermute | solution.py:363
  28.8 5.0 %collective-permute-start.9 = (bf16[64,1024]{1,0:T(8,128)(2,1)S(1)}, bf16[64,1024]{1,0:T(8,128)(2,1)S(1)}, u32[]{:S(2)}, u32[]{:S(2)}) collective-permute-start(bf16[64,1024]{1,0:T(8,128)(2,1)S(1)} %shard_map.156.pairs0), channel_id=1, source_target_pairs={{1,2},{3,4},{5,6},{7,8},{9,10},{11,12},{13,14},{2,1},{4,3},{6,5},{... | collective-permute-start | bytes 393224 | tf_op jit(solution)/shard_map/ppermute | solution.py:366
  29.5 4.3 %collective-permute-start.6 = (bf16[64,512]{1,0:T(8,128)(2,1)S(1)}, bf16[64,512]{1,0:T(8,128)(2,1)S(1)}, u32[]{:S(2)}, u32[]{:S(2)}) collective-permute-start(bf16[64,512]{1,0:T(8,128)(2,1)S(1)} %get-tuple-element.30), channel_id=1, source_target_pairs={{0,16},{16,0},{1,17},{17,1},{2,18},{18,2},{3,19},{19,3},{4,20},{20... | collective-permute-start | bytes 196616 | tf_op jit(solution)/shard_map/ppermute | solution.py:360
  35.1 4.3 %collective-permute-start.10 = (bf16[32,1024]{1,0:T(8,128)(2,1)S(1)}, bf16[32,1024]{1,0:T(8,128)(2,1)S(1)}, u32[]{:S(2)}, u32[]{:S(2)}) collective-permute-start(bf16[32,1024]{1,0:T(8,128)(2,1)S(1)} %get-tuple-element.35), channel_id=1, source_target_pairs={{0,16},{16,0},{1,17},{17,1},{2,18},{18,2},{3,19},{19,3},{4,20},{20... | collective-permute-start | bytes 196616 | tf_op jit(solution)/shard_map/ppermute | solution.py:354
  39.4 2.3 %collective-permute-start.11 = (bf16[32,1024]{1,0:T(8,128)(2,1)S(1)}, bf16[32,1024]{1,0:T(8,128)(2,1)S(1)}, u32[]{:S(2)}, u32[]{:S(2)}) collective-permute-start(bf16[32,1024]{1,0:T(8,128)(2,1)S(1)} %shard_map.158.up0), channel_id=1, source_target_pairs={{0,1},{1,0},{2,3},{3,2},{4,5},{5,4},{6,7},{7,6},{8,9},{9,8},{10,11... | collective-permute-start | bytes 196616 | tf_op jit(solution)/shard_map/ppermute | solution.py:363
  41.7 2.0 %collective-permute-start.16 = (bf16[576,512]{1,0:T(8,128)(2,1)S(1)}, bf16[576,512]{1,0:T(8,128)(2,1)S(1)}, u32[]{:S(2)}, u32[]{:S(2)}) collective-permute-start(bf16[576,512]{1,0:T(8,128)(2,1)S(1)} %shard_map.161.part0), channel_id=1, source_target_pairs={{0,1},{1,0},{2,3},{3,2},{4,5},{5,4},{6,7},{7,6},{8,9},{9,8},{10,11... | collective-permute-start | bytes 1769480 | tf_op jit(solution)/shard_map/ppermute | solution.py:363
  42.0 1.3 %collective-permute-start.12 = (bf16[32,1024]{1,0:T(8,128)(2,1)S(1)}, bf16[32,1024]{1,0:T(8,128)(2,1)S(1)}, u32[]{:S(2)}, u32[]{:S(2)}) collective-permute-start(bf16[32,1024]{1,0:T(8,128)(2,1)S(1)} %shard_map.158.up0), channel_id=1, source_target_pairs={{1,2},{3,4},{5,6},{7,8},{9,10},{11,12},{13,14},{2,1},{4,3},{6,5},{... | collective-permute-start | bytes 196616 | tf_op jit(solution)/shard_map/ppermute | solution.py:366
  (6 other events, 6.4 us)

commit v5 on v4

--- a/solution.py
+++ b/solution.py
@@ -184,8 +184,11 @@
         latent_ref[...] = jnp.zeros_like(latent_ref)
 
 
-def add_kernel(mine, theirs, out_ref):
+def add_kernel(mine, theirs, out_ref, left_ref, right_ref):
+    half = left_ref.shape[1]
     out_ref[...] = (mine[...] + theirs[...].astype(F32)).astype(BF16)
+    left_ref[...] = out_ref[:, :half]
+    right_ref[...] = out_ref[:, half:]
 
 
 def later_kernel(latent, w_ref, send_ref, pairs_ref):
@@ -225,15 +228,18 @@
         keys_ref[...] = jnp.zeros(keys_ref.shape, BF16)
 
 
-def pairs_kernel(mine, keys, values, out_ref):
+def pairs_kernel(mine, keys, values, out_ref, keys_ref, values_ref):
     half = keys.shape[1]
     first = lax.axis_index("dp") == 0
-    out_ref[:, :half] = jnp.where(first, keys[...], mine[:, :half])
-    out_ref[:, half:] = jnp.where(first, values[...], mine[:, half:])
+    keys_ref[...] = jnp.where(first, keys[...], mine[:, :half])
+    values_ref[...] = jnp.where(first, values[...], mine[:, half:])
+    out_ref[:, :half] = keys_ref[...]
+    out_ref[:, half:] = values_ref[...]
 
 
 def mesh_kernel(
-    index_ref, latent, mine, came, pairs0, pairs1, pairs2, wo_ref, keep_ref, send_ref, sums_ref
+    index_ref, latent, mine, came, pairs0, keys1, values1, pairs2, wo_ref, keep_ref, send_ref,
+    sums_ref,
 ):
     both, half = mine.shape
     nodes = both // 2
@@ -242,8 +248,8 @@
     per_head = half // heads
     first = lax.axis_index("dp") == 0
     queries = jnp.where(first, mine[...], came[...])
-    pairs = jnp.concatenate([pairs0[...], pairs1[...], pairs2[...]], axis=0)
-    keys, values = pairs[:, :half], pairs[:, half:]
+    keys = jnp.concatenate([pairs0[:, :half], keys1[...], pairs2[:, :half]], axis=0)
+    values = jnp.concatenate([pairs0[:, half:], values1[...], pairs2[:, half:]], axis=0)
     place = side_block(jnp.transpose(index_ref[...]), nodes)
     near = lax.broadcasted_iota(jnp.int32, (nodes, rows), 1)
     code = (near // both) * nodes + near % nodes
@@ -276,37 +282,39 @@
     send_ref[...] = sums_ref[pl.ds(theirs, nodes), :].astype(BF16)
 
 
-def decode_kernel(
-    limit, index_ref, fields, target, area, up0, up1, up2,
-    w1_ref, part0, part1, w2_ref,
-    pred_ref, sums_ref, norm_ref, there_ref,
-):
-    count_field, slots = fields.shape
-    keep = lax.broadcasted_iota(jnp.int32, (8, slots), 1) < limit[0]
-    keep = keep.astype(F32)
-    weight = keep * area[...]
+def decode_kernel(index_ref, up0, left, right, up2, w1_ref, w2_ref, norm_ref, part_ref):
     nodes, width = up0.shape
-    entries = index_ref.shape[0]
+    entries, slots = index_ref.shape
     place = side_block(jnp.transpose(index_ref[...]), nodes)
     near = lax.broadcasted_iota(jnp.int32, (slots, nodes), 1)
     mean = 0.0
-    for i, updated in enumerate((up0, up1, up2)):
+    up1 = jnp.concatenate([left[...], right[...]], axis=1)
+    for i, updated in enumerate((up0[...], up1, up2[...])):
         times = sum((place[:, k : k + 1] == near + i * nodes).astype(F32) for k in range(entries))
-        mean += dot(times.astype(BF16), updated[...])
+        mean += dot(times.astype(BF16), updated)
     norm_ref[...] = normalize(mean * (1.0 / entries)).astype(BF16)
+    hidden = silu(dot(norm_ref[...], w1_ref[...])).astype(BF16)
+    part_ref[...] = dot_nt(w2_ref[...], hidden)
+
+
+def errors_kernel(
+    limit_ref, fields, target, area, norm_ref, part_ref, part0, part1, pred_ref, sums_ref,
+    there_ref,
+):
+    count_field, slots = fields.shape
+    keep = (lax.broadcasted_iota(jnp.int32, (8, slots), 1) < limit_ref[...]).astype(F32)
+    weight = keep * area[...]
     core = lax.axis_index("space") % 2
-    hidden = silu(dot(norm_ref[...], w1_ref[...])).astype(BF16)
-    hidden_there = 0.0
-    size = width // 2
+    size = norm_ref.shape[1] // 2
     tail = part0.shape[0] - size
+    hidden = 0.0
     for i, block in enumerate((part0, part1)):
         part = pl.multiple_of((core ^ i) * size, size)
-        hidden_there += dot(norm_ref[:, pl.ds(part, size)], block[:size, :])
+        hidden += dot(norm_ref[:, pl.ds(part, size)], block[:size, :])
         start = pl.multiple_of((core ^ i) * tail, tail)
         there_ref[pl.ds(start, tail), :] = block[size:, :]
-    hidden_there = silu(hidden_there).astype(BF16)
-    increment = dot_nt(w2_ref[...], hidden)
-    increment += dot_nt(there_ref[:count_field, :], hidden_there)
+    hidden = silu(hidden).astype(BF16)
+    increment = part_ref[...] + dot_nt(there_ref[:count_field, :], hidden)
     valid = keep[:1] > 0
     predicted = jnp.where(valid, fields[...].astype(F32) + increment, 0.0)
     pred_ref[...] = predicted.astype(BF16)
@@ -431,7 +439,11 @@
         (latent, came, w_qkv),
         flops=2 * 2 * nodes * width * 3 * half,
     )
-    (pairs,) = call(pairs_kernel, (shape((2 * nodes, width)),), (pairs, keys, values))
+    pairs, keys, values = call(
+        pairs_kernel,
+        (shape((2 * nodes, width)),) + (shape((2 * nodes, half)),) * 2,
+        (pairs, keys, values),
+    )
     (share,) = call(
         functools.partial(join_kernel, 4, tail),
         (shape((2 * share.shape[0], half)),),
@@ -441,27 +453,37 @@
     keep, send = call(
         mesh_kernel,
         (shape((nodes, width), F32), shape((nodes, width))),
-        (proc_index.T, latent, queries, to_second(send), pairs, over_pair(pairs),
-         over_link(pairs), w_out),
+        (proc_index.T, latent, queries, to_second(send), pairs, over_pair(keys),
+         over_pair(values), over_link(pairs), w_out),
         scratch=[pltpu.VMEM((2 * nodes, width), F32)],
-        flops=2 * 2 * nodes * width * width,
+        flops=4 * BUSY,
     )
     (share,) = call(
         functools.partial(join_kernel, 2, 2 * tail),
         (shape((2 * share.shape[0], half)),),
         (share, came_share),
     )
-    (updated,) = call(add_kernel, (shape((nodes, width)),), (keep, over_dp(send)))
-    up1 = over_pair(updated)
-    came_share = over_pair(after(share, up1))
+    updated, left, right = call(
+        add_kernel,
+        (shape((nodes, width)),) + (shape((nodes, half)),) * 2,
+        (keep, over_dp(send)),
+    )
+    left, right = over_pair(left), over_pair(right)
+    up2 = over_link(updated)
+    share = after(share, left, right, up2)
+    came_share = over_pair(share)
+    norm, part = call(
+        decode_kernel,
+        (shape((slots, width)), shape((field_count, slots), F32)),
+        (dec_index.T, updated, left, right, up2, w_dec1, w2),
+        flops=2 * slots * width * half,
+    )
     predicted, sums = call(
-        decode_kernel,
+        errors_kernel,
         (shape((field_count, slots)), shape((space * samples, 8, field_count), F32)),
-        (grid_count, dec_index.T, own, goal, area_weight[None], updated, up1,
-         over_link(updated), w_dec1, share, came_share, w2),
-        scratch=[pltpu.VMEM((slots, width), BF16), pltpu.VMEM((8 * tail, half), BF16)],
-        flops=2 * slots * width * (width + field_count),
-        smem=(0,),
+        (grid_count[None], own, goal, area_weight[None], norm, part, share, came_share),
+        scratch=[pltpu.VMEM((8 * tail, half), BF16)],
+        flops=2 * slots * width * half,
     )
     parts = lax.all_to_all(sums, ("dp", "space"), 0, 0)
     (loss,) = call(loss_kernel, (shape((1, 1), F32),), (parts,))

time: 65.6 us -> 62 us (0.945)
  blocking collectives: 18.9 us -> 13.2 us
  starting transfers between devices: 20.2 us -> 25.3 us
  local copies, waits for them, and re-layouts: 3.32 us -> 1.21 us
  waiting for transfers between devices: 11.6 us -> 10.6 us
    all_to_all x1, blocking collectives: 18.9 us -> 13.2 us  [small_body(): parts = lax.all_to_all(sums, ('dp', 'space'), 0, 0)]
    ppermute x4 -> x6, starting transfers between devices: 2.31 us -> 7.48 us  [over_pair(): return lax.ppermute(x, 'space', pair)]
    ppermute x2, waiting for transfers between devices: 6.63 us -> 3.94 us  [to_second(): return lax.ppermute(x, 'dp', swap)]
    unnamed x26, local copies, waits for them, and re-layouts: 3.32 us -> 1.21 us
    ppermute x4, waiting for transfers between devices: 3.64 us -> 5.53 us  [over_dp(): return lax.ppermute(x, 'dp', swap)]
    ppermute x4, starting transfers between devices: 4.05 us -> 5.69 us  [over_dp(): return lax.ppermute(x, 'dp', swap)]
    ppermute x1, starting transfers between devices: 2.32 us -> 1.22 us  [over_quad(): return lax.ppermute(x, 'space', [(i, i ^ 2) for i in range(space)])]
    ppermute x2, starting transfers between devices: 1.82 us -> 0.97 us  [to_second(): return lax.ppermute(x, 'dp', swap)]
  transfers between devices with their start and end apart: 17 -> 19, of which waited for: 7 -> 7; matrix products, arithmetic and copies ran while one was open for 0% -> 0% of each run, Pallas kernels for 11% -> 10%
where the time goes in v5:
time: 62 us; the launch traced here: 61.7 us
  starting transfers between devices  25.3 us (41%)
  blocking collectives  13.2 us (21%)
  waiting for transfers between devices  10.6 us (17%)
  Pallas kernels  9.89 us (16%)
  between operations  1.53 us (2%)
  local copies, waits for them, and re-layouts  1.21 us (2%)
    all_to_all x1, blocking collectives, small_body(): parts = lax.all_to_all(sums, ('dp', 'space'), 0, 0)  13.2 us
    pallas_call x16, Pallas kernels, call(): pl.pallas_call(kernel, out_shape=tuple(outs), in_specs=[pl.BlockSpec(memo...  9.89 us
    ppermute x6, starting transfers between devices, over_pair(): return lax.ppermute(x, 'space', pair)  7.48 us
    ppermute x4, starting transfers between devices, over_dp(): return lax.ppermute(x, 'dp', swap)  5.69 us
    ppermute x4, waiting for transfers between devices, over_dp(): return lax.ppermute(x, 'dp', swap)  5.53 us
    ppermute x1, starting transfers between devices, small_body(): lax.ppermute(share, 'space', [(i, i ^ 4) for i in range(space)])  5.02 us
    ppermute x2, waiting for transfers between devices, to_second(): return lax.ppermute(x, 'dp', swap)  3.94 us
    ppermute x2, starting transfers between devices, to_first(): return lax.ppermute(x, 'dp', swap)  2.98 us
  transfers between devices with their start and end apart: 19, of which 7 were waited for; matrix products, arithmetic and copies ran while one was open for 0% of the time, Pallas kernels for 10%

profile of v5, /device:TPU:0, one launch (start us, length us, event | category | flops | bytes accessed | tf_op | source)
XLA Modules:
  0.0 61.7 jit_solution(12855811438290290296)
XLA Ops:
  1.8 2.6 %collective-permute-start.3 = (bf16[100,512]{1,0:T(8,128)(2,1)}, bf16[100,512]{1,0:T(8,128)(2,1)S(1)}, u32[]{:S(2)}, u32[]{:S(2)}) collective-permute-start(bf16[100,512]{1,0:T(8,128)(2,1)} %we_here.3), channel_id=1, source_target_pairs={{0,16},{16,0},{1,17},{17,1},{2,18},{18,2},{3,19},{19,3},{4,20},{20... | collective-permute-start | bytes 307208 | tf_op jit(solution)/shard_map/ppermute | solution.py:362
  4.4 0.7 %copy-done.11 = s32[32,12]{0,1:T(8,128)S(1)} copy-done((s32[32,12]{0,1:T(8,128)S(1)}, s32[32,12]{0,1:T(8,128)}, u32[]{:S(2)}) %copy-start.11) | copy-done | bytes 1560
  6.2 1.1 %collective-permute-done.3.we_there = bf16[100,512]{1,0:T(8,128)(2,1)S(1)} collective-permute-done((bf16[100,512]{1,0:T(8,128)(2,1)}, bf16[100,512]{1,0:T(8,128)(2,1)S(1)}, u32[]{:S(2)}, u32[]{:S(2)}) %collective-permute-start.3) | collective-permute-done | bytes 102432 | tf_op jit(solution)/shard_map/ppermute | solution.py:362
  7.5 2.0 %shard_map.151 = (bf16[384,1024]{1,0:T(8,128)(2,1)S(1)}, bf16[16,384]{1,0:T(8,128)(2,1)S(1)}) custom-call(bf16[32,1024]{1,0:T(8,128)(2,1)S(1)} %copy-done.3, f32[384,128]{1,0:T(8,128)S(1)} %get-tuple-element.30.present_ref, bf16[100,384]{1,0:T(8,128)(2,1)S(1)} %shard_map.150.near_ref, bf16[100,512]{1,0:T(8,128)(2,1)S(1)} %copy-done.10, ...), custom_call_target="tpu_custom_call" | custom-call | flops 883949568 | bytes 2640896 | tf_op jit(solution)/shard_map/pallas_call | solution.py:44
  9.5 1.1 %collective-permute-done.2.near_ref = bf16[100,384]{1,0:T(8,128)(2,1)S(1)} collective-permute-done((bf16[100,384]{1,0:T(8,128)(2,1)S(1)}, bf16[100,384]{1,0:T(8,128)(2,1)S(1)}, u32[]{:S(2)}, u32[]{:S(2)}) %collective-permute-start.2) | collective-permute-done | bytes 76832 | tf_op jit(solution)/shard_map/ppermute | solution.py:362
  10.6 2.0 %shard_map.152 = (bf16[384,1024]{1,0:T(8,128)(2,1)S(1)}, bf16[16,768]{1,0:T(8,128)(2,1)S(1)}) custom-call(bf16[32,1024]{1,0:T(8,128)(2,1)S(1)} %copy-done.3, f32[384,128]{1,0:T(8,128)S(1)} %get-tuple-element.30.present_ref, bf16[100,384]{1,0:T(8,128)(2,1)S(1)} %collective-permute-done.2.near_ref, bf16[100,512]{1,0:T(8,128)(2,1)S(1)} %copy-done.10, ...), custom_call_target="tpu_custom_call" | custom-call | flops 883949568 | bytes 2653184 | tf_op jit(solution)/shard_map/pallas_call | solution.py:44
  12.8 2.0 %collective-permute-start.15 = (bf16[144,512]{1,0:T(8,128)(2,1)S(1)}, bf16[144,512]{1,0:T(8,128)(2,1)S(1)}, u32[]{:S(2)}, u32[]{:S(2)}) collective-permute-start(bf16[144,512]{1,0:T(8,128)(2,1)S(1)} %shard_map.160), channel_id=1, source_target_pairs={{0,16},{16,0},{1,17},{17,1},{2,18},{18,2},{3,19},{19,3},{4,20},{20... | collective-permute-start | bytes 442376 | tf_op jit(solution)/shard_map/ppermute | solution.py:362
  14.8 1.7 %collective-permute-done.4.probs = bf16[16,768]{1,0:T(8,128)(2,1)S(1)} collective-permute-done((bf16[16,768]{1,0:T(8,128)(2,1)S(1)}, bf16[16,768]{1,0:T(8,128)(2,1)S(1)}, u32[]{:S(2)}, u32[]{:S(2)}) %collective-permute-start.4) | collective-permute-done | bytes 24608 | tf_op jit(solution)/shard_map/ppermute | solution.py:368
  16.6 0.7 %collective-permute-start.5 = (bf16[64,1024]{1,0:T(8,128)(2,1)S(1)}, bf16[64,1024]{1,0:T(8,128)(2,1)S(1)}, u32[]{:S(2)}, u32[]{:S(2)}) collective-permute-start(bf16[64,1024]{1,0:T(8,128)(2,1)S(1)} %shard_map.153.mine.latent), channel_id=1, source_target_pairs={{0,16},{16,0},{1,17},{17,1},{2,18},{18,2},{3,19},{19,3},{4,20},{20... | collective-permute-start | bytes 393224 | tf_op jit(solution)/shard_map/ppermute | solution.py:365
  17.3 2.3 %collective-permute-start.7 = (bf16[64,512]{1,0:T(8,128)(2,1)S(1)}, bf16[64,512]{1,0:T(8,128)(2,1)S(1)}, u32[]{:S(2)}, u32[]{:S(2)}) collective-permute-start(bf16[64,512]{1,0:T(8,128)(2,1)S(1)} %get-tuple-element.41), channel_id=1, source_target_pairs={{0,16},{16,0},{1,17},{17,1},{2,18},{18,2},{3,19},{19,3},{4,20},{20... | collective-permute-start | bytes 196616 | tf_op jit(solution)/shard_map/ppermute | solution.py:365
  19.6 5.0 %collective-permute-start.16 = (bf16[144,512]{1,0:T(8,128)(2,1)S(1)}, bf16[144,512]{1,0:T(8,128)(2,1)S(1)}, u32[]{:S(2)}, u32[]{:S(2)}) collective-permute-start(bf16[144,512]{1,0:T(8,128)(2,1)S(1)} %collective-permute-done.15.mine), channel_id=1, source_target_pairs={{0,4},{1,5},{2,6},{3,7},{4,0},{5,1},{6,2},{7,3},{8,12},{9,13},{10,... | collective-permute-start | bytes 442376 | tf_op jit(solution)/shard_map/ppermute | solution.py:428
  24.6 0.8 %shard_map.154 = (bf16[64,1024]{1,0:T(8,128)(2,1)S(1)}, bf16[64,512]{1,0:T(8,128)(2,1)S(1)}, bf16[64,512]{1,0:T(8,128)(2,1)S(1)}, bf16[64,512]{1,0:T(8,128)(2,1)S(1)}) custom-call(bf16[64,1024]{1,0:T(8,128)(2,1)S(1)} %shard_map.153.mine.latent, bf16[64,1024]{1,0:T(8,128)(2,1)S(1)} %collective-permute-done.5.came, bf16[1024,1536]{1,0:T(8,128)(2,1)S(1)} %copy-done), custom_call_target="tpu_custom_call" | custom-call | flops 201326592 | bytes 3407872 | tf_op jit(solution)/shard_map/pallas_call | solution.py:44
  26.1 3.6 %collective-permute-start.8 = (bf16[64,512]{1,0:T(8,128)(2,1)S(1)}, bf16[64,512]{1,0:T(8,128)(2,1)S(1)}, u32[]{:S(2)}, u32[]{:S(2)}) collective-permute-start(bf16[64,512]{1,0:T(8,128)(2,1)S(1)} %get-tuple-element.43), channel_id=1, source_target_pairs={{0,1},{1,0},{2,3},{3,2},{4,5},{5,4},{6,7},{7,6},{8,9},{9,8},{10,11... | collective-permute-start | bytes 196616 | tf_op jit(solution)/shard_map/ppermute | solution.py:371
  29.8 0.9 %collective-permute-start.6 = (bf16[64,512]{1,0:T(8,128)(2,1)S(1)}, bf16[64,512]{1,0:T(8,128)(2,1)S(1)}, u32[]{:S(2)}, u32[]{:S(2)}) collective-permute-start(bf16[64,512]{1,0:T(8,128)(2,1)S(1)} %get-tuple-element.38), channel_id=1, source_target_pairs={{0,16},{16,0},{1,17},{17,1},{2,18},{18,2},{3,19},{19,3},{4,20},{20... | collective-permute-start | bytes 196616 | tf_op jit(solution)/shard_map/ppermute | solution.py:368
  30.8 1.2 %collective-permute-start.17 = (bf16[288,512]{1,0:T(8,128)(2,1)S(1)}, bf16[288,512]{1,0:T(8,128)(2,1)S(1)}, u32[]{:S(2)}, u32[]{:S(2)}) collective-permute-start(bf16[288,512]{1,0:T(8,128)(2,1)S(1)} %shard_map.161.mine), channel_id=1, source_target_pairs={{0,2},{1,3},{2,0},{3,1},{4,6},{5,7},{6,4},{7,5},{8,10},{9,11},{10,... | collective-permute-start | bytes 884744 | tf_op jit(solution)/shard_map/ppermute | solution.py:381
  32.0 2.3 %collective-permute-done.6.came = bf16[64,512]{1,0:T(8,128)(2,1)S(1)} collective-permute-done((bf16[64,512]{1,0:T(8,128)(2,1)S(1)}, bf16[64,512]{1,0:T(8,128)(2,1)S(1)}, u32[]{:S(2)}, u32[]{:S(2)}) %collective-permute-start.6) | collective-permute-done | bytes 65568 | tf_op jit(solution)/shard_map/ppermute | solution.py:368
  34.3 1.2 %shard_map.157 = (f32[32,1024]{1,0:T(8,128)S(1)}, bf16[32,1024]{1,0:T(8,128)(2,1)S(1)}) custom-call(s32[16,32]{1,0:T(8,128)S(1)} %bitcast.27, bf16[64,1024]{1,0:T(8,128)(2,1)S(1)} %get-tuple-element.36.latent, bf16[64,512]{1,0:T(8,128)(2,1)S(1)} %get-tuple-element.37.mine, bf16[64,512]{1,0:T(8,128)(2,1)S(1)} %collective-permute-done.6.came, ...), custom_call_target="tpu_custom_call" | custom-call | flops 16000000000 | bytes 1705984 | tf_op jit(solution)/shard_map/pallas_call | solution.py:44
  35.5 1.0 %collective-permute-start.11 = (bf16[32,1024]{1,0:T(8,128)(2,1)S(1)}, bf16[32,1024]{1,0:T(8,128)(2,1)S(1)}, u32[]{:S(2)}, u32[]{:S(2)}) collective-permute-start(bf16[32,1024]{1,0:T(8,128)(2,1)S(1)} %get-tuple-element.46), channel_id=1, source_target_pairs={{0,16},{16,0},{1,17},{17,1},{2,18},{18,2},{3,19},{19,3},{4,20},{20... | collective-permute-start | bytes 196616 | tf_op jit(solution)/shard_map/ppermute | solution.py:362
  36.5 3.3 %collective-permute-done.11.theirs = bf16[32,1024]{1,0:T(8,128)(2,1)S(1)} collective-permute-done((bf16[32,1024]{1,0:T(8,128)(2,1)S(1)}, bf16[32,1024]{1,0:T(8,128)(2,1)S(1)}, u32[]{:S(2)}, u32[]{:S(2)}) %collective-permute-start.11) | collective-permute-done | bytes 65568 | tf_op jit(solution)/shard_map/ppermute | solution.py:362
  40.6 2.5 %collective-permute-start.12 = (bf16[32,512]{1,0:T(8,128)(2,1)S(1)}, bf16[32,512]{1,0:T(8,128)(2,1)S(1)}, u32[]{:S(2)}, u32[]{:S(2)}) collective-permute-start(bf16[32,512]{1,0:T(8,128)(2,1)S(1)} %get-tuple-element.48), channel_id=1, source_target_pairs={{0,1},{1,0},{2,3},{3,2},{4,5},{5,4},{6,7},{7,6},{8,9},{9,8},{10,11... | collective-permute-start | bytes 98312 | tf_op jit(solution)/shard_map/ppermute | solution.py:371
  43.2 0.7 %collective-permute-done.12.left = bf16[32,512]{1,0:T(8,128)(2,1)S(1)} collective-permute-done((bf16[32,512]{1,0:T(8,128)(2,1)S(1)}, bf16[32,512]{1,0:T(8,128)(2,1)S(1)}, u32[]{:S(2)}, u32[]{:S(2)}) %collective-permute-start.12) | collective-permute-done | bytes 32800 | tf_op jit(solution)/shard_map/ppermute | solution.py:371
  45.6 1.2 %shard_map.159 = (bf16[128,1024]{1,0:T(8,128)(2,1)S(1)}, f32[100,128]{1,0:T(8,128)S(1)}) custom-call(s32[3,128]{1,0:T(4,128)S(1)} %bitcast.24, bf16[32,1024]{1,0:T(8,128)(2,1)S(1)} %get-tuple-element.47.up0, bf16[32,512]{1,0:T(8,128)(2,1)S(1)} %collective-permute-done.12.left, bf16[32,512]{1,0:T(8,128)(2,1)S(1)} %collective-permute-done.13.right, ...), custom_call_target="tpu_custom_call" | custom-call | flops 134217728 | bytes 1349120 | tf_op jit(solution)/shard_map/pallas_call | solution.py:44
  46.8 1.1 %shard_map.163 = (bf16[100,128]{1,0:T(8,128)(2,1)}, f32[32,8,100]{2,1,0:T(8,128)S(1)}) custom-call(s32[1,1]{1,0:T(1,128)} %bitcast.16.limit_ref, bf16[100,128]{1,0:T(8,128)(2,1)S(1)} %bitcast.22, bf16[100,128]{1,0:T(8,128)(2,1)S(1)} %bitcast.23, f32[1,128]{1,0:T(1,128)S(1)} %bitcast.25, bf16[128,1024]{1,0:T(8,128)(2,1)S(1)} %get-tuple-element.50.norm_ref, ...), custom_call_target="tpu_custom_call" | custom-call | flops 134217728 | bytes 1544708 | tf_op jit(solution)/shard_map/pallas_call | solution.py:44
  47.9 13.2 %all_to_all.5.parts = f32[32,8,100]{2,1,0:T(8,128)S(1)} all-to-all(f32[32,8,100]{2,1,0:T(8,128)S(1)} %get-tuple-element.57), channel_id=1, replica_groups=mesh['dp'=2,'space'=16] {'dp','space'}, dimensions={0} | all-to-all | bytes 204800 | tf_op jit(solution)/shard_map/all_to_all | solution.py:488
  (57 shorter events, 5.9 us)
Async XLA Ops:
  0.6 4.9 %collective-permute-start = (bf16[100,128]{1,0:T(8,128)(2,1)}, bf16[100,128]{1,0:T(8,128)(2,1)S(1)}, u32[]{:S(2)}, u32[]{:S(2)}) collective-permute-start(bf16[100,128]{1,0:T(8,128)(2,1)} %bitcast.19), channel_id=1, source_target_pairs={{0,1},{1,0},{2,3},{3,2},{4,5},{5,4},{6,7},{7,6},{8,9},{9,8},{10,11... | collective-permute-start | bytes 76808 | tf_op jit(solution)/shard_map/ppermute | solution.py:371
  1.1 4.4 %collective-permute-start.1 = (bf16[100,128]{1,0:T(8,128)(2,1)}, bf16[100,128]{1,0:T(8,128)(2,1)S(1)}, u32[]{:S(2)}, u32[]{:S(2)}) collective-permute-start(bf16[100,128]{1,0:T(8,128)(2,1)} %bitcast.20), channel_id=1, source_target_pairs={{1,2},{3,4},{5,6},{7,8},{9,10},{11,12},{13,14},{2,1},{4,3},{6,5},{... | collective-permute-start | bytes 76808 | tf_op jit(solution)/shard_map/ppermute | solution.py:374
  1.8 5.5 %collective-permute-start.3 = (bf16[100,512]{1,0:T(8,128)(2,1)}, bf16[100,512]{1,0:T(8,128)(2,1)S(1)}, u32[]{:S(2)}, u32[]{:S(2)}) collective-permute-start(bf16[100,512]{1,0:T(8,128)(2,1)} %we_here.3), channel_id=1, source_target_pairs={{0,16},{16,0},{1,17},{17,1},{2,18},{18,2},{3,19},{19,3},{4,20},{20... | collective-permute-start | bytes 307208 | tf_op jit(solution)/shard_map/ppermute | solution.py:362
  6.1 4.5 %collective-permute-start.2 = (bf16[100,384]{1,0:T(8,128)(2,1)S(1)}, bf16[100,384]{1,0:T(8,128)(2,1)S(1)}, u32[]{:S(2)}, u32[]{:S(2)}) collective-permute-start(bf16[100,384]{1,0:T(8,128)(2,1)S(1)} %shard_map.150.near_ref), channel_id=1, source_target_pairs={{0,16},{16,0},{1,17},{17,1},{2,18},{18,2},{3,19},{19,3},{4,20},{20... | collective-permute-start | bytes 230408 | tf_op jit(solution)/shard_map/ppermute | solution.py:362
  12.6 3.9 %collective-permute-start.4 = (bf16[16,768]{1,0:T(8,128)(2,1)S(1)}, bf16[16,768]{1,0:T(8,128)(2,1)S(1)}, u32[]{:S(2)}, u32[]{:S(2)}) collective-permute-start(bf16[16,768]{1,0:T(8,128)(2,1)S(1)} %get-tuple-element.33), channel_id=1, source_target_pairs={{0,16},{16,0},{1,17},{17,1},{2,18},{18,2},{3,19},{19,3},{4,20},{20... | collective-permute-start | bytes 73736 | tf_op jit(solution)/shard_map/ppermute | solution.py:368
  12.8 6.8 %collective-permute-start.15 = (bf16[144,512]{1,0:T(8,128)(2,1)S(1)}, bf16[144,512]{1,0:T(8,128)(2,1)S(1)}, u32[]{:S(2)}, u32[]{:S(2)}) collective-permute-start(bf16[144,512]{1,0:T(8,128)(2,1)S(1)} %shard_map.160), channel_id=1, source_target_pairs={{0,16},{16,0},{1,17},{17,1},{2,18},{18,2},{3,19},{19,3},{4,20},{20... | collective-permute-start | bytes 442376 | tf_op jit(solution)/shard_map/ppermute | solution.py:362
  16.5 17.8 %copy-start.9 = (bf16[512,1024]{1,0:T(8,128)(2,1)S(1)}, bf16[512,1024]{1,0:T(8,128)(2,1)}, u32[]{:S(2)}) copy-start(bf16[512,1024]{1,0:T(8,128)(2,1)} %wo_ref.1) | copy-start | bytes 3145732
  16.5 17.7 %copy-start.12 = (s32[32,16]{0,1:T(8,128)S(1)}, s32[32,16]{0,1:T(8,128)}, u32[]{:S(2)}) copy-start(s32[32,16]{0,1:T(8,128)} %param.20) | copy-start | bytes 6148
  16.6 8.0 %collective-permute-start.5 = (bf16[64,1024]{1,0:T(8,128)(2,1)S(1)}, bf16[64,1024]{1,0:T(8,128)(2,1)S(1)}, u32[]{:S(2)}, u32[]{:S(2)}) collective-permute-start(bf16[64,1024]{1,0:T(8,128)(2,1)S(1)} %shard_map.153.mine.latent), channel_id=1, source_target_pairs={{0,16},{16,0},{1,17},{17,1},{2,18},{18,2},{3,19},{19,3},{4,20},{20... | collective-permute-start | bytes 393224 | tf_op jit(solution)/shard_map/ppermute | solution.py:365
  17.3 8.2 %collective-permute-start.7 = (bf16[64,512]{1,0:T(8,128)(2,1)S(1)}, bf16[64,512]{1,0:T(8,128)(2,1)S(1)}, u32[]{:S(2)}, u32[]{:S(2)}) collective-permute-start(bf16[64,512]{1,0:T(8,128)(2,1)S(1)} %get-tuple-element.41), channel_id=1, source_target_pairs={{0,16},{16,0},{1,17},{17,1},{2,18},{18,2},{3,19},{19,3},{4,20},{20... | collective-permute-start | bytes 196616 | tf_op jit(solution)/shard_map/ppermute | solution.py:365
  19.6 11.2 %collective-permute-start.16 = (bf16[144,512]{1,0:T(8,128)(2,1)S(1)}, bf16[144,512]{1,0:T(8,128)(2,1)S(1)}, u32[]{:S(2)}, u32[]{:S(2)}) collective-permute-start(bf16[144,512]{1,0:T(8,128)(2,1)S(1)} %collective-permute-done.15.mine), channel_id=1, source_target_pairs={{0,4},{1,5},{2,6},{3,7},{4,0},{5,1},{6,2},{7,3},{8,12},{9,13},{10,... | collective-permute-start | bytes 442376 | tf_op jit(solution)/shard_map/ppermute | solution.py:428
  25.5 8.8 %collective-permute-start.10 = (bf16[64,1024]{1,0:T(8,128)(2,1)S(1)}, bf16[64,1024]{1,0:T(8,128)(2,1)S(1)}, u32[]{:S(2)}, u32[]{:S(2)}) collective-permute-start(bf16[64,1024]{1,0:T(8,128)(2,1)S(1)} %get-tuple-element.42.pairs0), channel_id=1, source_target_pairs={{1,2},{3,4},{5,6},{7,8},{9,10},{11,12},{13,14},{2,1},{4,3},{6,5},{... | collective-permute-start | bytes 393224 | tf_op jit(solution)/shard_map/ppermute | solution.py:374
  26.1 5.9 %collective-permute-start.8 = (bf16[64,512]{1,0:T(8,128)(2,1)S(1)}, bf16[64,512]{1,0:T(8,128)(2,1)S(1)}, u32[]{:S(2)}, u32[]{:S(2)}) collective-permute-start(bf16[64,512]{1,0:T(8,128)(2,1)S(1)} %get-tuple-element.43), channel_id=1, source_target_pairs={{0,1},{1,0},{2,3},{3,2},{4,5},{5,4},{6,7},{7,6},{8,9},{9,8},{10,11... | collective-permute-start | bytes 196616 | tf_op jit(solution)/shard_map/ppermute | solution.py:371
  29.8 2.3 %collective-permute-start.9 = (bf16[64,512]{1,0:T(8,128)(2,1)S(1)}, bf16[64,512]{1,0:T(8,128)(2,1)S(1)}, u32[]{:S(2)}, u32[]{:S(2)}) collective-permute-start(bf16[64,512]{1,0:T(8,128)(2,1)S(1)} %get-tuple-element.44), channel_id=1, source_target_pairs={{0,1},{1,0},{2,3},{3,2},{4,5},{5,4},{6,7},{7,6},{8,9},{9,8},{10,11... | collective-permute-start | bytes 196616 | tf_op jit(solution)/shard_map/ppermute | solution.py:371
  29.8 4.4 %collective-permute-start.6 = (bf16[64,512]{1,0:T(8,128)(2,1)S(1)}, bf16[64,512]{1,0:T(8,128)(2,1)S(1)}, u32[]{:S(2)}, u32[]{:S(2)}) collective-permute-start(bf16[64,512]{1,0:T(8,128)(2,1)S(1)} %get-tuple-element.38), channel_id=1, source_target_pairs={{0,16},{16,0},{1,17},{17,1},{2,18},{18,2},{3,19},{19,3},{4,20},{20... | collective-permute-start | bytes 196616 | tf_op jit(solution)/shard_map/ppermute | solution.py:368
  30.8 12.4 %collective-permute-start.17 = (bf16[288,512]{1,0:T(8,128)(2,1)S(1)}, bf16[288,512]{1,0:T(8,128)(2,1)S(1)}, u32[]{:S(2)}, u32[]{:S(2)}) collective-permute-start(bf16[288,512]{1,0:T(8,128)(2,1)S(1)} %shard_map.161.mine), channel_id=1, source_target_pairs={{0,2},{1,3},{2,0},{3,1},{4,6},{5,7},{6,4},{7,5},{8,10},{9,11},{10,... | collective-permute-start | bytes 884744 | tf_op jit(solution)/shard_map/ppermute | solution.py:381
  34.3 11.3 %copy-start.6 = (s32[128,3]{0,1:T(4,128)S(1)}, s32[128,3]{0,1:T(4,128)}, u32[]{:S(2)}) copy-start(s32[128,3]{0,1:T(4,128)} %param.21) | copy-start | bytes 4612
  34.3 12.5 %copy-start.5 = (bf16[1,128,100]{1,2,0:T(8,128)(2,1)S(1)}, bf16[1,128,100]{1,2,0:T(8,128)(2,1)}, u32[]{:S(2)}) copy-start(bf16[1,128,100]{1,2,0:T(8,128)(2,1)} %param.15) | copy-start | bytes 76804
  34.3 12.5 %copy-start.7 = (f32[128]{0:T(128)S(1)}, f32[128]{0:T(128)}, u32[]{:S(2)}) copy-start(f32[128]{0:T(128)} %param.16) | copy-start | bytes 1540
  35.5 4.3 %collective-permute-start.11 = (bf16[32,1024]{1,0:T(8,128)(2,1)S(1)}, bf16[32,1024]{1,0:T(8,128)(2,1)S(1)}, u32[]{:S(2)}, u32[]{:S(2)}) collective-permute-start(bf16[32,1024]{1,0:T(8,128)(2,1)S(1)} %get-tuple-element.46), channel_id=1, source_target_pairs={{0,16},{16,0},{1,17},{17,1},{2,18},{18,2},{3,19},{19,3},{4,20},{20... | collective-permute-start | bytes 196616 | tf_op jit(solution)/shard_map/ppermute | solution.py:362
  39.9 4.4 %collective-permute-start.14 = (bf16[32,1024]{1,0:T(8,128)(2,1)S(1)}, bf16[32,1024]{1,0:T(8,128)(2,1)S(1)}, u32[]{:S(2)}, u32[]{:S(2)}) collective-permute-start(bf16[32,1024]{1,0:T(8,128)(2,1)S(1)} %get-tuple-element.47.up0), channel_id=1, source_target_pairs={{1,2},{3,4},{5,6},{7,8},{9,10},{11,12},{13,14},{2,1},{4,3},{6,5},{... | collective-permute-start | bytes 196616 | tf_op jit(solution)/shard_map/ppermute | solution.py:374
  40.6 3.4 %collective-permute-start.12 = (bf16[32,512]{1,0:T(8,128)(2,1)S(1)}, bf16[32,512]{1,0:T(8,128)(2,1)S(1)}, u32[]{:S(2)}, u32[]{:S(2)}) collective-permute-start(bf16[32,512]{1,0:T(8,128)(2,1)S(1)} %get-tuple-element.48), channel_id=1, source_target_pairs={{0,1},{1,0},{2,3},{3,2},{4,5},{5,4},{6,7},{7,6},{8,9},{9,8},{10,11... | collective-permute-start | bytes 98312 | tf_op jit(solution)/shard_map/ppermute | solution.py:371
  43.1 1.2 %collective-permute-start.13 = (bf16[32,512]{1,0:T(8,128)(2,1)S(1)}, bf16[32,512]{1,0:T(8,128)(2,1)S(1)}, u32[]{:S(2)}, u32[]{:S(2)}) collective-permute-start(bf16[32,512]{1,0:T(8,128)(2,1)S(1)} %get-tuple-element.49), channel_id=1, source_target_pairs={{0,1},{1,0},{2,3},{3,2},{4,5},{5,4},{6,7},{7,6},{8,9},{9,8},{10,11... | collective-permute-start | bytes 98312 | tf_op jit(solution)/shard_map/ppermute | solution.py:371
  44.3 2.5 %collective-permute-start.18 = (bf16[576,512]{1,0:T(8,128)(2,1)S(1)}, bf16[576,512]{1,0:T(8,128)(2,1)S(1)}, u32[]{:S(2)}, u32[]{:S(2)}) collective-permute-start(bf16[576,512]{1,0:T(8,128)(2,1)S(1)} %shard_map.162.part0), channel_id=1, source_target_pairs={{0,1},{1,0},{2,3},{3,2},{4,5},{5,4},{6,7},{7,6},{8,9},{9,8},{10,11... | collective-permute-start | bytes 1769480 | tf_op jit(solution)/shard_map/ppermute | solution.py:371
  (8 other events, 21.2 us)

commit v6 on v5

--- a/solution.py
+++ b/solution.py
@@ -82,11 +82,27 @@
     present_ref[...] = jnp.broadcast_to(present.astype(F32), present_ref.shape)
 
 
-def share_kernel(w1_ref, w2_ref, out_ref, pad_ref):
+def share_kernel(
+    proc_ref, dec_ref, w1_ref, w2_ref, out_ref, times_ref, counts_ref, pad_ref
+):
     size = w1_ref.shape[0] // 8
     tail = pad_ref.shape[0] // 8
     spot = lax.axis_index("space")
     share = (spot % 2) * 4 + ((spot // 2) % 2) * 2 + (spot // 4) % 2
+    both, rows = times_ref.shape
+    nodes = both // 2
+    place = side_block(jnp.transpose(proc_ref[...]), nodes)
+    near = lax.broadcasted_iota(jnp.int32, (nodes, rows), 1)
+    code = (near // both) * nodes + near % nodes
+    times = sum((place[:, j : j + 1] == code).astype(F32) for j in range(proc_ref.shape[0]))
+    second = (near // nodes) % 2
+    times_ref[:nodes, :] = jnp.where(second == 0, times, 0.0)
+    times_ref[nodes:, :] = jnp.where(second == 1, times, 0.0)
+    slots, rows = counts_ref.shape
+    place = side_block(jnp.transpose(dec_ref[...]), nodes)
+    near = lax.broadcasted_iota(jnp.int32, (slots, rows), 1)
+    counts = sum((place[:, k : k + 1] == near).astype(F32) for k in range(dec_ref.shape[0]))
+    counts_ref[...] = counts.astype(BF16)
     pad_ref[...] = jnp.zeros(pad_ref.shape, BF16)
     pad_ref[: w2_ref.shape[0], :] = w2_ref[...]
     out_ref[:size, :] = w1_ref[pl.ds(pl.multiple_of(share * size, size), size), :]
@@ -217,7 +233,10 @@
         latent_ref[...] = came[...]
         norm = normalize(came[...].astype(F32)).astype(BF16)
         queries_ref[...] = dot(norm, w_ref[:, :half]).astype(BF16)
-        send_ref[...] = dot(norm, w_ref[:, half : 2 * half]).astype(BF16)
+        send_ref[: norm.shape[0], :] = dot(norm, w_ref[:, half : 2 * half]).astype(BF16)
+        send_ref[norm.shape[0] :, :] = jnp.zeros(
+            (send_ref.shape[0] - norm.shape[0], half), BF16
+        )
         keys_ref[...] = dot(norm, w_ref[:, 2 * half :]).astype(BF16)
 
     @pl.when(jnp.logical_not(first))
@@ -237,97 +256,107 @@
     out_ref[:, half:] = values_ref[...]
 
 
-def mesh_kernel(
-    index_ref, latent, mine, came, pairs0, keys1, values1, pairs2, wo_ref, keep_ref, send_ref,
-    sums_ref,
-):
+def mesh_attend(sample, times_ref, mine, came, pairs0, keys1, values1, pairs2, wo_ref):
     both, half = mine.shape
     nodes = both // 2
     rows = 3 * both
     heads = HEADS // 2
     per_head = half // heads
+    start = pl.multiple_of(sample * nodes, nodes)
     first = lax.axis_index("dp") == 0
-    queries = jnp.where(first, mine[...], came[...])
+    queries = jnp.where(first, mine[pl.ds(start, nodes), :], came[pl.ds(start, nodes), :])
     keys = jnp.concatenate([pairs0[:, :half], keys1[...], pairs2[:, :half]], axis=0)
     values = jnp.concatenate([pairs0[:, half:], values1[...], pairs2[:, half:]], axis=0)
-    place = side_block(jnp.transpose(index_ref[...]), nodes)
-    near = lax.broadcasted_iota(jnp.int32, (nodes, rows), 1)
-    code = (near // both) * nodes + near % nodes
-    times = sum((place[:, j : j + 1] == code).astype(F32) for j in range(index_ref.shape[0]))
-    second = (near // nodes) % 2
-    times = jnp.concatenate(
-        [jnp.where(second == 0, times, 0.0), jnp.where(second == 1, times, 0.0)], axis=0
-    )[None]
-    head_of = lax.broadcasted_iota(jnp.int32, (both, half), 1) // per_head
+    times = times_ref[pl.ds(start, nodes), :][None]
+    head_of = lax.broadcasted_iota(jnp.int32, (nodes, half), 1) // per_head
     zero = jnp.zeros_like(queries)
     stacked = jnp.concatenate(
         [jnp.where(head_of == h, queries, zero) for h in range(heads)], axis=0
     )
     logits = dot_nt(stacked, keys) * (1.0 / math.sqrt(per_head))
-    logits = logits.reshape(heads, both, rows)
+    logits = logits.reshape(heads, nodes, rows)
     logits = jnp.where(times > 0, logits, -1e30)
     top = jnp.max(logits, axis=-1, keepdims=True)
     weight = times * jnp.exp(logits - top)
     weight = weight / jnp.sum(weight, axis=-1, keepdims=True)
-    mixed = dot(weight.astype(BF16).reshape(heads * both, rows), values)
-    mixed = mixed.reshape(heads, both, half)
+    mixed = dot(weight.astype(BF16).reshape(heads * nodes, rows), values)
+    mixed = mixed.reshape(heads, nodes, half)
     total = jnp.where(head_of == 0, mixed[0], 0.0)
     for h in range(1, heads):
         total = jnp.where(head_of == h, mixed[h], total)
-    sums_ref[...] = dot(total.astype(BF16), wo_ref[...])
+    return dot(total.astype(BF16), wo_ref[...])
+
+
+def send_kernel(
+    times_ref, mine, came, pairs0, keys1, values1, pairs2, wo_ref, send_ref
+):
+    other = 1 - lax.axis_index("dp")
+    projected = mesh_attend(other, times_ref, mine, came, pairs0, keys1, values1, pairs2, wo_ref)
+    send_ref[...] = projected.astype(BF16)
+
+
+def keep_kernel(
+    latent, limit, target, area, times_ref, mine, came, pairs0, keys1, values1, pairs2, wo_ref,
+    keep_ref, weight_ref, base_ref,
+):
+    count_field, slots = target.shape
+    valid = (lax.broadcasted_iota(jnp.int32, (8, slots), 1) < limit[...]).astype(F32)
+    weight = valid * area[...]
+    row = lax.broadcasted_iota(jnp.int32, (8, slots), 0)
+    weight_ref[...] = jnp.where(row == 0, weight, valid)
+    goal = target[...].astype(F32)
+    squares = dot_nt(valid, goal * goal, lax.Precision.HIGHEST)
+    here_count = jnp.broadcast_to(jnp.sum(valid, axis=1, keepdims=True), (8, count_field))
+    here_weight = jnp.broadcast_to(jnp.sum(weight, axis=1, keepdims=True), (8, count_field))
+    row = lax.broadcasted_iota(jnp.int32, (8, count_field), 0)
+    base_ref[...] = jnp.where(row == 1, squares, jnp.where(row == 2, here_count, here_weight))
     ours = lax.axis_index("dp")
-    mine = pl.multiple_of(ours * nodes, nodes)
-    theirs = pl.multiple_of((1 - ours) * nodes, nodes)
-    keep_ref[...] = latent[pl.ds(mine, nodes), :].astype(F32) + sums_ref[pl.ds(mine, nodes), :]
-    send_ref[...] = sums_ref[pl.ds(theirs, nodes), :].astype(BF16)
-
-
-def decode_kernel(index_ref, up0, left, right, up2, w1_ref, w2_ref, norm_ref, part_ref):
-    nodes, width = up0.shape
-    entries, slots = index_ref.shape
-    place = side_block(jnp.transpose(index_ref[...]), nodes)
-    near = lax.broadcasted_iota(jnp.int32, (slots, nodes), 1)
+    nodes = keep_ref.shape[0]
+    projected = mesh_attend(ours, times_ref, mine, came, pairs0, keys1, values1, pairs2, wo_ref)
+    start = pl.multiple_of(ours * nodes, nodes)
+    keep_ref[...] = latent[pl.ds(start, nodes), :].astype(F32) + projected
+
+
+def decode_kernel(
+    entries, counts, up0, left, right, up2, w1_ref, w2_ref, share,
+    part_ref, rest_ref, hidden_ref, norm_ref,
+):
+    nodes = up0.shape[0]
+    up1 = jnp.concatenate([left[...], right[...]], axis=1)
     mean = 0.0
-    up1 = jnp.concatenate([left[...], right[...]], axis=1)
     for i, updated in enumerate((up0[...], up1, up2[...])):
-        times = sum((place[:, k : k + 1] == near + i * nodes).astype(F32) for k in range(entries))
-        mean += dot(times.astype(BF16), updated)
+        mean += dot(counts[:, i * nodes : (i + 1) * nodes], updated)
     norm_ref[...] = normalize(mean * (1.0 / entries)).astype(BF16)
     hidden = silu(dot(norm_ref[...], w1_ref[...])).astype(BF16)
     part_ref[...] = dot_nt(w2_ref[...], hidden)
+    size = hidden_ref.shape[1]
+    core = lax.axis_index("space") % 2
+    here = pl.multiple_of(core * size, size)
+    there = pl.multiple_of((1 - core) * size, size)
+    hidden_ref[...] = dot(norm_ref[:, pl.ds(here, size)], share[:size, :])
+    rest_ref[...] = norm_ref[:, pl.ds(there, size)]
 
 
 def errors_kernel(
-    limit_ref, fields, target, area, norm_ref, part_ref, part0, part1, pred_ref, sums_ref,
-    there_ref,
+    weight_ref, base_ref, fields, target, part_ref, rest_ref, hidden_ref, part0, part1,
+    pred_ref, sums_ref, there_ref,
 ):
     count_field, slots = fields.shape
-    keep = (lax.broadcasted_iota(jnp.int32, (8, slots), 1) < limit_ref[...]).astype(F32)
-    weight = keep * area[...]
     core = lax.axis_index("space") % 2
-    size = norm_ref.shape[1] // 2
+    size = hidden_ref.shape[1]
     tail = part0.shape[0] - size
-    hidden = 0.0
     for i, block in enumerate((part0, part1)):
-        part = pl.multiple_of((core ^ i) * size, size)
-        hidden += dot(norm_ref[:, pl.ds(part, size)], block[:size, :])
         start = pl.multiple_of((core ^ i) * tail, tail)
         there_ref[pl.ds(start, tail), :] = block[size:, :]
-    hidden = silu(hidden).astype(BF16)
+    hidden = silu(hidden_ref[...] + dot(rest_ref[...], part1[:size, :])).astype(BF16)
     increment = part_ref[...] + dot_nt(there_ref[:count_field, :], hidden)
-    valid = keep[:1] > 0
+    valid = weight_ref[1:2, :] > 0
     predicted = jnp.where(valid, fields[...].astype(F32) + increment, 0.0)
     pred_ref[...] = predicted.astype(BF16)
-    goal = target[...].astype(F32)
-    misfit = predicted - goal
-    errors = dot_nt(weight, misfit * misfit, lax.Precision.HIGHEST)
-    squares = dot_nt(keep, goal * goal, lax.Precision.HIGHEST)
-    here_count = jnp.broadcast_to(jnp.sum(keep, axis=1, keepdims=True), (8, count_field))
-    here_weight = jnp.broadcast_to(jnp.sum(weight, axis=1, keepdims=True), (8, count_field))
+    misfit = predicted - target[...].astype(F32)
+    errors = dot_nt(weight_ref[...], misfit * misfit, lax.Precision.HIGHEST)
     row = lax.broadcasted_iota(jnp.int32, (8, count_field), 0)
-    sums = jnp.where(
-        row == 0, errors, jnp.where(row == 1, squares, jnp.where(row == 2, here_count, here_weight))
-    )
+    sums = jnp.where(row == 0, errors, base_ref[...])
     sums_ref[...] = jnp.broadcast_to(sums[None], sums_ref.shape)
 
 
@@ -397,10 +426,14 @@
     )
     other = over_dp(near)
     tail = 16 * pl.cdiv(field_count, 128)
-    (share,) = call(
+    share, times, counts = call(
         share_kernel,
-        (shape((width // 8 + tail, half)),),
-        (after(w_dec1, near), w2),
+        (
+            shape((width // 8 + tail, half)),
+            shape((2 * nodes, 6 * nodes), F32),
+            shape((slots, 3 * nodes)),
+        ),
+        (proc_index.T, dec_index.T, after(w_dec1, near), w2),
         scratch=[pltpu.VMEM((8 * tail, half), BF16)],
         flops=BUSY,
     )
@@ -435,7 +468,12 @@
     values = to_first(send)
     latent, queries, send, keys = call(
         first_kernel,
-        (shape((2 * nodes, width)),) + (shape((2 * nodes, half)),) * 3,
+        (
+            shape((2 * nodes, width)),
+            shape((2 * nodes, half)),
+            shape((2 * nodes + 16, half)),
+            shape((2 * nodes, half)),
+        ),
         (latent, came, w_qkv),
         flops=2 * 2 * nodes * width * 3 * half,
     )
@@ -450,13 +488,16 @@
         (share, came_share),
     )
     came_share = over_quad(share)
-    keep, send = call(
-        mesh_kernel,
-        (shape((nodes, width), F32), shape((nodes, width))),
-        (proc_index.T, latent, queries, to_second(send), pairs, over_pair(keys),
-         over_pair(values), over_link(pairs), w_out),
-        scratch=[pltpu.VMEM((2 * nodes, width), F32)],
-        flops=4 * BUSY,
+    window = (
+        times, queries, to_second(send), pairs, over_pair(keys), over_pair(values),
+        over_link(pairs), w_out,
+    )
+    (send,) = call(send_kernel, (shape((nodes, width)),), window, flops=4 * BUSY)
+    keep, weight, base = call(
+        keep_kernel,
+        (shape((nodes, width), F32), shape((8, slots), F32), shape((8, field_count), F32)),
+        (latent, grid_count[None], goal, area_weight[None]) + window,
+        flops=2 * nodes * width * width,
     )
     (share,) = call(
         functools.partial(join_kernel, 2, 2 * tail),
@@ -472,16 +513,17 @@
     up2 = over_link(updated)
     share = after(share, left, right, up2)
     came_share = over_pair(share)
-    norm, part = call(
-        decode_kernel,
-        (shape((slots, width)), shape((field_count, slots), F32)),
-        (dec_index.T, updated, left, right, up2, w_dec1, w2),
+    part, rest, hidden = call(
+        functools.partial(decode_kernel, dec_index.shape[1]),
+        (shape((field_count, slots), F32), shape((slots, half)), shape((slots, half), F32)),
+        (counts, updated, left, right, up2, w_dec1, w2, share),
+        scratch=[pltpu.VMEM((slots, width), BF16)],
         flops=2 * slots * width * half,
     )
     predicted, sums = call(
         errors_kernel,
         (shape((field_count, slots)), shape((space * samples, 8, field_count), F32)),
-        (grid_count[None], own, goal, area_weight[None], norm, part, share, came_share),
+        (weight, base, own, goal, part, rest, hidden, share, came_share),
         scratch=[pltpu.VMEM((8 * tail, half), BF16)],
         flops=2 * slots * width * half,
     )

time: 62 us -> 62 us (level)
  waiting for transfers between devices: 10.6 us -> 7.36 us
  starting transfers between devices: 25.3 us -> 27.5 us
  Pallas kernels: 9.89 us -> 10.8 us
    ppermute x2, waiting for transfers between devices: 3.94 us -> 1.36 us  [to_second(): return lax.ppermute(x, 'dp', swap)]
    ppermute x6, starting transfers between devices: 7.48 us -> 9.78 us  [over_pair(): return lax.ppermute(x, 'space', pair)]
    ppermute x4, waiting for transfers between devices: 5.53 us -> 4.35 us  [over_dp(): return lax.ppermute(x, 'dp', swap)]
    pallas_call x16 -> x17, Pallas kernels: 9.89 us -> 10.8 us  [call(): pl.pallas_call(kernel, out_shape=tuple(outs), in_specs=[pl.BlockSpec(memo...]
  transfers between devices with their start and end apart: 19 -> 19, of which waited for: 7 -> 9; matrix products, arithmetic and copies ran while one was open for 0% -> 0% of each run, Pallas kernels for 10% -> 11%
where the time goes in v6:
time: 62 us; the launch traced here: 61.6 us
  starting transfers between devices  27.5 us (44%)
  blocking collectives  13.3 us (21%)
  Pallas kernels  10.8 us (17%)
  waiting for transfers between devices  7.36 us (12%)
  between operations  1.53 us (2%)
  local copies, waits for them, and re-layouts  1.21 us (2%)
    all_to_all x1, blocking collectives, small_body(): parts = lax.all_to_all(sums, ('dp', 'space'), 0, 0)  13.3 us
    pallas_call x17, Pallas kernels, call(): pl.pallas_call(kernel, out_shape=tuple(outs), in_specs=[pl.BlockSpec(memo...  10.8 us
    ppermute x6, starting transfers between devices, over_pair(): return lax.ppermute(x, 'space', pair)  9.78 us
    ppermute x4, starting transfers between devices, over_dp(): return lax.ppermute(x, 'dp', swap)  5.84 us
    ppermute x1, starting transfers between devices, small_body(): lax.ppermute(share, 'space', [(i, i ^ 4) for i in range(space)])  5.08 us
    ppermute x4, waiting for transfers between devices, over_dp(): return lax.ppermute(x, 'dp', swap)  4.35 us
    ppermute x2, starting transfers between devices, to_first(): return lax.ppermute(x, 'dp', swap)  2.97 us
    ppermute x3, starting transfers between devices, over_link(): return lax.ppermute(x, 'space', link)  1.98 us
  transfers between devices with their start and end apart: 19, of which 9 were waited for; matrix products, arithmetic and copies ran while one was open for 0% of the time, Pallas kernels for 11%

profile of v6, /device:TPU:0, one launch (start us, length us, event | category | flops | bytes accessed | tf_op | source)
XLA Modules:
  0.0 61.6 jit_solution(14580571102852224916)
XLA Ops:
  1.8 2.6 %collective-permute-start.3 = (bf16[100,512]{1,0:T(8,128)(2,1)}, bf16[100,512]{1,0:T(8,128)(2,1)S(1)}, u32[]{:S(2)}, u32[]{:S(2)}) collective-permute-start(bf16[100,512]{1,0:T(8,128)(2,1)} %we_here.3), channel_id=1, source_target_pairs={{0,16},{16,0},{1,17},{17,1},{2,18},{18,2},{3,19},{19,3},{4,20},{20... | collective-permute-start | bytes 307208 | tf_op jit(solution)/shard_map/ppermute | solution.py:391
  4.4 0.7 %copy-done.10 = s32[32,12]{0,1:T(8,128)S(1)} copy-done((s32[32,12]{0,1:T(8,128)S(1)}, s32[32,12]{0,1:T(8,128)}, u32[]{:S(2)}) %copy-start.10) | copy-done | bytes 1560
  6.2 1.1 %collective-permute-done.3.we_there = bf16[100,512]{1,0:T(8,128)(2,1)S(1)} collective-permute-done((bf16[100,512]{1,0:T(8,128)(2,1)}, bf16[100,512]{1,0:T(8,128)(2,1)S(1)}, u32[]{:S(2)}, u32[]{:S(2)}) %collective-permute-start.3) | collective-permute-done | bytes 102432 | tf_op jit(solution)/shard_map/ppermute | solution.py:391
  7.5 2.1 %shard_map.151 = (bf16[384,1024]{1,0:T(8,128)(2,1)S(1)}, bf16[16,384]{1,0:T(8,128)(2,1)S(1)}) custom-call(bf16[32,1024]{1,0:T(8,128)(2,1)S(1)} %copy-done.5, f32[384,128]{1,0:T(8,128)S(1)} %get-tuple-element.35.present_ref, bf16[100,384]{1,0:T(8,128)(2,1)S(1)} %shard_map.150.near_ref, bf16[100,512]{1,0:T(8,128)(2,1)S(1)} %copy-done.9, ...), custom_call_target="tpu_custom_call" | custom-call | flops 883949568 | bytes 2640896 | tf_op jit(solution)/shard_map/pallas_call | solution.py:44
  9.5 1.0 %collective-permute-done.2.near_ref = bf16[100,384]{1,0:T(8,128)(2,1)S(1)} collective-permute-done((bf16[100,384]{1,0:T(8,128)(2,1)S(1)}, bf16[100,384]{1,0:T(8,128)(2,1)S(1)}, u32[]{:S(2)}, u32[]{:S(2)}) %collective-permute-start.2) | collective-permute-done | bytes 76832 | tf_op jit(solution)/shard_map/ppermute | solution.py:391
  10.6 2.0 %shard_map.152 = (bf16[384,1024]{1,0:T(8,128)(2,1)S(1)}, bf16[16,768]{1,0:T(8,128)(2,1)S(1)}) custom-call(bf16[32,1024]{1,0:T(8,128)(2,1)S(1)} %copy-done.5, f32[384,128]{1,0:T(8,128)S(1)} %get-tuple-element.35.present_ref, bf16[100,384]{1,0:T(8,128)(2,1)S(1)} %collective-permute-done.2.near_ref, bf16[100,512]{1,0:T(8,128)(2,1)S(1)} %copy-done.9, ...), custom_call_target="tpu_custom_call" | custom-call | flops 883949568 | bytes 2653184 | tf_op jit(solution)/shard_map/pallas_call | solution.py:44
  13.1 2.1 %collective-permute-start.15 = (bf16[144,512]{1,0:T(8,128)(2,1)S(1)}, bf16[144,512]{1,0:T(8,128)(2,1)S(1)}, u32[]{:S(2)}, u32[]{:S(2)}) collective-permute-start(bf16[144,512]{1,0:T(8,128)(2,1)S(1)} %get-tuple-element.60), channel_id=1, source_target_pairs={{0,16},{16,0},{1,17},{17,1},{2,18},{18,2},{3,19},{19,3},{4,20},{20... | collective-permute-start | bytes 442376 | tf_op jit(solution)/shard_map/ppermute | solution.py:391
  15.1 1.4 %collective-permute-done.4.probs = bf16[16,768]{1,0:T(8,128)(2,1)S(1)} collective-permute-done((bf16[16,768]{1,0:T(8,128)(2,1)S(1)}, bf16[16,768]{1,0:T(8,128)(2,1)S(1)}, u32[]{:S(2)}, u32[]{:S(2)}) %collective-permute-start.4) | collective-permute-done | bytes 24608 | tf_op jit(solution)/shard_map/ppermute | solution.py:397
  16.5 0.7 %collective-permute-start.5 = (bf16[64,1024]{1,0:T(8,128)(2,1)S(1)}, bf16[64,1024]{1,0:T(8,128)(2,1)S(1)}, u32[]{:S(2)}, u32[]{:S(2)}) collective-permute-start(bf16[64,1024]{1,0:T(8,128)(2,1)S(1)} %shard_map.153.mine.latent), channel_id=1, source_target_pairs={{0,16},{16,0},{1,17},{17,1},{2,18},{18,2},{3,19},{19,3},{4,20},{20... | collective-permute-start | bytes 393224 | tf_op jit(solution)/shard_map/ppermute | solution.py:394
  17.2 2.3 %collective-permute-start.7 = (bf16[64,512]{1,0:T(8,128)(2,1)S(1)}, bf16[64,512]{1,0:T(8,128)(2,1)S(1)}, u32[]{:S(2)}, u32[]{:S(2)}) collective-permute-start(bf16[64,512]{1,0:T(8,128)(2,1)S(1)} %get-tuple-element.48), channel_id=1, source_target_pairs={{0,16},{16,0},{1,17},{17,1},{2,18},{18,2},{3,19},{19,3},{4,20},{20... | collective-permute-start | bytes 196616 | tf_op jit(solution)/shard_map/ppermute | solution.py:394
  19.7 5.1 %collective-permute-start.16 = (bf16[144,512]{1,0:T(8,128)(2,1)S(1)}, bf16[144,512]{1,0:T(8,128)(2,1)S(1)}, u32[]{:S(2)}, u32[]{:S(2)}) collective-permute-start(bf16[144,512]{1,0:T(8,128)(2,1)S(1)} %collective-permute-done.15.mine), channel_id=1, source_target_pairs={{0,4},{1,5},{2,6},{3,7},{4,0},{5,1},{6,2},{7,3},{8,12},{9,13},{10,... | collective-permute-start | bytes 442376 | tf_op jit(solution)/shard_map/ppermute | solution.py:461
  24.8 0.8 %shard_map.154 = (bf16[64,1024]{1,0:T(8,128)(2,1)S(1)}, bf16[64,512]{1,0:T(8,128)(2,1)S(1)}, bf16[80,512]{1,0:T(8,128)(2,1)S(1)}, bf16[64,512]{1,0:T(8,128)(2,1)S(1)}) custom-call(bf16[64,1024]{1,0:T(8,128)(2,1)S(1)} %shard_map.153.mine.latent, bf16[64,1024]{1,0:T(8,128)(2,1)S(1)} %collective-permute-done.5.came, bf16[1024,1536]{1,0:T(8,128)(2,1)S(1)} %copy-done), custom_call_target="tpu_custom_call" | custom-call | flops 201326592 | bytes 3407872 | tf_op jit(solution)/shard_map/pallas_call | solution.py:44
  26.4 0.7 %collective-permute-start.6 = (bf16[80,512]{1,0:T(8,128)(2,1)S(1)}, bf16[80,512]{1,0:T(8,128)(2,1)S(1)}, u32[]{:S(2)}, u32[]{:S(2)}) collective-permute-start(bf16[80,512]{1,0:T(8,128)(2,1)S(1)} %get-tuple-element.45), channel_id=1, source_target_pairs={{0,16},{16,0},{1,17},{17,1},{2,18},{18,2},{3,19},{19,3},{4,20},{20... | collective-permute-start | bytes 245768 | tf_op jit(solution)/shard_map/ppermute | solution.py:397
  27.1 3.6 %collective-permute-start.8 = (bf16[64,512]{1,0:T(8,128)(2,1)S(1)}, bf16[64,512]{1,0:T(8,128)(2,1)S(1)}, u32[]{:S(2)}, u32[]{:S(2)}) collective-permute-start(bf16[64,512]{1,0:T(8,128)(2,1)S(1)} %get-tuple-element.50), channel_id=1, source_target_pairs={{0,1},{1,0},{2,3},{3,2},{4,5},{5,4},{6,7},{7,6},{8,9},{9,8},{10,11... | collective-permute-start | bytes 196616 | tf_op jit(solution)/shard_map/ppermute | solution.py:400
  30.8 1.1 %collective-permute-start.17 = (bf16[288,512]{1,0:T(8,128)(2,1)S(1)}, bf16[288,512]{1,0:T(8,128)(2,1)S(1)}, u32[]{:S(2)}, u32[]{:S(2)}) collective-permute-start(bf16[288,512]{1,0:T(8,128)(2,1)S(1)} %shard_map.161.mine), channel_id=1, source_target_pairs={{0,2},{1,3},{2,0},{3,1},{4,6},{5,7},{6,4},{7,5},{8,10},{9,11},{10,... | collective-permute-start | bytes 884744 | tf_op jit(solution)/shard_map/ppermute | solution.py:410
  32.0 0.9 %shard_map.159 = bf16[32,1024]{1,0:T(8,128)(2,1)S(1)} custom-call(f32[64,192]{1,0:T(8,128)S(1)} %get-tuple-element.43.times_ref, bf16[64,512]{1,0:T(8,128)(2,1)S(1)} %get-tuple-element.44.mine, bf16[80,512]{1,0:T(8,128)(2,1)S(1)} %collective-permute-done.6.came, bf16[64,1024]{1,0:T(8,128)(2,1)S(1)} %get-tuple-element.49.pairs0, ...), custom_call_target="tpu_custom_call" | custom-call | flops 16000000000 | bytes 1638400 | tf_op jit(solution)/shard_map/pallas_call | solution.py:44
  32.9 1.1 %collective-permute-start.11 = (bf16[32,1024]{1,0:T(8,128)(2,1)S(1)}, bf16[32,1024]{1,0:T(8,128)(2,1)S(1)}, u32[]{:S(2)}, u32[]{:S(2)}) collective-permute-start(bf16[32,1024]{1,0:T(8,128)(2,1)S(1)} %shard_map.159), channel_id=1, source_target_pairs={{0,16},{16,0},{1,17},{17,1},{2,18},{18,2},{3,19},{19,3},{4,20},{20... | collective-permute-start | bytes 196616 | tf_op jit(solution)/shard_map/ppermute | solution.py:391
  34.7 0.9 %shard_map.158 = (f32[32,1024]{1,0:T(8,128)S(1)}, f32[8,128]{1,0:T(8,128)S(1)}, f32[8,100]{1,0:T(8,128)S(1)}) custom-call(bf16[64,1024]{1,0:T(8,128)(2,1)S(1)} %get-tuple-element.41.latent, s32[1,1]{1,0:T(1,128)} %bitcast.16.limit, bf16[100,128]{1,0:T(8,128)(2,1)S(1)} %bitcast.19, f32[1,128]{1,0:T(1,128)S(1)} %bitcast.25, ...), custom_call_target="tpu_custom_call" | custom-call | flops 67108864 | bytes 1795588 | tf_op jit(solution)/shard_map/pallas_call | solution.py:44
  35.6 2.0 %collective-permute-done.11.theirs = bf16[32,1024]{1,0:T(8,128)(2,1)S(1)} collective-permute-done((bf16[32,1024]{1,0:T(8,128)(2,1)S(1)}, bf16[32,1024]{1,0:T(8,128)(2,1)S(1)}, u32[]{:S(2)}, u32[]{:S(2)}) %collective-permute-start.11) | collective-permute-done | bytes 65568 | tf_op jit(solution)/shard_map/ppermute | solution.py:391
  38.3 4.9 %collective-permute-start.12 = (bf16[32,512]{1,0:T(8,128)(2,1)S(1)}, bf16[32,512]{1,0:T(8,128)(2,1)S(1)}, u32[]{:S(2)}, u32[]{:S(2)}) collective-permute-start(bf16[32,512]{1,0:T(8,128)(2,1)S(1)} %get-tuple-element.57), channel_id=1, source_target_pairs={{0,1},{1,0},{2,3},{3,2},{4,5},{5,4},{6,7},{7,6},{8,9},{9,8},{10,11... | collective-permute-start | bytes 98312 | tf_op jit(solution)/shard_map/ppermute | solution.py:400
  43.3 0.7 %collective-permute-done.12.left = bf16[32,512]{1,0:T(8,128)(2,1)S(1)} collective-permute-done((bf16[32,512]{1,0:T(8,128)(2,1)S(1)}, bf16[32,512]{1,0:T(8,128)(2,1)S(1)}, u32[]{:S(2)}, u32[]{:S(2)}) %collective-permute-start.12) | collective-permute-done | bytes 32800 | tf_op jit(solution)/shard_map/ppermute | solution.py:400
  45.0 1.2 %shard_map.163 = (f32[100,128]{1,0:T(8,128)S(1)}, bf16[128,512]{1,0:T(8,128)(2,1)S(1)}, f32[128,512]{1,0:T(8,128)S(1)}) custom-call(bf16[128,96]{1,0:T(8,128)(2,1)S(1)} %get-tuple-element.54.counts, bf16[32,1024]{1,0:T(8,128)(2,1)S(1)} %get-tuple-element.56.up0, bf16[32,512]{1,0:T(8,128)(2,1)S(1)} %collective-permute-done.12.left, ...), custom_call_target="tpu_custom_call" | custom-call | flops 134217728 | bytes 1961984 | tf_op jit(solution)/shard_map/pallas_call | solution.py:44
  46.7 1.1 %shard_map.164 = (bf16[100,128]{1,0:T(8,128)(2,1)}, f32[32,8,100]{2,1,0:T(8,128)S(1)}) custom-call(f32[8,128]{1,0:T(8,128)S(1)} %get-tuple-element.52.weight_ref, f32[8,100]{1,0:T(8,128)S(1)} %get-tuple-element.53.base_ref, bf16[100,128]{1,0:T(8,128)(2,1)S(1)} %bitcast.24, bf16[100,128]{1,0:T(8,128)(2,1)S(1)} %bitcast.20, ...), custom_call_target="tpu_custom_call" | custom-call | flops 134217728 | bytes 1682560 | tf_op jit(solution)/shard_map/pallas_call | solution.py:44
  47.7 13.3 %all_to_all.5.parts = f32[32,8,100]{2,1,0:T(8,128)S(1)} all-to-all(f32[32,8,100]{2,1,0:T(8,128)S(1)} %get-tuple-element.67), channel_id=1, replica_groups=mesh['dp'=2,'space'=16] {'dp','space'}, dimensions={0} | all-to-all | bytes 204800 | tf_op jit(solution)/shard_map/all_to_all | solution.py:530
  (58 shorter events, 6.9 us)
Async XLA Ops:
  0.6 4.9 %collective-permute-start = (bf16[100,128]{1,0:T(8,128)(2,1)}, bf16[100,128]{1,0:T(8,128)(2,1)S(1)}, u32[]{:S(2)}, u32[]{:S(2)}) collective-permute-start(bf16[100,128]{1,0:T(8,128)(2,1)} %bitcast.21), channel_id=1, source_target_pairs={{0,1},{1,0},{2,3},{3,2},{4,5},{5,4},{6,7},{7,6},{8,9},{9,8},{10,11... | collective-permute-start | bytes 76808 | tf_op jit(solution)/shard_map/ppermute | solution.py:400
  1.1 4.4 %collective-permute-start.1 = (bf16[100,128]{1,0:T(8,128)(2,1)}, bf16[100,128]{1,0:T(8,128)(2,1)S(1)}, u32[]{:S(2)}, u32[]{:S(2)}) collective-permute-start(bf16[100,128]{1,0:T(8,128)(2,1)} %bitcast.22), channel_id=1, source_target_pairs={{1,2},{3,4},{5,6},{7,8},{9,10},{11,12},{13,14},{2,1},{4,3},{6,5},{... | collective-permute-start | bytes 76808 | tf_op jit(solution)/shard_map/ppermute | solution.py:403
  1.8 5.5 %collective-permute-start.3 = (bf16[100,512]{1,0:T(8,128)(2,1)}, bf16[100,512]{1,0:T(8,128)(2,1)S(1)}, u32[]{:S(2)}, u32[]{:S(2)}) collective-permute-start(bf16[100,512]{1,0:T(8,128)(2,1)} %we_here.3), channel_id=1, source_target_pairs={{0,16},{16,0},{1,17},{17,1},{2,18},{18,2},{3,19},{19,3},{4,20},{20... | collective-permute-start | bytes 307208 | tf_op jit(solution)/shard_map/ppermute | solution.py:391
  6.1 4.5 %collective-permute-start.2 = (bf16[100,384]{1,0:T(8,128)(2,1)S(1)}, bf16[100,384]{1,0:T(8,128)(2,1)S(1)}, u32[]{:S(2)}, u32[]{:S(2)}) collective-permute-start(bf16[100,384]{1,0:T(8,128)(2,1)S(1)} %shard_map.150.near_ref), channel_id=1, source_target_pairs={{0,16},{16,0},{1,17},{17,1},{2,18},{18,2},{3,19},{19,3},{4,20},{20... | collective-permute-start | bytes 230408 | tf_op jit(solution)/shard_map/ppermute | solution.py:391
  7.5 5.2 %copy-start.2 = (bf16[1024,512]{1,0:T(8,128)(2,1)S(1)}, bf16[1024,512]{1,0:T(8,128)(2,1)}, u32[]{:S(2)}) copy-start(bf16[1024,512]{1,0:T(8,128)(2,1)} %w1_ref.2) | copy-start | bytes 3145732
  7.5 5.2 %copy-start.3 = (bf16[512,100]{0,1:T(8,128)(2,1)S(1)}, bf16[512,100]{0,1:T(8,128)(2,1)}, u32[]{:S(2)}) copy-start(bf16[512,100]{0,1:T(8,128)(2,1)} %param.27) | copy-start | bytes 307204
  7.5 5.2 %copy-start.11 = (s32[32,16]{0,1:T(8,128)S(1)}, s32[32,16]{0,1:T(8,128)}, u32[]{:S(2)}) copy-start(s32[32,16]{0,1:T(8,128)} %param.20) | copy-start | bytes 6148
  7.5 5.2 %copy-start.12 = (s32[128,3]{0,1:T(4,128)S(1)}, s32[128,3]{0,1:T(4,128)}, u32[]{:S(2)}) copy-start(s32[128,3]{0,1:T(4,128)} %param.21) | copy-start | bytes 4612
  12.6 3.9 %collective-permute-start.4 = (bf16[16,768]{1,0:T(8,128)(2,1)S(1)}, bf16[16,768]{1,0:T(8,128)(2,1)S(1)}, u32[]{:S(2)}, u32[]{:S(2)}) collective-permute-start(bf16[16,768]{1,0:T(8,128)(2,1)S(1)} %get-tuple-element.38), channel_id=1, source_target_pairs={{0,16},{16,0},{1,17},{17,1},{2,18},{18,2},{3,19},{19,3},{4,20},{20... | collective-permute-start | bytes 73736 | tf_op jit(solution)/shard_map/ppermute | solution.py:397
  13.1 6.7 %collective-permute-start.15 = (bf16[144,512]{1,0:T(8,128)(2,1)S(1)}, bf16[144,512]{1,0:T(8,128)(2,1)S(1)}, u32[]{:S(2)}, u32[]{:S(2)}) collective-permute-start(bf16[144,512]{1,0:T(8,128)(2,1)S(1)} %get-tuple-element.60), channel_id=1, source_target_pairs={{0,16},{16,0},{1,17},{17,1},{2,18},{18,2},{3,19},{19,3},{4,20},{20... | collective-permute-start | bytes 442376 | tf_op jit(solution)/shard_map/ppermute | solution.py:391
  16.5 15.5 %copy-start.1 = (bf16[512,1024]{1,0:T(8,128)(2,1)S(1)}, bf16[512,1024]{1,0:T(8,128)(2,1)}, u32[]{:S(2)}) copy-start(bf16[512,1024]{1,0:T(8,128)(2,1)} %wo_ref.3) | copy-start | bytes 3145732
  16.5 8.3 %collective-permute-start.5 = (bf16[64,1024]{1,0:T(8,128)(2,1)S(1)}, bf16[64,1024]{1,0:T(8,128)(2,1)S(1)}, u32[]{:S(2)}, u32[]{:S(2)}) collective-permute-start(bf16[64,1024]{1,0:T(8,128)(2,1)S(1)} %shard_map.153.mine.latent), channel_id=1, source_target_pairs={{0,16},{16,0},{1,17},{17,1},{2,18},{18,2},{3,19},{19,3},{4,20},{20... | collective-permute-start | bytes 393224 | tf_op jit(solution)/shard_map/ppermute | solution.py:394
  17.2 8.4 %collective-permute-start.7 = (bf16[64,512]{1,0:T(8,128)(2,1)S(1)}, bf16[64,512]{1,0:T(8,128)(2,1)S(1)}, u32[]{:S(2)}, u32[]{:S(2)}) collective-permute-start(bf16[64,512]{1,0:T(8,128)(2,1)S(1)} %get-tuple-element.48), channel_id=1, source_target_pairs={{0,16},{16,0},{1,17},{17,1},{2,18},{18,2},{3,19},{19,3},{4,20},{20... | collective-permute-start | bytes 196616 | tf_op jit(solution)/shard_map/ppermute | solution.py:394
  19.7 11.0 %collective-permute-start.16 = (bf16[144,512]{1,0:T(8,128)(2,1)S(1)}, bf16[144,512]{1,0:T(8,128)(2,1)S(1)}, u32[]{:S(2)}, u32[]{:S(2)}) collective-permute-start(bf16[144,512]{1,0:T(8,128)(2,1)S(1)} %collective-permute-done.15.mine), channel_id=1, source_target_pairs={{0,4},{1,5},{2,6},{3,7},{4,0},{5,1},{6,2},{7,3},{8,12},{9,13},{10,... | collective-permute-start | bytes 442376 | tf_op jit(solution)/shard_map/ppermute | solution.py:461
  25.7 6.3 %collective-permute-start.10 = (bf16[64,1024]{1,0:T(8,128)(2,1)S(1)}, bf16[64,1024]{1,0:T(8,128)(2,1)S(1)}, u32[]{:S(2)}, u32[]{:S(2)}) collective-permute-start(bf16[64,1024]{1,0:T(8,128)(2,1)S(1)} %get-tuple-element.49.pairs0), channel_id=1, source_target_pairs={{1,2},{3,4},{5,6},{7,8},{9,10},{11,12},{13,14},{2,1},{4,3},{6,5},{... | collective-permute-start | bytes 393224 | tf_op jit(solution)/shard_map/ppermute | solution.py:403
  26.4 5.6 %collective-permute-start.6 = (bf16[80,512]{1,0:T(8,128)(2,1)S(1)}, bf16[80,512]{1,0:T(8,128)(2,1)S(1)}, u32[]{:S(2)}, u32[]{:S(2)}) collective-permute-start(bf16[80,512]{1,0:T(8,128)(2,1)S(1)} %get-tuple-element.45), channel_id=1, source_target_pairs={{0,16},{16,0},{1,17},{17,1},{2,18},{18,2},{3,19},{19,3},{4,20},{20... | collective-permute-start | bytes 245768 | tf_op jit(solution)/shard_map/ppermute | solution.py:397
  27.1 4.8 %collective-permute-start.8 = (bf16[64,512]{1,0:T(8,128)(2,1)S(1)}, bf16[64,512]{1,0:T(8,128)(2,1)S(1)}, u32[]{:S(2)}, u32[]{:S(2)}) collective-permute-start(bf16[64,512]{1,0:T(8,128)(2,1)S(1)} %get-tuple-element.50), channel_id=1, source_target_pairs={{0,1},{1,0},{2,3},{3,2},{4,5},{5,4},{6,7},{7,6},{8,9},{9,8},{10,11... | collective-permute-start | bytes 196616 | tf_op jit(solution)/shard_map/ppermute | solution.py:400
  30.7 1.3 %collective-permute-start.9 = (bf16[64,512]{1,0:T(8,128)(2,1)S(1)}, bf16[64,512]{1,0:T(8,128)(2,1)S(1)}, u32[]{:S(2)}, u32[]{:S(2)}) collective-permute-start(bf16[64,512]{1,0:T(8,128)(2,1)S(1)} %get-tuple-element.51), channel_id=1, source_target_pairs={{0,1},{1,0},{2,3},{3,2},{4,5},{5,4},{6,7},{7,6},{8,9},{9,8},{10,11... | collective-permute-start | bytes 196616 | tf_op jit(solution)/shard_map/ppermute | solution.py:400
  30.8 12.5 %collective-permute-start.17 = (bf16[288,512]{1,0:T(8,128)(2,1)S(1)}, bf16[288,512]{1,0:T(8,128)(2,1)S(1)}, u32[]{:S(2)}, u32[]{:S(2)}) collective-permute-start(bf16[288,512]{1,0:T(8,128)(2,1)S(1)} %shard_map.161.mine), channel_id=1, source_target_pairs={{0,2},{1,3},{2,0},{3,1},{4,6},{5,7},{6,4},{7,5},{8,10},{9,11},{10,... | collective-permute-start | bytes 884744 | tf_op jit(solution)/shard_map/ppermute | solution.py:410
  32.9 4.7 %collective-permute-start.11 = (bf16[32,1024]{1,0:T(8,128)(2,1)S(1)}, bf16[32,1024]{1,0:T(8,128)(2,1)S(1)}, u32[]{:S(2)}, u32[]{:S(2)}) collective-permute-start(bf16[32,1024]{1,0:T(8,128)(2,1)S(1)} %shard_map.159), channel_id=1, source_target_pairs={{0,16},{16,0},{1,17},{17,1},{2,18},{18,2},{3,19},{19,3},{4,20},{20... | collective-permute-start | bytes 196616 | tf_op jit(solution)/shard_map/ppermute | solution.py:391
  37.6 6.8 %collective-permute-start.14 = (bf16[32,1024]{1,0:T(8,128)(2,1)S(1)}, bf16[32,1024]{1,0:T(8,128)(2,1)S(1)}, u32[]{:S(2)}, u32[]{:S(2)}) collective-permute-start(bf16[32,1024]{1,0:T(8,128)(2,1)S(1)} %get-tuple-element.56.up0), channel_id=1, source_target_pairs={{1,2},{3,4},{5,6},{7,8},{9,10},{11,12},{13,14},{2,1},{4,3},{6,5},{... | collective-permute-start | bytes 196616 | tf_op jit(solution)/shard_map/ppermute | solution.py:403
  38.3 5.8 %collective-permute-start.12 = (bf16[32,512]{1,0:T(8,128)(2,1)S(1)}, bf16[32,512]{1,0:T(8,128)(2,1)S(1)}, u32[]{:S(2)}, u32[]{:S(2)}) collective-permute-start(bf16[32,512]{1,0:T(8,128)(2,1)S(1)} %get-tuple-element.57), channel_id=1, source_target_pairs={{0,1},{1,0},{2,3},{3,2},{4,5},{5,4},{6,7},{7,6},{8,9},{9,8},{10,11... | collective-permute-start | bytes 98312 | tf_op jit(solution)/shard_map/ppermute | solution.py:400
  43.2 1.2 %collective-permute-start.13 = (bf16[32,512]{1,0:T(8,128)(2,1)S(1)}, bf16[32,512]{1,0:T(8,128)(2,1)S(1)}, u32[]{:S(2)}, u32[]{:S(2)}) collective-permute-start(bf16[32,512]{1,0:T(8,128)(2,1)S(1)} %get-tuple-element.58), channel_id=1, source_target_pairs={{0,1},{1,0},{2,3},{3,2},{4,5},{5,4},{6,7},{7,6},{8,9},{9,8},{10,11... | collective-permute-start | bytes 98312 | tf_op jit(solution)/shard_map/ppermute | solution.py:400
  44.4 2.3 %collective-permute-start.18 = (bf16[576,512]{1,0:T(8,128)(2,1)S(1)}, bf16[576,512]{1,0:T(8,128)(2,1)S(1)}, u32[]{:S(2)}, u32[]{:S(2)}) collective-permute-start(bf16[576,512]{1,0:T(8,128)(2,1)S(1)} %shard_map.162.share.part0), channel_id=1, source_target_pairs={{0,1},{1,0},{2,3},{3,2},{4,5},{5,4},{6,7},{7,6},{8,9},{9,8},{10,11... | collective-permute-start | bytes 1769480 | tf_op jit(solution)/shard_map/ppermute | solution.py:400
  (8 other events, 16.1 us)

commit v7 on v6

--- a/solution.py
+++ b/solution.py
@@ -83,10 +83,10 @@
 
 
 def share_kernel(
-    proc_ref, dec_ref, w1_ref, w2_ref, out_ref, times_ref, counts_ref, pad_ref
+    proc_ref, dec_ref, w1_ref, w2_ref, out_ref, times_ref, counts_ref
 ):
     size = w1_ref.shape[0] // 8
-    tail = pad_ref.shape[0] // 8
+    tail = out_ref.shape[0] - size
     spot = lax.axis_index("space")
     share = (spot % 2) * 4 + ((spot // 2) % 2) * 2 + (spot // 4) % 2
     both, rows = times_ref.shape
@@ -103,10 +103,11 @@
     near = lax.broadcasted_iota(jnp.int32, (slots, rows), 1)
     counts = sum((place[:, k : k + 1] == near).astype(F32) for k in range(dec_ref.shape[0]))
     counts_ref[...] = counts.astype(BF16)
-    pad_ref[...] = jnp.zeros(pad_ref.shape, BF16)
-    pad_ref[: w2_ref.shape[0], :] = w2_ref[...]
     out_ref[:size, :] = w1_ref[pl.ds(pl.multiple_of(share * size, size), size), :]
-    out_ref[size:, :] = pad_ref[pl.ds(pl.multiple_of(share * tail, tail), tail), :]
+    count_field = w2_ref.shape[0]
+    row = lax.broadcasted_iota(jnp.int32, (tail, count_field), 0) + share * tail
+    which = row == lax.broadcasted_iota(jnp.int32, (tail, count_field), 1)
+    out_ref[size:, :] = dot(which.astype(BF16), w2_ref[...]).astype(BF16)
 
 
 def join_kernel(step, tail, mine, theirs, out_ref):
@@ -349,7 +350,7 @@
         start = pl.multiple_of((core ^ i) * tail, tail)
         there_ref[pl.ds(start, tail), :] = block[size:, :]
     hidden = silu(hidden_ref[...] + dot(rest_ref[...], part1[:size, :])).astype(BF16)
-    increment = part_ref[...] + dot_nt(there_ref[:count_field, :], hidden)
+    increment = part_ref[...] + dot_nt(there_ref[...], hidden)[:count_field]
     valid = weight_ref[1:2, :] > 0
     predicted = jnp.where(valid, fields[...].astype(F32) + increment, 0.0)
     pred_ref[...] = predicted.astype(BF16)
@@ -434,7 +435,6 @@
             shape((slots, 3 * nodes)),
         ),
         (proc_index.T, dec_index.T, after(w_dec1, near), w2),
-        scratch=[pltpu.VMEM((8 * tail, half), BF16)],
         flops=BUSY,
     )
     pairs_own, probs = call(

time: 62 us -> 62 us (level)
  no operation moved by 1% of the time
where the time goes in v7:
time: 62 us; the launch traced here: 61.6 us
  starting transfers between devices  27.5 us (44%)
  blocking collectives  13.3 us (21%)
  Pallas kernels  10.8 us (17%)
  waiting for transfers between devices  7.36 us (12%)
  between operations  1.53 us (2%)
  local copies, waits for them, and re-layouts  1.21 us (2%)
    all_to_all x1, blocking collectives, small_body(): parts = lax.all_to_all(sums, ('dp', 'space'), 0, 0)  13.3 us
    pallas_call x17, Pallas kernels, call(): pl.pallas_call(kernel, out_shape=tuple(outs), in_specs=[pl.BlockSpec(memo...  10.8 us
    ppermute x6, starting transfers between devices, over_pair(): return lax.ppermute(x, 'space', pair)  9.77 us
    ppermute x4, starting transfers between devices, over_dp(): return lax.ppermute(x, 'dp', swap)  5.84 us
    ppermute x1, starting transfers between devices, small_body(): lax.ppermute(share, 'space', [(i, i ^ 4) for i in range(space)])  5.08 us
    ppermute x4, waiting for transfers between devices, over_dp(): return lax.ppermute(x, 'dp', swap)  4.35 us
    ppermute x2, starting transfers between devices, to_first(): return lax.ppermute(x, 'dp', swap)  2.97 us
    ppermute x3, starting transfers between devices, over_link(): return lax.ppermute(x, 'space', link)  1.98 us
  transfers between devices with their start and end apart: 19, of which 9 were waited for; matrix products, arithmetic and copies ran while one was open for 0% of the time, Pallas kernels for 11%

profile of v7, /device:TPU:0, one launch (start us, length us, event | category | flops | bytes accessed | tf_op | source)
XLA Modules:
  0.0 61.6 jit_solution(15151111314647752635)
XLA Ops:
  1.8 2.6 %collective-permute-start.3 = (bf16[100,512]{1,0:T(8,128)(2,1)}, bf16[100,512]{1,0:T(8,128)(2,1)S(1)}, u32[]{:S(2)}, u32[]{:S(2)}) collective-permute-start(bf16[100,512]{1,0:T(8,128)(2,1)} %we_here.3), channel_id=1, source_target_pairs={{0,16},{16,0},{1,17},{17,1},{2,18},{18,2},{3,19},{19,3},{4,20},{20... | collective-permute-start | bytes 307208 | tf_op jit(solution)/shard_map/ppermute | solution.py:392
  4.4 0.7 %copy-done.10 = s32[32,12]{0,1:T(8,128)S(1)} copy-done((s32[32,12]{0,1:T(8,128)S(1)}, s32[32,12]{0,1:T(8,128)}, u32[]{:S(2)}) %copy-start.10) | copy-done | bytes 1560
  6.2 1.1 %collective-permute-done.3.we_there = bf16[100,512]{1,0:T(8,128)(2,1)S(1)} collective-permute-done((bf16[100,512]{1,0:T(8,128)(2,1)}, bf16[100,512]{1,0:T(8,128)(2,1)S(1)}, u32[]{:S(2)}, u32[]{:S(2)}) %collective-permute-start.3) | collective-permute-done | bytes 102432 | tf_op jit(solution)/shard_map/ppermute | solution.py:392
  7.5 2.1 %shard_map.151 = (bf16[384,1024]{1,0:T(8,128)(2,1)S(1)}, bf16[16,384]{1,0:T(8,128)(2,1)S(1)}) custom-call(bf16[32,1024]{1,0:T(8,128)(2,1)S(1)} %copy-done.5, f32[384,128]{1,0:T(8,128)S(1)} %get-tuple-element.35.present_ref, bf16[100,384]{1,0:T(8,128)(2,1)S(1)} %shard_map.150.near_ref, bf16[100,512]{1,0:T(8,128)(2,1)S(1)} %copy-done.9, ...), custom_call_target="tpu_custom_call" | custom-call | flops 883949568 | bytes 2640896 | tf_op jit(solution)/shard_map/pallas_call | solution.py:44
  9.5 1.0 %collective-permute-done.2.near_ref = bf16[100,384]{1,0:T(8,128)(2,1)S(1)} collective-permute-done((bf16[100,384]{1,0:T(8,128)(2,1)S(1)}, bf16[100,384]{1,0:T(8,128)(2,1)S(1)}, u32[]{:S(2)}, u32[]{:S(2)}) %collective-permute-start.2) | collective-permute-done | bytes 76832 | tf_op jit(solution)/shard_map/ppermute | solution.py:392
  10.6 2.0 %shard_map.152 = (bf16[384,1024]{1,0:T(8,128)(2,1)S(1)}, bf16[16,768]{1,0:T(8,128)(2,1)S(1)}) custom-call(bf16[32,1024]{1,0:T(8,128)(2,1)S(1)} %copy-done.5, f32[384,128]{1,0:T(8,128)S(1)} %get-tuple-element.35.present_ref, bf16[100,384]{1,0:T(8,128)(2,1)S(1)} %collective-permute-done.2.near_ref, bf16[100,512]{1,0:T(8,128)(2,1)S(1)} %copy-done.9, ...), custom_call_target="tpu_custom_call" | custom-call | flops 883949568 | bytes 2653184 | tf_op jit(solution)/shard_map/pallas_call | solution.py:44
  13.1 2.1 %collective-permute-start.15 = (bf16[144,512]{1,0:T(8,128)(2,1)S(1)}, bf16[144,512]{1,0:T(8,128)(2,1)S(1)}, u32[]{:S(2)}, u32[]{:S(2)}) collective-permute-start(bf16[144,512]{1,0:T(8,128)(2,1)S(1)} %get-tuple-element.60), channel_id=1, source_target_pairs={{0,16},{16,0},{1,17},{17,1},{2,18},{18,2},{3,19},{19,3},{4,20},{20... | collective-permute-start | bytes 442376 | tf_op jit(solution)/shard_map/ppermute | solution.py:392
  15.1 1.4 %collective-permute-done.4.probs = bf16[16,768]{1,0:T(8,128)(2,1)S(1)} collective-permute-done((bf16[16,768]{1,0:T(8,128)(2,1)S(1)}, bf16[16,768]{1,0:T(8,128)(2,1)S(1)}, u32[]{:S(2)}, u32[]{:S(2)}) %collective-permute-start.4) | collective-permute-done | bytes 24608 | tf_op jit(solution)/shard_map/ppermute | solution.py:398
  16.5 0.7 %collective-permute-start.5 = (bf16[64,1024]{1,0:T(8,128)(2,1)S(1)}, bf16[64,1024]{1,0:T(8,128)(2,1)S(1)}, u32[]{:S(2)}, u32[]{:S(2)}) collective-permute-start(bf16[64,1024]{1,0:T(8,128)(2,1)S(1)} %shard_map.153.mine.latent), channel_id=1, source_target_pairs={{0,16},{16,0},{1,17},{17,1},{2,18},{18,2},{3,19},{19,3},{4,20},{20... | collective-permute-start | bytes 393224 | tf_op jit(solution)/shard_map/ppermute | solution.py:395
  17.2 2.3 %collective-permute-start.7 = (bf16[64,512]{1,0:T(8,128)(2,1)S(1)}, bf16[64,512]{1,0:T(8,128)(2,1)S(1)}, u32[]{:S(2)}, u32[]{:S(2)}) collective-permute-start(bf16[64,512]{1,0:T(8,128)(2,1)S(1)} %get-tuple-element.48), channel_id=1, source_target_pairs={{0,16},{16,0},{1,17},{17,1},{2,18},{18,2},{3,19},{19,3},{4,20},{20... | collective-permute-start | bytes 196616 | tf_op jit(solution)/shard_map/ppermute | solution.py:395
  19.7 5.1 %collective-permute-start.16 = (bf16[144,512]{1,0:T(8,128)(2,1)S(1)}, bf16[144,512]{1,0:T(8,128)(2,1)S(1)}, u32[]{:S(2)}, u32[]{:S(2)}) collective-permute-start(bf16[144,512]{1,0:T(8,128)(2,1)S(1)} %collective-permute-done.15.mine), channel_id=1, source_target_pairs={{0,4},{1,5},{2,6},{3,7},{4,0},{5,1},{6,2},{7,3},{8,12},{9,13},{10,... | collective-permute-start | bytes 442376 | tf_op jit(solution)/shard_map/ppermute | solution.py:461
  24.8 0.8 %shard_map.154 = (bf16[64,1024]{1,0:T(8,128)(2,1)S(1)}, bf16[64,512]{1,0:T(8,128)(2,1)S(1)}, bf16[80,512]{1,0:T(8,128)(2,1)S(1)}, bf16[64,512]{1,0:T(8,128)(2,1)S(1)}) custom-call(bf16[64,1024]{1,0:T(8,128)(2,1)S(1)} %shard_map.153.mine.latent, bf16[64,1024]{1,0:T(8,128)(2,1)S(1)} %collective-permute-done.5.came, bf16[1024,1536]{1,0:T(8,128)(2,1)S(1)} %copy-done), custom_call_target="tpu_custom_call" | custom-call | flops 201326592 | bytes 3407872 | tf_op jit(solution)/shard_map/pallas_call | solution.py:44
  26.4 0.7 %collective-permute-start.6 = (bf16[80,512]{1,0:T(8,128)(2,1)S(1)}, bf16[80,512]{1,0:T(8,128)(2,1)S(1)}, u32[]{:S(2)}, u32[]{:S(2)}) collective-permute-start(bf16[80,512]{1,0:T(8,128)(2,1)S(1)} %get-tuple-element.45), channel_id=1, source_target_pairs={{0,16},{16,0},{1,17},{17,1},{2,18},{18,2},{3,19},{19,3},{4,20},{20... | collective-permute-start | bytes 245768 | tf_op jit(solution)/shard_map/ppermute | solution.py:398
  27.1 3.6 %collective-permute-start.8 = (bf16[64,512]{1,0:T(8,128)(2,1)S(1)}, bf16[64,512]{1,0:T(8,128)(2,1)S(1)}, u32[]{:S(2)}, u32[]{:S(2)}) collective-permute-start(bf16[64,512]{1,0:T(8,128)(2,1)S(1)} %get-tuple-element.50), channel_id=1, source_target_pairs={{0,1},{1,0},{2,3},{3,2},{4,5},{5,4},{6,7},{7,6},{8,9},{9,8},{10,11... | collective-permute-start | bytes 196616 | tf_op jit(solution)/shard_map/ppermute | solution.py:401
  30.8 1.1 %collective-permute-start.17 = (bf16[288,512]{1,0:T(8,128)(2,1)S(1)}, bf16[288,512]{1,0:T(8,128)(2,1)S(1)}, u32[]{:S(2)}, u32[]{:S(2)}) collective-permute-start(bf16[288,512]{1,0:T(8,128)(2,1)S(1)} %shard_map.161.mine), channel_id=1, source_target_pairs={{0,2},{1,3},{2,0},{3,1},{4,6},{5,7},{6,4},{7,5},{8,10},{9,11},{10,... | collective-permute-start | bytes 884744 | tf_op jit(solution)/shard_map/ppermute | solution.py:411
  32.0 0.9 %shard_map.159 = bf16[32,1024]{1,0:T(8,128)(2,1)S(1)} custom-call(f32[64,192]{1,0:T(8,128)S(1)} %get-tuple-element.43.times_ref, bf16[64,512]{1,0:T(8,128)(2,1)S(1)} %get-tuple-element.44.mine, bf16[80,512]{1,0:T(8,128)(2,1)S(1)} %collective-permute-done.6.came, bf16[64,1024]{1,0:T(8,128)(2,1)S(1)} %get-tuple-element.49.pairs0, ...), custom_call_target="tpu_custom_call" | custom-call | flops 16000000000 | bytes 1638400 | tf_op jit(solution)/shard_map/pallas_call | solution.py:44
  32.9 1.1 %collective-permute-start.11 = (bf16[32,1024]{1,0:T(8,128)(2,1)S(1)}, bf16[32,1024]{1,0:T(8,128)(2,1)S(1)}, u32[]{:S(2)}, u32[]{:S(2)}) collective-permute-start(bf16[32,1024]{1,0:T(8,128)(2,1)S(1)} %shard_map.159), channel_id=1, source_target_pairs={{0,16},{16,0},{1,17},{17,1},{2,18},{18,2},{3,19},{19,3},{4,20},{20... | collective-permute-start | bytes 196616 | tf_op jit(solution)/shard_map/ppermute | solution.py:392
  34.7 0.9 %shard_map.158 = (f32[32,1024]{1,0:T(8,128)S(1)}, f32[8,128]{1,0:T(8,128)S(1)}, f32[8,100]{1,0:T(8,128)S(1)}) custom-call(bf16[64,1024]{1,0:T(8,128)(2,1)S(1)} %get-tuple-element.41.latent, s32[1,1]{1,0:T(1,128)} %bitcast.16.limit, bf16[100,128]{1,0:T(8,128)(2,1)S(1)} %bitcast.19, f32[1,128]{1,0:T(1,128)S(1)} %bitcast.25, ...), custom_call_target="tpu_custom_call" | custom-call | flops 67108864 | bytes 1795588 | tf_op jit(solution)/shard_map/pallas_call | solution.py:44
  35.6 2.0 %collective-permute-done.11.theirs = bf16[32,1024]{1,0:T(8,128)(2,1)S(1)} collective-permute-done((bf16[32,1024]{1,0:T(8,128)(2,1)S(1)}, bf16[32,1024]{1,0:T(8,128)(2,1)S(1)}, u32[]{:S(2)}, u32[]{:S(2)}) %collective-permute-start.11) | collective-permute-done | bytes 65568 | tf_op jit(solution)/shard_map/ppermute | solution.py:392
  38.3 4.9 %collective-permute-start.12 = (bf16[32,512]{1,0:T(8,128)(2,1)S(1)}, bf16[32,512]{1,0:T(8,128)(2,1)S(1)}, u32[]{:S(2)}, u32[]{:S(2)}) collective-permute-start(bf16[32,512]{1,0:T(8,128)(2,1)S(1)} %get-tuple-element.57), channel_id=1, source_target_pairs={{0,1},{1,0},{2,3},{3,2},{4,5},{5,4},{6,7},{7,6},{8,9},{9,8},{10,11... | collective-permute-start | bytes 98312 | tf_op jit(solution)/shard_map/ppermute | solution.py:401
  43.3 0.7 %collective-permute-done.12.left = bf16[32,512]{1,0:T(8,128)(2,1)S(1)} collective-permute-done((bf16[32,512]{1,0:T(8,128)(2,1)S(1)}, bf16[32,512]{1,0:T(8,128)(2,1)S(1)}, u32[]{:S(2)}, u32[]{:S(2)}) %collective-permute-start.12) | collective-permute-done | bytes 32800 | tf_op jit(solution)/shard_map/ppermute | solution.py:401
  45.0 1.2 %shard_map.163 = (f32[100,128]{1,0:T(8,128)S(1)}, bf16[128,512]{1,0:T(8,128)(2,1)S(1)}, f32[128,512]{1,0:T(8,128)S(1)}) custom-call(bf16[128,96]{1,0:T(8,128)(2,1)S(1)} %get-tuple-element.54.counts, bf16[32,1024]{1,0:T(8,128)(2,1)S(1)} %get-tuple-element.56.up0, bf16[32,512]{1,0:T(8,128)(2,1)S(1)} %collective-permute-done.12.left, ...), custom_call_target="tpu_custom_call" | custom-call | flops 134217728 | bytes 1961984 | tf_op jit(solution)/shard_map/pallas_call | solution.py:44
  46.7 1.1 %shard_map.164 = (bf16[100,128]{1,0:T(8,128)(2,1)}, f32[32,8,100]{2,1,0:T(8,128)S(1)}) custom-call(f32[8,128]{1,0:T(8,128)S(1)} %get-tuple-element.52.weight_ref, f32[8,100]{1,0:T(8,128)S(1)} %get-tuple-element.53.base_ref, bf16[100,128]{1,0:T(8,128)(2,1)S(1)} %bitcast.24, bf16[100,128]{1,0:T(8,128)(2,1)S(1)} %bitcast.20, ...), custom_call_target="tpu_custom_call" | custom-call | flops 134217728 | bytes 1682560 | tf_op jit(solution)/shard_map/pallas_call | solution.py:44
  47.7 13.3 %all_to_all.5.parts = f32[32,8,100]{2,1,0:T(8,128)S(1)} all-to-all(f32[32,8,100]{2,1,0:T(8,128)S(1)} %get-tuple-element.67), channel_id=1, replica_groups=mesh['dp'=2,'space'=16] {'dp','space'}, dimensions={0} | all-to-all | bytes 204800 | tf_op jit(solution)/shard_map/all_to_all | solution.py:530
  (58 shorter events, 6.9 us)
Async XLA Ops:
  0.6 4.9 %collective-permute-start = (bf16[100,128]{1,0:T(8,128)(2,1)}, bf16[100,128]{1,0:T(8,128)(2,1)S(1)}, u32[]{:S(2)}, u32[]{:S(2)}) collective-permute-start(bf16[100,128]{1,0:T(8,128)(2,1)} %bitcast.21), channel_id=1, source_target_pairs={{0,1},{1,0},{2,3},{3,2},{4,5},{5,4},{6,7},{7,6},{8,9},{9,8},{10,11... | collective-permute-start | bytes 76808 | tf_op jit(solution)/shard_map/ppermute | solution.py:401
  1.1 4.4 %collective-permute-start.1 = (bf16[100,128]{1,0:T(8,128)(2,1)}, bf16[100,128]{1,0:T(8,128)(2,1)S(1)}, u32[]{:S(2)}, u32[]{:S(2)}) collective-permute-start(bf16[100,128]{1,0:T(8,128)(2,1)} %bitcast.22), channel_id=1, source_target_pairs={{1,2},{3,4},{5,6},{7,8},{9,10},{11,12},{13,14},{2,1},{4,3},{6,5},{... | collective-permute-start | bytes 76808 | tf_op jit(solution)/shard_map/ppermute | solution.py:404
  1.8 5.5 %collective-permute-start.3 = (bf16[100,512]{1,0:T(8,128)(2,1)}, bf16[100,512]{1,0:T(8,128)(2,1)S(1)}, u32[]{:S(2)}, u32[]{:S(2)}) collective-permute-start(bf16[100,512]{1,0:T(8,128)(2,1)} %we_here.3), channel_id=1, source_target_pairs={{0,16},{16,0},{1,17},{17,1},{2,18},{18,2},{3,19},{19,3},{4,20},{20... | collective-permute-start | bytes 307208 | tf_op jit(solution)/shard_map/ppermute | solution.py:392
  6.1 4.5 %collective-permute-start.2 = (bf16[100,384]{1,0:T(8,128)(2,1)S(1)}, bf16[100,384]{1,0:T(8,128)(2,1)S(1)}, u32[]{:S(2)}, u32[]{:S(2)}) collective-permute-start(bf16[100,384]{1,0:T(8,128)(2,1)S(1)} %shard_map.150.near_ref), channel_id=1, source_target_pairs={{0,16},{16,0},{1,17},{17,1},{2,18},{18,2},{3,19},{19,3},{4,20},{20... | collective-permute-start | bytes 230408 | tf_op jit(solution)/shard_map/ppermute | solution.py:392
  7.5 5.2 %copy-start.2 = (bf16[1024,512]{1,0:T(8,128)(2,1)S(1)}, bf16[1024,512]{1,0:T(8,128)(2,1)}, u32[]{:S(2)}) copy-start(bf16[1024,512]{1,0:T(8,128)(2,1)} %w1_ref.2) | copy-start | bytes 3145732
  7.5 5.2 %copy-start.3 = (bf16[512,100]{0,1:T(8,128)(2,1)S(1)}, bf16[512,100]{0,1:T(8,128)(2,1)}, u32[]{:S(2)}) copy-start(bf16[512,100]{0,1:T(8,128)(2,1)} %param.27) | copy-start | bytes 307204
  7.5 5.2 %copy-start.11 = (s32[32,16]{0,1:T(8,128)S(1)}, s32[32,16]{0,1:T(8,128)}, u32[]{:S(2)}) copy-start(s32[32,16]{0,1:T(8,128)} %param.20) | copy-start | bytes 6148
  7.5 5.2 %copy-start.12 = (s32[128,3]{0,1:T(4,128)S(1)}, s32[128,3]{0,1:T(4,128)}, u32[]{:S(2)}) copy-start(s32[128,3]{0,1:T(4,128)} %param.21) | copy-start | bytes 4612
  12.6 3.9 %collective-permute-start.4 = (bf16[16,768]{1,0:T(8,128)(2,1)S(1)}, bf16[16,768]{1,0:T(8,128)(2,1)S(1)}, u32[]{:S(2)}, u32[]{:S(2)}) collective-permute-start(bf16[16,768]{1,0:T(8,128)(2,1)S(1)} %get-tuple-element.38), channel_id=1, source_target_pairs={{0,16},{16,0},{1,17},{17,1},{2,18},{18,2},{3,19},{19,3},{4,20},{20... | collective-permute-start | bytes 73736 | tf_op jit(solution)/shard_map/ppermute | solution.py:398
  13.1 6.7 %collective-permute-start.15 = (bf16[144,512]{1,0:T(8,128)(2,1)S(1)}, bf16[144,512]{1,0:T(8,128)(2,1)S(1)}, u32[]{:S(2)}, u32[]{:S(2)}) collective-permute-start(bf16[144,512]{1,0:T(8,128)(2,1)S(1)} %get-tuple-element.60), channel_id=1, source_target_pairs={{0,16},{16,0},{1,17},{17,1},{2,18},{18,2},{3,19},{19,3},{4,20},{20... | collective-permute-start | bytes 442376 | tf_op jit(solution)/shard_map/ppermute | solution.py:392
  16.5 15.5 %copy-start.1 = (bf16[512,1024]{1,0:T(8,128)(2,1)S(1)}, bf16[512,1024]{1,0:T(8,128)(2,1)}, u32[]{:S(2)}) copy-start(bf16[512,1024]{1,0:T(8,128)(2,1)} %wo_ref.3) | copy-start | bytes 3145732
  16.5 8.3 %collective-permute-start.5 = (bf16[64,1024]{1,0:T(8,128)(2,1)S(1)}, bf16[64,1024]{1,0:T(8,128)(2,1)S(1)}, u32[]{:S(2)}, u32[]{:S(2)}) collective-permute-start(bf16[64,1024]{1,0:T(8,128)(2,1)S(1)} %shard_map.153.mine.latent), channel_id=1, source_target_pairs={{0,16},{16,0},{1,17},{17,1},{2,18},{18,2},{3,19},{19,3},{4,20},{20... | collective-permute-start | bytes 393224 | tf_op jit(solution)/shard_map/ppermute | solution.py:395
  17.2 8.4 %collective-permute-start.7 = (bf16[64,512]{1,0:T(8,128)(2,1)S(1)}, bf16[64,512]{1,0:T(8,128)(2,1)S(1)}, u32[]{:S(2)}, u32[]{:S(2)}) collective-permute-start(bf16[64,512]{1,0:T(8,128)(2,1)S(1)} %get-tuple-element.48), channel_id=1, source_target_pairs={{0,16},{16,0},{1,17},{17,1},{2,18},{18,2},{3,19},{19,3},{4,20},{20... | collective-permute-start | bytes 196616 | tf_op jit(solution)/shard_map/ppermute | solution.py:395
  19.7 11.0 %collective-permute-start.16 = (bf16[144,512]{1,0:T(8,128)(2,1)S(1)}, bf16[144,512]{1,0:T(8,128)(2,1)S(1)}, u32[]{:S(2)}, u32[]{:S(2)}) collective-permute-start(bf16[144,512]{1,0:T(8,128)(2,1)S(1)} %collective-permute-done.15.mine), channel_id=1, source_target_pairs={{0,4},{1,5},{2,6},{3,7},{4,0},{5,1},{6,2},{7,3},{8,12},{9,13},{10,... | collective-permute-start | bytes 442376 | tf_op jit(solution)/shard_map/ppermute | solution.py:461
  25.7 6.3 %collective-permute-start.10 = (bf16[64,1024]{1,0:T(8,128)(2,1)S(1)}, bf16[64,1024]{1,0:T(8,128)(2,1)S(1)}, u32[]{:S(2)}, u32[]{:S(2)}) collective-permute-start(bf16[64,1024]{1,0:T(8,128)(2,1)S(1)} %get-tuple-element.49.pairs0), channel_id=1, source_target_pairs={{1,2},{3,4},{5,6},{7,8},{9,10},{11,12},{13,14},{2,1},{4,3},{6,5},{... | collective-permute-start | bytes 393224 | tf_op jit(solution)/shard_map/ppermute | solution.py:404
  26.4 5.6 %collective-permute-start.6 = (bf16[80,512]{1,0:T(8,128)(2,1)S(1)}, bf16[80,512]{1,0:T(8,128)(2,1)S(1)}, u32[]{:S(2)}, u32[]{:S(2)}) collective-permute-start(bf16[80,512]{1,0:T(8,128)(2,1)S(1)} %get-tuple-element.45), channel_id=1, source_target_pairs={{0,16},{16,0},{1,17},{17,1},{2,18},{18,2},{3,19},{19,3},{4,20},{20... | collective-permute-start | bytes 245768 | tf_op jit(solution)/shard_map/ppermute | solution.py:398
  27.1 4.8 %collective-permute-start.8 = (bf16[64,512]{1,0:T(8,128)(2,1)S(1)}, bf16[64,512]{1,0:T(8,128)(2,1)S(1)}, u32[]{:S(2)}, u32[]{:S(2)}) collective-permute-start(bf16[64,512]{1,0:T(8,128)(2,1)S(1)} %get-tuple-element.50), channel_id=1, source_target_pairs={{0,1},{1,0},{2,3},{3,2},{4,5},{5,4},{6,7},{7,6},{8,9},{9,8},{10,11... | collective-permute-start | bytes 196616 | tf_op jit(solution)/shard_map/ppermute | solution.py:401
  30.7 1.3 %collective-permute-start.9 = (bf16[64,512]{1,0:T(8,128)(2,1)S(1)}, bf16[64,512]{1,0:T(8,128)(2,1)S(1)}, u32[]{:S(2)}, u32[]{:S(2)}) collective-permute-start(bf16[64,512]{1,0:T(8,128)(2,1)S(1)} %get-tuple-element.51), channel_id=1, source_target_pairs={{0,1},{1,0},{2,3},{3,2},{4,5},{5,4},{6,7},{7,6},{8,9},{9,8},{10,11... | collective-permute-start | bytes 196616 | tf_op jit(solution)/shard_map/ppermute | solution.py:401
  30.8 12.5 %collective-permute-start.17 = (bf16[288,512]{1,0:T(8,128)(2,1)S(1)}, bf16[288,512]{1,0:T(8,128)(2,1)S(1)}, u32[]{:S(2)}, u32[]{:S(2)}) collective-permute-start(bf16[288,512]{1,0:T(8,128)(2,1)S(1)} %shard_map.161.mine), channel_id=1, source_target_pairs={{0,2},{1,3},{2,0},{3,1},{4,6},{5,7},{6,4},{7,5},{8,10},{9,11},{10,... | collective-permute-start | bytes 884744 | tf_op jit(solution)/shard_map/ppermute | solution.py:411
  32.9 4.7 %collective-permute-start.11 = (bf16[32,1024]{1,0:T(8,128)(2,1)S(1)}, bf16[32,1024]{1,0:T(8,128)(2,1)S(1)}, u32[]{:S(2)}, u32[]{:S(2)}) collective-permute-start(bf16[32,1024]{1,0:T(8,128)(2,1)S(1)} %shard_map.159), channel_id=1, source_target_pairs={{0,16},{16,0},{1,17},{17,1},{2,18},{18,2},{3,19},{19,3},{4,20},{20... | collective-permute-start | bytes 196616 | tf_op jit(solution)/shard_map/ppermute | solution.py:392
  37.6 6.8 %collective-permute-start.14 = (bf16[32,1024]{1,0:T(8,128)(2,1)S(1)}, bf16[32,1024]{1,0:T(8,128)(2,1)S(1)}, u32[]{:S(2)}, u32[]{:S(2)}) collective-permute-start(bf16[32,1024]{1,0:T(8,128)(2,1)S(1)} %get-tuple-element.56.up0), channel_id=1, source_target_pairs={{1,2},{3,4},{5,6},{7,8},{9,10},{11,12},{13,14},{2,1},{4,3},{6,5},{... | collective-permute-start | bytes 196616 | tf_op jit(solution)/shard_map/ppermute | solution.py:404
  38.3 5.7 %collective-permute-start.12 = (bf16[32,512]{1,0:T(8,128)(2,1)S(1)}, bf16[32,512]{1,0:T(8,128)(2,1)S(1)}, u32[]{:S(2)}, u32[]{:S(2)}) collective-permute-start(bf16[32,512]{1,0:T(8,128)(2,1)S(1)} %get-tuple-element.57), channel_id=1, source_target_pairs={{0,1},{1,0},{2,3},{3,2},{4,5},{5,4},{6,7},{7,6},{8,9},{9,8},{10,11... | collective-permute-start | bytes 98312 | tf_op jit(solution)/shard_map/ppermute | solution.py:401
  43.2 1.2 %collective-permute-start.13 = (bf16[32,512]{1,0:T(8,128)(2,1)S(1)}, bf16[32,512]{1,0:T(8,128)(2,1)S(1)}, u32[]{:S(2)}, u32[]{:S(2)}) collective-permute-start(bf16[32,512]{1,0:T(8,128)(2,1)S(1)} %get-tuple-element.58), channel_id=1, source_target_pairs={{0,1},{1,0},{2,3},{3,2},{4,5},{5,4},{6,7},{7,6},{8,9},{9,8},{10,11... | collective-permute-start | bytes 98312 | tf_op jit(solution)/shard_map/ppermute | solution.py:401
  44.4 2.3 %collective-permute-start.18 = (bf16[576,512]{1,0:T(8,128)(2,1)S(1)}, bf16[576,512]{1,0:T(8,128)(2,1)S(1)}, u32[]{:S(2)}, u32[]{:S(2)}) collective-permute-start(bf16[576,512]{1,0:T(8,128)(2,1)S(1)} %shard_map.162.share.part0), channel_id=1, source_target_pairs={{0,1},{1,0},{2,3},{3,2},{4,5},{5,4},{6,7},{7,6},{8,9},{9,8},{10,11... | collective-permute-start | bytes 1769480 | tf_op jit(solution)/shard_map/ppermute | solution.py:401
  (8 other events, 16.1 us)
